TPU v7x, 256 devices: a whole 4x4x8 slice. The times are simulated.
256 devices in a mesh: lat: 32 (over z, y_lo, core), lon: 8 (over y_hi, x).
Axes of the slice: x: 4, y: 4 (y_hi: 2, y_lo: 2; y = y_hi * 2 + y_lo), z: 8, core: 2. Of those that a mesh axis runs over, the one named last changes fastest.
Arguments:
- queries: bfloat16 [128, 256, 1024], P('lat', 'lon'), may hold values from -6 to 6
- keys: bfloat16 [128, 256, 1024], P('lat', 'lon'), may hold values from -6 to 6
- values: bfloat16 [128, 256, 1024], P('lat', 'lon'), may hold values from -6 to 6
- conv_kernel: float32 [9, 1024], replicated, may hold values from -2 to 2
- cotangent: bfloat16 [128, 256, 1024], P('lat', 'lon'), may hold values from -6 to 6
- pattern: int32 [128, 2], replicated, may hold values from -2 to 5, as said below
- polar: int32 [128], replicated, may hold values from 0 to 1, as said below
Outputs:
- mixed: bfloat16 [128, 256, 1024], P('lat', 'lon')
- query_grad: bfloat16 [128, 256, 1024], P('lat', 'lon')
- key_grad: bfloat16 [128, 256, 1024], P('lat', 'lon')
- value_grad: bfloat16 [128, 256, 1024], P('lat', 'lon')
- kernel_grad: float32 [9, 1024], replicated
Inputs may be any that keep to these rules, and one draw needn't show every extreme that they name: `pattern`: column 0 of row i is o_i and column 1 is w_i, with -2 <= o_i <= 0 and 1 <= w_i <= 3 - o_i, so that the window of row i runs from o_i to o_i + w_i - 1 blocks around the query's block; some row spans 5 blocks. `polar`: 1 exactly on the first one to 2 and on the last one to 2 latitude rows, 0 on all others.
All inputs are finite; a program needn't handle non-finite values.
Results may differ from a plain program's by a relative error of at most 0.017.
Values may be sent and summed in bfloat16 or wider, within the bound.
No kernel may reach another device: no remote copies, remote signals or barrier semaphores. Data moves between devices by JAX's collectives and lax.ppermute only.
A program may use at most 128 MiB of HBM per device.

v0:
```python
import jax
import jax.numpy as jnp
from jax import lax
from jax.sharding import PartitionSpec as P

HEADS = 16
HEAD = 64
BLK = 8
REACH = 2


NEG = -1e30


def padded_2(cells, sides, width):
    for axis, dim in sides:
        count = lax.axis_size(axis)
        head = lax.slice_in_dim(cells, 0, width, axis=dim)
        tail = lax.slice_in_dim(cells, cells.shape[dim] - width, cells.shape[dim], axis=dim)
        cells = jnp.concatenate(
            [
                lax.ppermute(tail, axis, [(i, (i + 1) % count) for i in range(count)]),
                cells,
                lax.ppermute(head, axis, [((i + 1) % count, i) for i in range(count)]),
            ],
            axis=dim,
        )
    return cells


def passed_along(block, axis, distance):
    devices = range(lax.axis_size(axis))
    route = [(i - distance, i) for i in devices if i - distance in devices]
    return lax.ppermute(block, axis, route)


def passed_along_2(block, axis, distance):
    devices = range(lax.axis_size(axis))
    route = [((i - distance) % len(devices), i) for i in devices]
    return lax.ppermute(block, axis, route)


def split_heads(array):
    return array.reshape(array.shape[:-1] + (HEADS, HEAD))


def join_heads(array):
    return array.reshape(array.shape[:-2] + (HEADS * HEAD,))


def window_forward(query_heads, key_pad, value_pad, masks, score_scale):
    row_count, col_count = (query_heads.shape[0], query_heads.shape[1])
    run_max = jnp.full((row_count, HEADS, col_count), NEG, jnp.float32)
    run_sum = jnp.zeros((row_count, HEADS, col_count), jnp.float32)
    accum = jnp.zeros((row_count, HEADS, col_count, HEAD), jnp.float32)
    for shift_row, allowed in enumerate(masks):
        key_rows = split_heads(key_pad[shift_row : shift_row + row_count])
        value_rows = split_heads(value_pad[shift_row : shift_row + row_count])
        scores = (
            jnp.einsum("rqhd,rkhd->rhqk", query_heads, key_rows, preferred_element_type=jnp.float32)
            * score_scale
        )
        scores = jnp.where(allowed[:, None], scores, NEG)
        new_max = jnp.maximum(run_max, jnp.max(scores, axis=-1))
        weights = jnp.where(allowed[:, None], jnp.exp(scores - new_max[..., None]), 0.0)
        factor = jnp.exp(run_max - new_max)
        run_sum = run_sum * factor + jnp.sum(weights, axis=-1)
        accum = accum * factor[..., None] + jnp.einsum(
            "rhqk,rkhd->rhqd",
            weights.astype(jnp.bfloat16),
            value_rows,
            preferred_element_type=jnp.float32,
        )
        run_max = new_max
    output = accum / run_sum[..., None]
    return (join_heads(jnp.transpose(output, (0, 2, 1, 3))), run_max + jnp.log(run_sum))


def window_backward(query_heads, grad_heads, lse, delta, key_pad, value_pad, masks, score_scale):
    row_count, col_count = (query_heads.shape[0], query_heads.shape[1])
    grad_query = jnp.zeros((row_count, col_count, HEADS, HEAD), jnp.float32)
    part_key = jnp.zeros(key_pad.shape[:2] + (HEADS, HEAD), jnp.float32)
    part_value = jnp.zeros(key_pad.shape[:2] + (HEADS, HEAD), jnp.float32)
    for shift_row, allowed in enumerate(masks):
        key_rows = split_heads(key_pad[shift_row : shift_row + row_count])
        value_rows = split_heads(value_pad[shift_row : shift_row + row_count])
        scores = (
            jnp.einsum("rqhd,rkhd->rhqk", query_heads, key_rows, preferred_element_type=jnp.float32)
            * score_scale
        )
        probs = jnp.where(allowed[:, None], jnp.exp(scores - lse[..., None]), 0.0)
        dprob = jnp.einsum(
            "rqhd,rkhd->rhqk", grad_heads, value_rows, preferred_element_type=jnp.float32
        )
        dscore = (probs * (dprob - delta[..., None])).astype(jnp.bfloat16)
        grad_query = grad_query + jnp.einsum(
            "rhqk,rkhd->rqhd", dscore, key_rows, preferred_element_type=jnp.float32
        )
        part_key = part_key.at[shift_row : shift_row + row_count].add(
            jnp.einsum("rhqk,rqhd->rkhd", dscore, query_heads, preferred_element_type=jnp.float32)
        )
        part_value = part_value.at[shift_row : shift_row + row_count].add(
            jnp.einsum(
                "rhqk,rqhd->rkhd",
                probs.astype(jnp.bfloat16),
                grad_heads,
                preferred_element_type=jnp.float32,
            )
        )
    return (join_heads(grad_query) * score_scale, join_heads(part_key), join_heads(part_value))


def pole_forward(query_part, key_part, value_part, score_scale):
    scores = (
        jnp.einsum(
            "rqhd,rkhd->rhqk",
            split_heads(query_part),
            split_heads(key_part),
            preferred_element_type=jnp.float32,
        )
        * score_scale
    )
    top = jnp.max(scores, axis=-1)
    weights = jnp.exp(scores - top[..., None])
    total = jnp.sum(weights, axis=-1)
    summed = jnp.einsum(
        "rhqk,rkhd->rhqd",
        weights.astype(jnp.bfloat16),
        split_heads(value_part),
        preferred_element_type=jnp.float32,
    )
    output = summed / total[..., None]
    return (join_heads(jnp.transpose(output, (0, 2, 1, 3))), top + jnp.log(total))


def pole_grads(query_part, grad_part, lse_part, delta_part, key_part, value_part, score_scale):
    query_heads = split_heads(query_part)
    grad_heads = split_heads(grad_part)
    key_heads = split_heads(key_part)
    value_heads = split_heads(value_part)
    scores = (
        jnp.einsum("rqhd,rkhd->rhqk", query_heads, key_heads, preferred_element_type=jnp.float32)
        * score_scale
    )
    probs = jnp.exp(scores - lse_part[..., None])
    dprob = jnp.einsum(
        "rqhd,rkhd->rhqk", grad_heads, value_heads, preferred_element_type=jnp.float32
    )
    dscore = (probs * (dprob - delta_part[..., None])).astype(jnp.bfloat16)
    grad_query = (
        jnp.einsum("rhqk,rkhd->rqhd", dscore, key_heads, preferred_element_type=jnp.float32)
        * score_scale
    )
    grad_key = (
        jnp.einsum("rhqk,rqhd->rkhd", dscore, query_heads, preferred_element_type=jnp.float32)
        * score_scale
    )
    grad_value = jnp.einsum(
        "rhqk,rqhd->rkhd",
        probs.astype(jnp.bfloat16),
        grad_heads,
        preferred_element_type=jnp.float32,
    )
    return (join_heads(grad_query), join_heads(grad_key), join_heads(grad_value))


def add_rows(array, extra, row_start):
    current = lax.dynamic_slice_in_dim(array, row_start, extra.shape[0], 0)
    return lax.dynamic_update_slice_in_dim(array, current + extra, row_start, 0)


def body(queries, keys, values, conv_kernel, cotangent, pattern, polar):
    row_count, col_count, channels = queries.shape
    lat_count = lax.axis_size("lat")
    lon_count = lax.axis_size("lon")
    lat_index = lax.axis_index("lat")
    total_rows = row_count * lat_count
    row_base = lat_index * row_count
    block_count = col_count // BLK
    side_cols = REACH * BLK
    wide_cols = col_count + 2 * side_cols
    span_rows = row_count + 2 * REACH
    score_scale = HEAD ** (-0.5)
    offsets_pad = lax.dynamic_slice_in_dim(
        jnp.pad(pattern[:, 0], (REACH, REACH)), row_base, span_rows, 0
    )
    widths_pad = lax.dynamic_slice_in_dim(
        jnp.pad(pattern[:, 1], (REACH, REACH)), row_base, span_rows, 0
    )
    polar_pad = lax.dynamic_slice_in_dim(jnp.pad(polar, (REACH, REACH)), row_base, span_rows, 0) > 0
    global_rows = row_base - REACH + jnp.arange(span_rows, dtype=jnp.int32)
    rows_valid = (global_rows >= 0) & (global_rows < total_rows)
    own_offset = offsets_pad[REACH : REACH + row_count]
    own_width = widths_pad[REACH : REACH + row_count]
    own_polar = polar_pad[REACH : REACH + row_count]
    own_blocks = jnp.arange(col_count, dtype=jnp.int32) // BLK
    pad_blocks = jnp.arange(wide_cols, dtype=jnp.int32) // BLK - REACH
    relative = pad_blocks[None, None, :] - own_blocks[None, :, None] - own_offset[:, None, None]
    in_window = (relative >= 0) & (relative < own_width[:, None, None])
    masks = [
        in_window & rows_valid[shift_row : shift_row + row_count][:, None, None]
        for shift_row in range(2 * REACH + 1)
    ]
    stacked = jnp.stack((keys, values)).reshape(2, row_count, block_count, BLK, channels)
    padded = padded_2(stacked, (("lat", 1), ("lon", 2)), REACH)
    padded = padded.reshape(2, span_rows, wide_cols, channels)
    key_pad = padded[0]
    value_pad = padded[1]
    query_heads = split_heads(queries)
    out_near, lse_near = window_forward(query_heads, key_pad, value_pad, masks, score_scale)
    pole_start = jnp.where(lat_index == 0, 0, row_count - REACH).astype(jnp.int32)
    cand_flags = lax.dynamic_slice_in_dim(own_polar, pole_start, REACH, 0)
    active = jnp.any(cand_flags)
    cand_query = lax.dynamic_slice_in_dim(queries, pole_start, REACH, 0)
    cand_key = lax.dynamic_slice_in_dim(keys, pole_start, REACH, 0)
    cand_value = lax.dynamic_slice_in_dim(values, pole_start, REACH, 0)
    full_keys, full_values = (
        lax.all_gather(cand_key, "lon", axis=1, tiled=True),
        lax.all_gather(cand_value, "lon", axis=1, tiled=True),
    )
    full_cols = full_keys.shape[1]

    def pole_on():
        return pole_forward(cand_query, full_keys, full_values, score_scale)

    def pole_off():
        return (
            jnp.zeros((REACH, col_count, channels), jnp.float32),
            jnp.zeros((REACH, HEADS, col_count), jnp.float32),
        )

    out_pole, lse_pole = lax.cond(active, pole_on, pole_off)
    cand_near = lax.dynamic_slice_in_dim(out_near, pole_start, REACH, 0)
    merged = jnp.where(cand_flags[:, None, None], out_pole, cand_near)
    attended = lax.dynamic_update_slice_in_dim(out_near, merged, pole_start, 0).astype(jnp.bfloat16)
    edge_rows = row_base - 1 + jnp.arange(row_count + 2, dtype=jnp.int32)
    edge_valid = ((edge_rows >= 0) & (edge_rows < total_rows))[:, None, None]
    att_pad = padded_2(attended, (("lat", 0), ("lon", 1)), 1)
    att_pad = jnp.where(edge_valid, att_pad, jnp.zeros_like(att_pad))
    cot_pad = padded_2(cotangent, (("lat", 0), ("lon", 1)), 1)
    cot_pad = jnp.where(edge_valid, cot_pad, jnp.zeros_like(cot_pad))
    conv_sum = jnp.zeros((row_count, col_count, channels), jnp.float32)
    back = cotangent.astype(jnp.float32)
    taps = []
    for tap_row in range(3):
        for tap_col in range(3):
            weight = conv_kernel[3 * tap_row + tap_col]
            shifted = att_pad[tap_row : tap_row + row_count, tap_col : tap_col + col_count]
            conv_sum = conv_sum + weight * shifted
            back = (
                back
                + weight
                * cot_pad[
                    2 - tap_row : 2 - tap_row + row_count, 2 - tap_col : 2 - tap_col + col_count
                ]
            )
            taps.append(
                jnp.einsum("ijc,ijc->c", cotangent, shifted, preferred_element_type=jnp.float32)
            )
    mixed = (attended.astype(jnp.float32) + conv_sum).astype(jnp.bfloat16)
    d_att = back.astype(jnp.bfloat16)
    norm_factor = (total_rows * col_count * lon_count) ** (-0.5)
    kernel_grad = lax.psum(jnp.stack(taps) * norm_factor, ("lat", "lon"))
    delta = jnp.einsum(
        "rqhd,rqhd->rhq",
        split_heads(d_att),
        split_heads(attended),
        preferred_element_type=jnp.float32,
    )
    keep_rows = (~own_polar)[:, None, None]
    grad_near = jnp.where(keep_rows, d_att, jnp.zeros_like(d_att))
    delta_near = jnp.where(keep_rows, delta, 0.0)
    cand_grad = lax.dynamic_slice_in_dim(d_att, pole_start, REACH, 0)
    cand_grad = jnp.where(cand_flags[:, None, None], cand_grad, jnp.zeros_like(cand_grad))
    cand_delta = jnp.where(
        cand_flags[:, None, None], lax.dynamic_slice_in_dim(delta, pole_start, REACH, 0), 0.0
    )
    grad_query, part_key, part_value = window_backward(
        query_heads,
        split_heads(grad_near),
        lse_near,
        delta_near,
        key_pad,
        value_pad,
        masks,
        score_scale,
    )
    from_south = passed_along(
        jnp.stack((part_key[:REACH], part_value[:REACH])).astype(jnp.bfloat16), "lat", -1
    ).astype(jnp.float32)
    from_north = passed_along(
        jnp.stack((part_key[row_count + REACH :], part_value[row_count + REACH :])).astype(
            jnp.bfloat16
        ),
        "lat",
        1,
    ).astype(jnp.float32)
    middle = jnp.stack((part_key[REACH : REACH + row_count], part_value[REACH : REACH + row_count]))
    middle = middle.at[:, row_count - REACH :].add(from_south)
    middle = middle.at[:, :REACH].add(from_north)
    from_east = passed_along_2(middle[:, :, :side_cols].astype(jnp.bfloat16), "lon", -1).astype(
        jnp.float32
    )
    from_west = passed_along_2(
        middle[:, :, col_count + side_cols :].astype(jnp.bfloat16), "lon", 1
    ).astype(jnp.float32)
    middle = middle.at[:, :, col_count : col_count + side_cols].add(from_east)
    middle = middle.at[:, :, side_cols : 2 * side_cols].add(from_west)
    grad_key = middle[0, :, side_cols : side_cols + col_count] * score_scale
    grad_value = middle[1, :, side_cols : side_cols + col_count]

    def pole_back_on():
        return pole_grads(
            cand_query, cand_grad, lse_pole, cand_delta, full_keys, full_values, score_scale
        )

    def pole_back_off():
        return (
            jnp.zeros((REACH, col_count, channels), jnp.float32),
            jnp.zeros((REACH, full_cols, channels), jnp.float32),
            jnp.zeros((REACH, full_cols, channels), jnp.float32),
        )

    pole_dq, pole_terms_key, pole_terms_value = lax.cond(active, pole_back_on, pole_back_off)
    pole_dk, pole_dv = (
        lax.psum_scatter(
            pole_terms_key.astype(jnp.bfloat16), "lon", scatter_dimension=1, tiled=True
        ).astype(jnp.float32),
        lax.psum_scatter(
            pole_terms_value.astype(jnp.bfloat16), "lon", scatter_dimension=1, tiled=True
        ).astype(jnp.float32),
    )
    grad_query = add_rows(grad_query, pole_dq, pole_start)
    grad_key = add_rows(grad_key, pole_dk, pole_start)
    grad_value = add_rows(grad_value, pole_dv, pole_start)
    return (
        mixed,
        grad_query.astype(jnp.bfloat16),
        grad_key.astype(jnp.bfloat16),
        grad_value.astype(jnp.bfloat16),
        kernel_grad,
    )


def solution(mesh):
    return jax.shard_map(
        body,
        mesh=mesh,
        in_specs=(
            P("lat", "lon", None),
            P("lat", "lon", None),
            P("lat", "lon", None),
            P(),
            P("lat", "lon", None),
            P(),
            P(),
        ),
        out_specs=(
            P("lat", "lon", None),
            P("lat", "lon", None),
            P("lat", "lon", None),
            P("lat", "lon", None),
            P(),
        ),
        check_vma=False,
    )
```

profile of v0, /device:TPU:32, one launch (start us, length us, event | category | flops | bytes accessed | tf_op | source)
XLA Modules:
  0.0 380.7 jit_solution(349177895163885882)
XLA Ops:
  21.5 5.3 %collective-permute-start.3 = (bf16[2,8,2,8,1024]{4,3,2,1,0:T(8,128)(2,1)S(1)}, bf16[2,8,2,8,1024]{4,3,2,1,0:T(8,128)(2,1)S(1)}, u32[]{:S(2)}, u32[]{:S(2)}) collective-permute-start(bf16[2,8,2,8,1024]{4,3,2,1,0:T(8,128)(2,1)S(1)} %get-tuple-element.331), channel_id=1, source_target_pairs={{1,0},{2,1},{3,2},{4,3},{5,4},{6,5},{7,6},{0,7},{9,8},{10,9},{11,1... | collective-permute-start | bytes 1572872 | tf_op jit(solution)/shard_map/ppermute | solution.py:24
  27.7 11.4 %collective-permute-done.3 = bf16[2,8,2,8,1024]{4,3,2,1,0:T(8,128)(2,1)S(1)} collective-permute-done((bf16[2,8,2,8,1024]{4,3,2,1,0:T(8,128)(2,1)S(1)}, bf16[2,8,2,8,1024]{4,3,2,1,0:T(8,128)(2,1)S(1)}, u32[]{:S(2)}, u32[]{:S(2)}) %collective-permute-start.3) | collective-permute-done | bytes 524320 | tf_op jit(solution)/shard_map/ppermute | solution.py:24
  39.0 6.2 %collective-permute-done.2 = bf16[2,8,2,8,1024]{4,3,2,1,0:T(8,128)(2,1)S(1)} collective-permute-done((bf16[2,8,2,8,1024]{4,3,2,1,0:T(8,128)(2,1)S(1)}, bf16[2,8,2,8,1024]{4,3,2,1,0:T(8,128)(2,1)S(1)}, u32[]{:S(2)}, u32[]{:S(2)}) %collective-permute-start.2) | collective-permute-done | bytes 524320 | tf_op jit(solution)/shard_map/ppermute | solution.py:22
  53.5 2.8 reshape.860
  56.3 2.5 reshape.858
  58.8 2.5 reshape.859
  61.3 2.5 reshape.861
  63.8 2.5 reshape.863
  66.3 3.0 reshape.865
  84.9 40.1 %all-gather.5.cloned.1.call-done = bf16[2,256,1024]{2,0,1:T(2,128)(2,1)} async-done(((bf16[2,32,1024]{2,0,1:T(2,128)(2,1)}), bf16[2,256,1024]{2,0,1:T(2,128)(2,1)}) %all-gather.5.cloned.1.call-update) | async-done | bytes 1048592 | tf_op jit(solution)/shard_map/all_gather | solution.py:219
  127.4 2.7 collective-permute-start.11
  130.6 5.2 %collective-permute-start.7 = (bf16[6,1,1024]{2,1,0:T(2,128)(2,1)S(1)}, bf16[6,1,1024]{2,1,0:T(2,128)(2,1)S(1)}, u32[]{:S(2)}, u32[]{:S(2)}) collective-permute-start(bf16[6,1,1024]{2,1,0:T(2,128)(2,1)S(1)} %get-tuple-element.337), channel_id=1, source_target_pairs={{1,0},{2,1},{3,2},{4,3},{5,4},{6,5},{7,6},{0,7},{9,8},{10,9},{11,1... | collective-permute-start | bytes 36872 | tf_op jit(solution)/shard_map/ppermute | solution.py:24
  137.5 6.0 %collective-permute-done.6 = bf16[6,1,1024]{2,1,0:T(2,128)(2,1)S(1)} collective-permute-done((bf16[6,1,1024]{2,1,0:T(2,128)(2,1)S(1)}, bf16[6,1,1024]{2,1,0:T(2,128)(2,1)S(1)}, u32[]{:S(2)}, u32[]{:S(2)}) %collective-permute-start.6) | collective-permute-done | bytes 12320 | tf_op jit(solution)/shard_map/ppermute | solution.py:22
  151.7 3.6 fusion.46
  167.4 2.5 constant_dynamic-update-slice_fusion.3
  170.4 2.9 scatter-add.46
  174.3 3.4 fusion.22
  177.8 3.5 fusion.20
  181.2 3.5 fusion.19
  184.7 3.8 %constant_dynamic-update-slice_fusion.4 = (f32[8,64,16,64]{3,1,2,0:T(8,128)}, bf16[4,64,16,64]{3,1,2,0:T(8,128)(2,1)}) fusion(f32[8,64,16,64]{3,1,2,0:T(8,128)} %fusion.19, bf16[4,16,32,64]{3,2,1,0:T(8,128)(2,1)S(1)} %fusion.49, bf16[4,32,16,64]{3,2,1,0:T(8,128)(2,1)S(1)} %reshape.856), kind=kOutput, calls=%fused_computation.271 | convolution fusion | flops 17301504 | bytes 5767168 | tf_op jit(solution)/shard_map/rhqk,rqhd->rkhd/dot_general | solution.py:100
  192.1 3.0 conditional.3
  222.5 2.9 copy.153
  242.6 97.2 %psum.7 = f32[9,1024]{1,0:T(8,128)} all-reduce(f32[9,1024]{1,0:T(8,128)S(1)} %broadcast_multiply_fusion), channel_id=1, replica_groups=mesh['lat'=32,'lon'=8] {'lat','lon'}, use_global_device_ids=true, to_apply=%region_19.20 | all-reduce | flops 9216 | bytes 73728 | tf_op jit(solution)/shard_map/psum | solution.py:263
  344.3 27.9 %reduce-scatter.5.cloned.1.call-done = bf16[2,32,1024]{2,1,0:T(8,128)(2,1)} async-done(((bf16[2,256,1024]{2,1,0:T(8,128)(2,1)}), bf16[2,32,1024]{2,1,0:T(8,128)(2,1)}) %reduce-scatter.5.cloned.1.call-update) | async-done | bytes 131088 | tf_op jit(solution)/shard_map/reduce_scatter | solution.py:329
  (332 shorter events, 120.5 us)
Async XLA Ops:
  7.2 77.7 %all-gather.3.cloned.1.call-start = ((), (), s32[]{:S(2)}) async-start(), calls=%async_computation.2 | async-start | bytes 1179648 | tf_op jit(solution)/shard_map/all_gather | solution.py:218
  9.1 115.9 %all-gather.5.cloned.1.call-start = ((), (), s32[]{:S(2)}) async-start(), calls=%async_computation.3 | async-start | bytes 1179648 | tf_op jit(solution)/shard_map/all_gather | solution.py:219
  10.3 10.9 %collective-permute-start.1 = (bf16[2,2,4,8,1024]{4,3,2,1,0:T(8,128)(2,1)S(1)}, bf16[2,2,4,8,1024]{4,3,2,1,0:T(8,128)(2,1)S(1)}, u32[]{:S(2)}, u32[]{:S(2)}) collective-permute-start(bf16[2,2,4,8,1024]{4,3,2,1,0:T(8,128)(2,1)S(1)} %get-tuple-element.333), channel_id=1, source_target_pairs={{8,0},{16,8},{24,16},{32,24},{40,32},{48,40},{56,48},{64,56},{72,6... | collective-permute-start | bytes 786440 | tf_op jit(solution)/shard_map/ppermute | solution.py:24
  11.0 10.2 %collective-permute-start = (bf16[2,2,4,8,1024]{4,3,2,1,0:T(8,128)(2,1)S(1)}, bf16[2,2,4,8,1024]{4,3,2,1,0:T(8,128)(2,1)S(1)}, u32[]{:S(2)}, u32[]{:S(2)}) collective-permute-start(bf16[2,2,4,8,1024]{4,3,2,1,0:T(8,128)(2,1)S(1)} %get-tuple-element.332), channel_id=1, source_target_pairs={{0,8},{8,16},{16,24},{24,32},{32,40},{40,48},{48,56},{56,64},{64,7... | collective-permute-start | bytes 786440 | tf_op jit(solution)/shard_map/ppermute | solution.py:22
  11.8 15.7 %collective-permute-start.8 = (bf16[1,32,1024]{2,1,0:T(8,128)(2,1)S(1)}, bf16[1,32,1024]{2,1,0:T(8,128)(2,1)S(1)}, u32[]{:S(2)}, u32[]{:S(2)}) collective-permute-start(bf16[1,32,1024]{2,1,0:T(8,128)(2,1)S(1)} %get-tuple-element.339), channel_id=1, source_target_pairs={{0,8},{8,16},{16,24},{24,32},{32,40},{40,48},{48,56},{56,64},{64,7... | collective-permute-start | bytes 196616 | tf_op jit(solution)/shard_map/ppermute | solution.py:22
  13.1 14.5 %collective-permute-start.9 = (bf16[1,32,1024]{2,1,0:T(8,128)(2,1)S(1)}, bf16[1,32,1024]{2,1,0:T(8,128)(2,1)S(1)}, u32[]{:S(2)}, u32[]{:S(2)}) collective-permute-start(bf16[1,32,1024]{2,1,0:T(8,128)(2,1)S(1)} %get-tuple-element.338), channel_id=1, source_target_pairs={{8,0},{16,8},{24,16},{32,24},{40,32},{48,40},{56,48},{64,56},{72,6... | collective-permute-start | bytes 196616 | tf_op jit(solution)/shard_map/ppermute | solution.py:24
  16.4 326.3 %reduce-scatter.3.cloned.1.call-start = ((), (), s32[]{:S(2)}) async-start(), calls=%async_computation.4 | async-start | bytes 1179648 | tf_op jit(solution)/shard_map/reduce_scatter | solution.py:326
  21.5 17.5 %collective-permute-start.3 = (bf16[2,8,2,8,1024]{4,3,2,1,0:T(8,128)(2,1)S(1)}, bf16[2,8,2,8,1024]{4,3,2,1,0:T(8,128)(2,1)S(1)}, u32[]{:S(2)}, u32[]{:S(2)}) collective-permute-start(bf16[2,8,2,8,1024]{4,3,2,1,0:T(8,128)(2,1)S(1)} %get-tuple-element.331), channel_id=1, source_target_pairs={{1,0},{2,1},{3,2},{4,3},{5,4},{6,5},{7,6},{0,7},{9,8},{10,9},{11,1... | collective-permute-start | bytes 1572872 | tf_op jit(solution)/shard_map/ppermute | solution.py:24
  26.8 18.4 %collective-permute-start.2 = (bf16[2,8,2,8,1024]{4,3,2,1,0:T(8,128)(2,1)S(1)}, bf16[2,8,2,8,1024]{4,3,2,1,0:T(8,128)(2,1)S(1)}, u32[]{:S(2)}, u32[]{:S(2)}) collective-permute-start(bf16[2,8,2,8,1024]{4,3,2,1,0:T(8,128)(2,1)S(1)} %get-tuple-element.330), channel_id=1, source_target_pairs={{0,1},{1,2},{2,3},{3,4},{4,5},{5,6},{6,7},{7,0},{8,9},{9,10},{10,1... | collective-permute-start | bytes 1572872 | tf_op jit(solution)/shard_map/ppermute | solution.py:22
  51.5 19.8 %copy-start.7 = (bf16[4,64,16,64]{3,2,1,0:T(8,128)(2,1)}, bf16[4,64,16,64]{3,2,1,0:T(8,128)(2,1)S(1)}, u32[]{:S(2)}) copy-start(bf16[4,64,16,64]{3,2,1,0:T(8,128)(2,1)S(1)} %reshape.864) | copy-start | bytes 1572868
  53.5 18.6 %copy-start.9 = (bf16[4,64,16,64]{3,2,1,0:T(8,128)(2,1)}, bf16[4,64,16,64]{3,2,1,0:T(8,128)(2,1)S(1)}, u32[]{:S(2)}) copy-start(bf16[4,64,16,64]{3,2,1,0:T(8,128)(2,1)S(1)} %reshape.862) | copy-start | bytes 1572868
  125.1 19.9 %copy-start.30 = (bf16[4,32,1024]{2,1,0:T(8,128)(2,1)S(1)}, bf16[4,32,1024]{2,1,0:T(8,128)(2,1)}, u32[]{:S(2)}) copy-start(bf16[4,32,1024]{2,1,0:T(8,128)(2,1)} %param.43) | copy-start | bytes 786436
  125.8 4.2 %collective-permute-start.5 = (bf16[1,32,1024]{2,1,0:T(8,128)(2,1)S(1)}, bf16[1,32,1024]{2,1,0:T(8,128)(2,1)S(1)}, u32[]{:S(2)}, u32[]{:S(2)}) collective-permute-start(bf16[1,32,1024]{2,1,0:T(8,128)(2,1)S(1)} %get-tuple-element.341), channel_id=1, source_target_pairs={{8,0},{16,8},{24,16},{32,24},{40,32},{48,40},{56,48},{64,56},{72,6... | collective-permute-start | bytes 196616 | tf_op jit(solution)/shard_map/ppermute | solution.py:24
  125.9 4.7 %collective-permute-start.4 = (bf16[1,32,1024]{2,1,0:T(8,128)(2,1)S(1)}, bf16[1,32,1024]{2,1,0:T(8,128)(2,1)S(1)}, u32[]{:S(2)}, u32[]{:S(2)}) collective-permute-start(bf16[1,32,1024]{2,1,0:T(8,128)(2,1)S(1)} %get-tuple-element.340), channel_id=1, source_target_pairs={{0,8},{8,16},{16,24},{24,32},{32,40},{40,48},{48,56},{56,64},{64,7... | collective-permute-start | bytes 196616 | tf_op jit(solution)/shard_map/ppermute | solution.py:22
  127.4 9.7 %collective-permute-start.11 = (bf16[6,1,1024]{2,1,0:T(2,128)(2,1)S(1)}, bf16[6,1,1024]{2,1,0:T(2,128)(2,1)S(1)}, u32[]{:S(2)}, u32[]{:S(2)}) collective-permute-start(bf16[6,1,1024]{2,1,0:T(2,128)(2,1)S(1)} %get-tuple-element.335), channel_id=1, source_target_pairs={{1,0},{2,1},{3,2},{4,3},{5,4},{6,5},{7,6},{0,7},{9,8},{10,9},{11,1... | collective-permute-start | bytes 36872 | tf_op jit(solution)/shard_map/ppermute | solution.py:24
  130.1 7.4 %collective-permute-start.10 = (bf16[6,1,1024]{2,1,0:T(2,128)(2,1)S(1)}, bf16[6,1,1024]{2,1,0:T(2,128)(2,1)S(1)}, u32[]{:S(2)}, u32[]{:S(2)}) collective-permute-start(bf16[6,1,1024]{2,1,0:T(2,128)(2,1)S(1)} %get-tuple-element.334), channel_id=1, source_target_pairs={{0,1},{1,2},{2,3},{3,4},{4,5},{5,6},{6,7},{7,0},{8,9},{9,10},{10,1... | collective-permute-start | bytes 36872 | tf_op jit(solution)/shard_map/ppermute | solution.py:22
  130.6 6.9 %collective-permute-start.7 = (bf16[6,1,1024]{2,1,0:T(2,128)(2,1)S(1)}, bf16[6,1,1024]{2,1,0:T(2,128)(2,1)S(1)}, u32[]{:S(2)}, u32[]{:S(2)}) collective-permute-start(bf16[6,1,1024]{2,1,0:T(2,128)(2,1)S(1)} %get-tuple-element.337), channel_id=1, source_target_pairs={{1,0},{2,1},{3,2},{4,3},{5,4},{6,5},{7,6},{0,7},{9,8},{10,9},{11,1... | collective-permute-start | bytes 36872 | tf_op jit(solution)/shard_map/ppermute | solution.py:24
  135.9 7.7 %collective-permute-start.6 = (bf16[6,1,1024]{2,1,0:T(2,128)(2,1)S(1)}, bf16[6,1,1024]{2,1,0:T(2,128)(2,1)S(1)}, u32[]{:S(2)}, u32[]{:S(2)}) collective-permute-start(bf16[6,1,1024]{2,1,0:T(2,128)(2,1)S(1)} %get-tuple-element.336), channel_id=1, source_target_pairs={{0,1},{1,2},{2,3},{3,4},{4,5},{5,6},{6,7},{7,0},{8,9},{9,10},{10,1... | collective-permute-start | bytes 36872 | tf_op jit(solution)/shard_map/ppermute | solution.py:22
  161.7 23.0 %copy-start.35 = (bf16[4,16,32,64]{3,2,1,0:T(8,128)(2,1)}, bf16[4,16,32,64]{3,2,1,0:T(8,128)(2,1)S(1)}, u32[]{:S(2)}) copy-start(bf16[4,16,32,64]{3,2,1,0:T(8,128)(2,1)S(1)} %fusion.49) | copy-start | bytes 786436
  197.5 174.6 %reduce-scatter.5.cloned.1.call-start = ((), (), s32[]{:S(2)}) async-start(), calls=%async_computation.5 | async-start | bytes 1179648 | tf_op jit(solution)/shard_map/reduce_scatter | solution.py:329
  198.4 36.9 %collective-permute-start.12 = (bf16[2,2,64,1024]{3,2,1,0:T(8,128)(2,1)}, bf16[2,2,64,1024]{3,2,1,0:T(8,128)(2,1)}, u32[]{:S(2)}, u32[]{:S(2)}) collective-permute-start(bf16[2,2,64,1024]{3,2,1,0:T(8,128)(2,1)} %pad_maximum_fusion.3), channel_id=1, source_target_pairs={{8,0},{16,8},{24,16},{32,24},{40,32},{48,40},{56,48},{64,56},{72,6... | collective-permute-start | bytes 1572872 | tf_op jit(solution)/shard_map/ppermute | solution.py:34
  207.8 29.1 %collective-permute-start.13 = (bf16[2,2,64,1024]{3,2,1,0:T(8,128)(2,1)}, bf16[2,2,64,1024]{3,2,1,0:T(8,128)(2,1)}, u32[]{:S(2)}, u32[]{:S(2)}) collective-permute-start(bf16[2,2,64,1024]{3,2,1,0:T(8,128)(2,1)} %pad_maximum_fusion.4), channel_id=1, source_target_pairs={{0,8},{8,16},{16,24},{24,32},{32,40},{40,48},{48,56},{56,64},{64,7... | collective-permute-start | bytes 1572872 | tf_op jit(solution)/shard_map/ppermute | solution.py:34
  239.3 101.2 %collective-permute-start.14 = (bf16[2,4,16,1024]{3,2,1,0:T(8,128)(2,1)}, bf16[2,4,16,1024]{3,2,1,0:T(8,128)(2,1)}, u32[]{:S(2)}, u32[]{:S(2)}) collective-permute-start(bf16[2,4,16,1024]{3,2,1,0:T(8,128)(2,1)} %get-tuple-element.329), channel_id=1, source_target_pairs={{1,0},{2,1},{3,2},{4,3},{5,4},{6,5},{7,6},{0,7},{9,8},{10,9},{11,1... | collective-permute-start | bytes 786440 | tf_op jit(solution)/shard_map/ppermute | solution.py:40
  240.5 101.0 %collective-permute-start.15 = (bf16[2,4,16,1024]{3,2,1,0:T(8,128)(2,1)}, bf16[2,4,16,1024]{3,2,1,0:T(8,128)(2,1)S(1)}, u32[]{:S(2)}, u32[]{:S(2)}) collective-permute-start(bf16[2,4,16,1024]{3,2,1,0:T(8,128)(2,1)} %get-tuple-element.328), channel_id=1, source_target_pairs={{7,0},{0,1},{1,2},{2,3},{3,4},{4,5},{5,6},{6,7},{15,8},{8,9},{9,10... | collective-permute-start | bytes 786440 | tf_op jit(solution)/shard_map/ppermute | solution.py:40
  (82 other events, 352.8 us)
Sparse Core Ops, SparseCore 0:
  11.3 59.1 all-gather.2
  73.6 51.3 all-gather.4
  197.7 93.9 reduce-scatter.2
  295.9 76.1 reduce-scatter.4
where the time goes:
time: 387 us; the launch traced here: 381 us
  blocking collectives  97.2 us (25%)
  waiting for transfers between devices  92.6 us (24%)
  local copies, waits for them, and re-layouts  75 us (19%)
  matrix products  43.9 us (11%)
  other arithmetic  31.6 us (8%)
  starting transfers between devices  23.9 us (6%)
  between operations  16.2 us (4%)
    psum x1, blocking collectives, body(): kernel_grad = lax.psum(jnp.stack(taps) * norm_factor, ('lat', 'lon'))  97.2 us
    all_gather x1, waiting for transfers between devices, body(): lax.all_gather(cand_value, 'lon', axis=1, tiled=True)  40.1 us
    reduce_scatter x1, waiting for transfers between devices, body(): lax.psum_scatter(pole_terms_value.astype(jnp.bfloat16), 'lon', scatter_di...  27.9 us
    reshape x14, local copies, waits for them, and re-layouts, split_heads(): return array.reshape(array.shape[:-1] + (HEADS, HEAD))  25 us
    ppermute x6, starting transfers between devices, padded_2(): lax.ppermute(head, axis, [((i + 1) % count, i) for i in range(count)])  15.4 us
    dot_general x5, matrix products, window_backward(): jnp.einsum('rhqk,rqhd->rkhd', dscore, query_heads, preferred_element_type...  14.7 us
    ppermute x6, waiting for transfers between devices, padded_2(): lax.ppermute(tail, axis, [(i, (i + 1) % count) for i in range(count)])  13.1 us
    ppermute x6, waiting for transfers between devices, padded_2(): lax.ppermute(head, axis, [((i + 1) % count, i) for i in range(count)])  11.4 us
  transfers between devices with their start and end apart: 20, of which 7 were waited for; matrix products, arithmetic and copies ran while one was open for 23% of the time, Pallas kernels for 0%

commit v1 on v0

v1 whole, which is shorter than its diff:
```python
import functools

import jax
import jax.numpy as jnp
import numpy as np
from jax import lax
from jax.experimental import pallas as pl
from jax.experimental.pallas import tpu as pltpu
from jax.sharding import PartitionSpec as P

HEADS = 16
HEAD = 64
BLK = 8
REACH = 2
NLAT = 128
NLON = 256
ROWS = 4
COLS = 32
SIDE = REACH * BLK
LANES = 128
PAIRS = 8
NEG = -1e30
SCALE = HEAD ** (-0.5)
F32 = jnp.float32
BF16 = jnp.bfloat16

LON_TOK = 144
LAT_TOK = 304
BACK_LAT = 288
BACK_LON = 144
POLE_IN = 320
POLE_OUT = 272


def params(mib, steps=1):
    return pltpu.CompilerParams(
        vmem_limit_bytes=mib * 2**20, dimension_semantics=("arbitrary",) * steps
    )


def lane_spec(*lead):
    zeros = (0,) * len(lead)
    return pl.BlockSpec(lead + (LANES,), lambda j: zeros + (j,))


SMEM = pl.BlockSpec(memory_space=pltpu.SMEM)


def nt(lhs, rhs):
    return lax.dot_general(lhs, rhs, (((1,), (1,)), ((), ())), preferred_element_type=F32)


def tn(lhs, rhs):
    return lax.dot_general(lhs, rhs, (((0,), (0,)), ((), ())), preferred_element_type=F32)


def nn(lhs, rhs):
    return lax.dot_general(lhs, rhs, (((1,), (0,)), ((), ())), preferred_element_type=F32)


def two_heads(array):
    first = lax.broadcasted_iota(jnp.int32, array.shape, 1) < HEAD
    return jnp.concatenate(
        [jnp.where(first, array, 0.0), jnp.where(first, 0.0, array)], axis=0
    ).astype(BF16)


def own_features(array):
    half = array.shape[1] // 2
    first = lax.broadcasted_iota(jnp.int32, (LANES, half), 0) < HEAD
    return jnp.where(first, array[:, :half], array[:, half:])


def attention(query, key, value, d_att, bias, valid):
    query2 = two_heads(query * SCALE)
    grad2 = two_heads(d_att)
    scores = nt(key, query2)
    if bias is not None:
        scores = scores + jnp.concatenate([bias, bias], axis=1)
    top = jnp.max(scores, axis=0, keepdims=True)
    weights = jnp.exp(scores - top)
    inverse = 1.0 / jnp.sum(weights, axis=0, keepdims=True)
    if valid is not None:
        inverse = inverse * jnp.concatenate([valid, valid], axis=1)
    att_t = own_features(tn(value, weights.astype(BF16)) * inverse).astype(BF16).astype(F32)
    product = d_att.T * att_t
    delta = jnp.concatenate(
        [
            jnp.sum(product[:HEAD], axis=0, keepdims=True),
            jnp.sum(product[HEAD:], axis=0, keepdims=True),
        ],
        axis=1,
    )
    probs = weights * inverse
    dscore = (probs * (nt(value, grad2) - delta)).astype(BF16)
    d_query = own_features(tn(key, dscore)).T * SCALE
    d_key = nn(dscore, query2)
    d_value = nn(probs.astype(BF16), grad2)
    return att_t.T, d_query, d_key, d_value


def pack_lon_kernel(pole_ref, q_ref, k_ref, v_ref, c_ref, east_ref, west_ref, pole_out, edge):
    half = ROWS * SIDE
    for out, start, col in ((east_ref, COLS - SIDE, COLS - 1), (west_ref, 0, 0)):
        out[0:half] = k_ref[:, start : start + SIDE].reshape(half, LANES)
        out[half : 2 * half] = v_ref[:, start : start + SIDE].reshape(half, LANES)
        edge[...] = jnp.zeros_like(edge)
        for row in range(ROWS):
            cells = c_ref[row].astype(F32)
            edge[row : row + 1] = cells[col : col + 1]
        out[2 * half :] = edge[...].astype(BF16)
    start = pole_ref[0]
    both = REACH * COLS
    pole_out[0, 0:both] = q_ref[pl.ds(start, REACH)].reshape(both, LANES)
    pole_out[0, both : 2 * both] = k_ref[pl.ds(start, REACH)].reshape(both, LANES)
    pole_out[0, 2 * both : 3 * both] = v_ref[pl.ds(start, REACH)].reshape(both, LANES)
    pole_out[0, 3 * both :] = c_ref[...].reshape(ROWS * COLS, LANES)


def pack_lat_kernel(k_ref, v_ref, c_ref, w_ref, e_ref, south_ref, north_ref, edge):
    own = REACH * COLS
    side = REACH * SIDE
    half = ROWS * SIDE
    west_cot = w_ref[2 * half :].astype(F32)
    east_cot = e_ref[2 * half :].astype(F32)
    for out, start, row in ((south_ref, ROWS - REACH, ROWS - 1), (north_ref, 0, 0)):
        for index, ref in enumerate((k_ref, v_ref)):
            base = index * (own + 2 * side)
            near = index * half + start * SIDE
            out[base : base + own] = ref[start : start + REACH].reshape(own, LANES)
            out[base + own : base + own + side] = w_ref[near : near + side]
            out[base + own + side : base + own + 2 * side] = e_ref[near : near + side]
        base = 2 * (own + 2 * side)
        out[base : base + COLS] = c_ref[row]
        edge[...] = jnp.zeros_like(edge)
        edge[0:1] = west_cot[row : row + 1]
        edge[1:2] = east_cot[row : row + 1]
        out[base + COLS :] = edge[...].astype(BF16)


def fill_rim(pad, row, middle, west, east):
    pad[row, 8 : 8 + COLS] = middle
    pad[row, 7:8] = west
    pad[row, 8 + COLS : 9 + COLS] = east


def window_kernel(
    q_ref, k_ref, v_ref, c_ref, w_ref, e_ref, n_ref, s_ref, conv_ref, bias_ref, valid_ref,
    att_ref, dq_ref, south_ref, north_ref, mid_ref, kg_ref, pad,
):
    tokens = ROWS * COLS
    half = ROWS * SIDE
    rim = 2 * REACH * SIDE + REACH * COLS
    west_cot = w_ref[2 * half :].astype(F32)
    east_cot = e_ref[2 * half :].astype(F32)
    for row in range(ROWS):
        fill_rim(
            pad, row + 1, c_ref[row].astype(F32), west_cot[row : row + 1], east_cot[row : row + 1]
        )
    for row, ref in ((0, n_ref), (ROWS + 1, s_ref)):
        cells = ref[2 * rim :].astype(F32)
        fill_rim(pad, row, cells[:COLS], cells[COLS : COLS + 1], cells[COLS + 1 : COLS + 2])
    back = c_ref[...].astype(F32)
    for a in range(3):
        for b in range(3):
            weight = conv_ref[3 * a + b : 3 * a + b + 1][None]
            back = back + weight * pad[2 - a : 2 - a + ROWS, 9 - b : 9 - b + COLS]
    d_att = back.astype(BF16).astype(F32).reshape(tokens, LANES)
    key = jnp.concatenate(
        [k_ref[...].reshape(tokens, LANES), w_ref[:half], e_ref[:half], n_ref[:rim], s_ref[:rim]],
        axis=0,
    )
    value = jnp.concatenate(
        [
            v_ref[...].reshape(tokens, LANES),
            w_ref[half : 2 * half],
            e_ref[half : 2 * half],
            n_ref[rim : 2 * rim],
            s_ref[rim : 2 * rim],
        ],
        axis=0,
    )
    query = q_ref[...].reshape(tokens, LANES).astype(F32)
    att, d_query, d_key, d_value = attention(
        query, key, value, d_att, bias_ref[...], valid_ref[...]
    )
    att_b = att.astype(BF16)
    att_ref[...] = att_b
    dq_ref[...] = d_query.astype(BF16)
    near = tokens + 2 * half
    mid_ref[0] = d_key[:near]
    mid_ref[1] = d_value[:near]
    for ref, start, row in ((north_ref, near, 0), (south_ref, near + rim, ROWS - 1)):
        ref[:rim] = d_key[start : start + rim].astype(BF16)
        ref[rim : 2 * rim] = d_value[start : start + rim].astype(BF16)
        ref[2 * rim :] = att_b[row * COLS : (row + 1) * COLS]
    att3 = att.reshape(ROWS, COLS, LANES)
    for a in range(3):
        for b in range(3):
            shifted = pad[2 - a : 2 - a + ROWS, 9 - b : 9 - b + COLS]
            total = jnp.sum((att3 * shifted).reshape(tokens, LANES), axis=0, keepdims=True)
            kg_ref[0, 3 * a + b : 3 * a + b + 1] = total


def pole_kernel(flag_ref, x_ref, conv_ref, y_ref, kg_ref, edge):
    both = REACH * COLS
    kg_ref[...] = jnp.zeros_like(kg_ref)

    @pl.when(flag_ref[1] + flag_ref[2] > 0)
    def _():
        edge[...] = jnp.zeros_like(edge)
        weights = conv_ref[0]
        rows = []
        for step in range(REACH + 2):
            row = flag_ref[0] + step - 1
            inside = jnp.where((row >= 0) & (row < ROWS), 1.0, 0.0)
            at = pl.multiple_of(3 * both + jnp.clip(row, 0, ROWS - 1) * COLS, COLS)
            rows.append(x_ref[:, pl.ds(at, COLS)].reshape(NLON, LANES).astype(F32) * inside)
        for r in range(REACH):
            taps = []
            back = rows[r + 1]
            for a in range(3):
                cells = rows[r + 2 - a]
                for b, shifted in enumerate(
                    (pltpu.roll(cells, NLON - 1, 0), cells, pltpu.roll(cells, 1, 0))
                ):
                    taps.append(shifted)
                    back = back + weights[3 * a + b : 3 * a + b + 1] * shifted
            query, key, value = (
                x_ref[:, part * both + r * COLS : part * both + (r + 1) * COLS].reshape(NLON, LANES)
                for part in range(3)
            )
            d_att = back.astype(BF16).astype(F32)
            att, d_query, d_key, d_value = attention(
                query.astype(F32), key, value, d_att, None, None
            )
            for part, array in enumerate((att, d_query, d_key, d_value)):
                y_ref[:, part * both + r * COLS : part * both + (r + 1) * COLS] = array.astype(
                    BF16
                ).reshape(PAIRS, COLS, LANES)
            for dest in range(PAIRS):
                west = (dest * COLS - 1) % NLON
                east = (dest * COLS + COLS) % NLON
                edge[dest, 2 * r : 2 * r + 1] = att[west : west + 1]
                edge[dest, 2 * r + 1 : 2 * r + 2] = att[east : east + 1]
            counted = jnp.where(flag_ref[1 + r] > 0, 1.0, 0.0)
            for tap in range(9):
                kg_ref[tap : tap + 1] += counted * jnp.sum(
                    att * taps[tap], axis=0, keepdims=True
                )
        y_ref[:, 4 * both :] = edge[...].astype(BF16)


def pack_back_kernel(mid_ref, att_ref, n_ref, s_ref, west_ref, east_ref, edge):
    half = ROWS * SIDE
    side = REACH * SIDE
    own = REACH * COLS
    rim = own + 2 * side
    for out, first, col in ((west_ref, 0, 0), (east_ref, 1, COLS - 1)):
        for index in range(2):
            source = index * rim + own + first * side
            cells = mid_ref[index, first * half : (first + 1) * half]
            out[index * half : index * half + side] = (
                cells[:side] + n_ref[source : source + side].astype(F32)
            ).astype(BF16)
            out[index * half + side : (index + 1) * half] = (
                cells[side:] + s_ref[source : source + side].astype(F32)
            ).astype(BF16)
        edge[...] = jnp.zeros_like(edge)
        edge[0:1] = n_ref[2 * rim :].astype(F32)[col : col + 1]
        edge[ROWS + 1 : ROWS + 2] = s_ref[2 * rim :].astype(F32)[col : col + 1]
        for row in range(ROWS):
            cells = att_ref[row * COLS : (row + 1) * COLS].astype(F32)
            edge[row + 1 : row + 2] = cells[col : col + 1]
        out[2 * half :] = edge[...].astype(BF16)


def final_kernel(
    flag_ref, att_ref, dq_ref, mid_ref, n_ref, s_ref, w_ref, e_ref, y_ref, conv_ref,
    mixed_out, dq_out, dk_out, dv_out, pad, dk_sum, dv_sum,
):
    half = ROWS * SIDE
    own = REACH * COLS
    both = own
    rim = own + 2 * REACH * SIDE
    west_att = w_ref[2 * half :].astype(F32)
    east_att = e_ref[2 * half :].astype(F32)
    middles = [n_ref[2 * rim :].astype(F32)]
    middles += [att_ref[row * COLS : (row + 1) * COLS].astype(F32) for row in range(ROWS)]
    middles += [s_ref[2 * rim :].astype(F32)]
    for row in range(ROWS + 2):
        fill_rim(pad, row, middles[row], west_att[row : row + 1], east_att[row : row + 1])
    dq_out[...] = dq_ref[...].reshape(ROWS, COLS, LANES)
    for index, total, factor in ((0, dk_sum, 1.0), (1, dv_sum, 1.0)):
        north = n_ref[index * rim : index * rim + own].astype(F32)
        south = s_ref[index * rim : index * rim + own].astype(F32)
        cells = mid_ref[index] + jnp.concatenate([north, south], axis=0)
        sides = jnp.concatenate(
            [
                w_ref[index * half : (index + 1) * half].astype(F32).reshape(ROWS, SIDE, LANES),
                e_ref[index * half : (index + 1) * half].astype(F32).reshape(ROWS, SIDE, LANES),
            ],
            axis=1,
        )
        total[...] = cells.reshape(ROWS, COLS, LANES) + sides
    start = flag_ref[0]
    for r in range(REACH):

        @pl.when(flag_ref[1 + r] > 0)
        def _():
            row = start + r
            ends = y_ref[0, 4 * both : POLE_OUT].astype(F32)
            part = [
                y_ref[0, p * both + r * COLS : p * both + (r + 1) * COLS] for p in range(4)
            ]
            fill_rim(
                pad,
                row + 1,
                part[0].astype(F32),
                ends[2 * r : 2 * r + 1],
                ends[2 * r + 1 : 2 * r + 2],
            )
            dq_out[row] = part[1]
            dk_sum[row] += part[2].astype(F32)
            dv_sum[row] += part[3].astype(F32)

    dk_out[...] = dk_sum[...].astype(BF16)
    dv_out[...] = dv_sum[...].astype(BF16)
    mixed = pad[1 : 1 + ROWS, 8 : 8 + COLS]
    for a in range(3):
        for b in range(3):
            weight = conv_ref[3 * a + b : 3 * a + b + 1][None]
            mixed = mixed + weight * pad[a : a + ROWS, 7 + b : 7 + b + COLS]
    mixed_out[...] = mixed.astype(BF16)


def key_places():
    rows, cols = [], []

    def add(row_range, col_range):
        for row in row_range:
            for col in col_range:
                rows.append(row)
                cols.append(col)

    inner, west, east = range(COLS), range(-SIDE, 0), range(COLS, COLS + SIDE)
    for part in (inner, west, east):
        add(range(ROWS), part)
    for row_range in (range(-REACH, 0), range(ROWS, ROWS + REACH)):
        for part in (inner, west, east):
            add(row_range, part)
    return np.array(rows, np.int32), np.array(cols, np.int32)


def shift(array, axis, step, wrap):
    count = lax.axis_size(axis)
    route = [(i, (i + step) % count) for i in range(count) if wrap or 0 <= i + step < count]
    return lax.ppermute(array, axis, route)


def sds(shape, dtype=BF16):
    return jax.ShapeDtypeStruct(shape, dtype)


def cost(flops, moved):
    return pl.CostEstimate(flops=flops, bytes_accessed=moved, transcendentals=0)


def body(queries, keys, values, conv_kernel, cotangent, pattern, polar):
    width = queries.shape[2]
    lat_count = lax.axis_size("lat")
    lat = lax.axis_index("lat")
    lon = lax.axis_index("lon")
    row_base = lat * ROWS
    tokens = ROWS * COLS
    full_rows = lane_spec(ROWS, COLS)
    edge = pltpu.VMEM((16, LANES), F32)
    rim_pad = pltpu.VMEM((ROWS + 2, 48, LANES), F32)

    own_polar = lax.dynamic_slice_in_dim(polar, row_base, ROWS, 0)
    pole_start = jnp.where(lat == 0, 0, ROWS - REACH).astype(jnp.int32)
    pole_flags = lax.dynamic_slice_in_dim(own_polar, pole_start, REACH, 0)
    flags = jnp.concatenate([pole_start[None], pole_flags]).astype(jnp.int32)

    east_pay, west_pay, pole_pay = pl.pallas_call(
        pack_lon_kernel,
        grid=(PAIRS,),
        in_specs=[SMEM] + [full_rows] * 4,
        out_specs=[
            lane_spec(LON_TOK),
            lane_spec(LON_TOK),
            pl.BlockSpec((1, POLE_IN, LANES), lambda j: (j, 0, 0)),
        ],
        out_shape=[
            sds((LON_TOK, width)),
            sds((LON_TOK, width)),
            sds((PAIRS, POLE_IN, LANES)),
        ],
        scratch_shapes=[edge],
        compiler_params=params(16),
        cost_estimate=cost(0, 3 * 2**20),
        name="pack_lon",
    )(flags, queries, keys, values, cotangent)
    from_west = shift(east_pay, "lon", 1, True)
    from_east = shift(west_pay, "lon", -1, True)
    pole_in = lax.all_to_all(pole_pay, "lon", 0, 0)

    south_pay, north_pay = pl.pallas_call(
        pack_lat_kernel,
        grid=(PAIRS,),
        in_specs=[full_rows] * 3 + [lane_spec(LON_TOK)] * 2,
        out_specs=[lane_spec(LAT_TOK)] * 2,
        out_shape=[sds((LAT_TOK, width))] * 2,
        scratch_shapes=[edge],
        compiler_params=params(16),
        cost_estimate=cost(0, 3 * 2**20),
        name="pack_lat",
    )(keys, values, cotangent, from_west, from_east)
    from_north = shift(south_pay, "lat", 1, False)
    from_south = shift(north_pay, "lat", -1, False)

    key_row, key_col = key_places()
    query_row, query_col = np.divmod(np.arange(tokens, dtype=np.int32), COLS)
    window = lax.dynamic_slice_in_dim(pattern, row_base, ROWS, 0)
    offset = jnp.repeat(window[:, 0], COLS)[None, :]
    count = jnp.repeat(window[:, 1], COLS)[None, :]
    distance = (key_col // BLK)[:, None] - (query_col // BLK)[None, :] - offset
    near = np.abs(key_row[:, None] - query_row[None, :]) <= REACH
    inside = (row_base + key_row >= 0) & (row_base + key_row < lat_count * ROWS)
    allowed = near & inside[:, None] & (distance >= 0) & (distance < count)
    bias = jnp.where(allowed, 0.0, NEG).astype(F32)
    valid = jnp.repeat(jnp.where(own_polar > 0, 0.0, 1.0).astype(F32), COLS)[None, :]

    pole_out, pole_kg = pl.pallas_call(
        pole_kernel,
        in_specs=[
            SMEM,
            pl.BlockSpec(memory_space=pltpu.VMEM),
            pl.BlockSpec(memory_space=pltpu.VMEM),
        ],
        out_specs=[pl.BlockSpec(memory_space=pltpu.VMEM)] * 2,
        out_shape=[sds((PAIRS, POLE_OUT, LANES)), sds((16, LANES), F32)],
        scratch_shapes=[pltpu.VMEM((PAIRS, 16, LANES), F32)],
        compiler_params=params(24, 0),
        cost_estimate=cost(10**9, 4 * 2**20),
        name="pole",
    )(
        flags,
        pole_in,
        lax.dynamic_slice_in_dim(
            conv_kernel.reshape(9, PAIRS, LANES), lon, 1, 1
        ).reshape(1, 9, LANES),
    )

    att, dq_near, south_back, north_back, mid, kg = pl.pallas_call(
        window_kernel,
        grid=(PAIRS,),
        in_specs=[full_rows] * 4
        + [lane_spec(LON_TOK)] * 2
        + [lane_spec(LAT_TOK)] * 2
        + [
            lane_spec(9),
            pl.BlockSpec((4 * tokens, tokens), lambda j: (0, 0)),
            pl.BlockSpec((1, tokens), lambda j: (0, 0)),
        ],
        out_specs=[
            lane_spec(tokens),
            lane_spec(tokens),
            lane_spec(BACK_LAT),
            lane_spec(BACK_LAT),
            lane_spec(2, 2 * tokens),
            pl.BlockSpec((1, 16, LANES), lambda j: (j, 0, 0)),
        ],
        out_shape=[
            sds((tokens, width)),
            sds((tokens, width)),
            sds((BACK_LAT, width)),
            sds((BACK_LAT, width)),
            sds((2, 2 * tokens, width), F32),
            sds((PAIRS, 16, LANES), F32),
        ],
        scratch_shapes=[rim_pad],
        compiler_params=params(24),
        cost_estimate=cost(4 * 10**9, 8 * 2**20),
        name="window",
    )(
        queries, keys, values, cotangent, from_west, from_east, from_north, from_south,
        conv_kernel, bias, valid,
    )

    back_north = shift(south_back, "lat", 1, False)
    back_south = shift(north_back, "lat", -1, False)

    mine = (jnp.arange(PAIRS) == lon)[:, None, None]
    kg = (kg + jnp.where(mine, pole_kg[None], 0.0))[:, :9].reshape(PAIRS * 9, LANES)
    high = lax.reduce_precision(kg, 8, 7)
    low = kg - high
    kg_pay = jnp.concatenate([high, low], axis=0).astype(BF16)
    back_pay = jnp.concatenate(
        [pole_out, jnp.broadcast_to(kg_pay[None], (PAIRS,) + kg_pay.shape)], axis=1
    )
    pole_back = lax.all_to_all(back_pay, "lon", 0, 0)
    kg_parts = jnp.sum(pole_back[:, POLE_OUT:].astype(F32), axis=0)
    kg_sum = kg_parts[: PAIRS * 9] + kg_parts[PAIRS * 9 :]
    step = 1
    while step < lat_count:
        kg_sum = kg_sum + lax.ppermute(kg_sum, "lat", [(i, i ^ step) for i in range(lat_count)])
        step *= 2
    norm_factor = (NLAT * NLON) ** (-0.5)
    kernel_grad = (
        jnp.transpose(kg_sum.reshape(PAIRS, 9, LANES), (1, 0, 2)).reshape(9, width) * norm_factor
    )

    west_back, east_back = pl.pallas_call(
        pack_back_kernel,
        grid=(PAIRS,),
        in_specs=[
            pl.BlockSpec((2, tokens, LANES), lambda j: (0, 1, j)),
            lane_spec(tokens),
            lane_spec(BACK_LAT),
            lane_spec(BACK_LAT),
        ],
        out_specs=[lane_spec(BACK_LON)] * 2,
        out_shape=[sds((BACK_LON, width))] * 2,
        scratch_shapes=[edge],
        compiler_params=params(16),
        cost_estimate=cost(0, 3 * 2**20),
        name="pack_back",
    )(mid, att, back_north, back_south)
    back_east = shift(west_back, "lon", -1, True)
    back_west = shift(east_back, "lon", 1, True)

    total_tok = POLE_OUT + 18 * PAIRS
    mixed, query_grad, key_grad, value_grad = pl.pallas_call(
        final_kernel,
        grid=(PAIRS,),
        in_specs=[
            SMEM,
            lane_spec(tokens),
            lane_spec(tokens),
            pl.BlockSpec((2, tokens, LANES), lambda j: (0, 0, j)),
            lane_spec(BACK_LAT),
            lane_spec(BACK_LAT),
            lane_spec(BACK_LON),
            lane_spec(BACK_LON),
            pl.BlockSpec((1, total_tok, LANES), lambda j: (j, 0, 0)),
            lane_spec(9),
        ],
        out_specs=[full_rows] * 4,
        out_shape=[sds((ROWS, COLS, width))] * 4,
        scratch_shapes=[rim_pad, pltpu.VMEM((ROWS, COLS, LANES), F32), pltpu.VMEM((ROWS, COLS, LANES), F32)],
        compiler_params=params(24),
        cost_estimate=cost(0, 6 * 2**20),
        name="final",
    )(
        flags, att, dq_near, mid, back_north, back_south, back_west, back_east, pole_back,
        conv_kernel,
    )
    return mixed, query_grad, key_grad, value_grad, kernel_grad


def solution(mesh):
    return jax.shard_map(
        body,
        mesh=mesh,
        in_specs=(
            P("lat", "lon", None),
            P("lat", "lon", None),
            P("lat", "lon", None),
            P(),
            P("lat", "lon", None),
            P(),
            P(),
        ),
        out_specs=(
            P("lat", "lon", None),
            P("lat", "lon", None),
            P("lat", "lon", None),
            P("lat", "lon", None),
            P(),
        ),
        check_vma=False,
    )
```

time: 387 us -> 141 us (0.36)
  blocking collectives: 97.2 us -> 0 us
  local copies, waits for them, and re-layouts: 75 us -> 13.8 us
  waiting for transfers between devices: 92.6 us -> 36.5 us
  matrix products: 43.9 us -> 0 us
  starting transfers between devices: 23.9 us -> 56.6 us
  other arithmetic: 31.6 us -> 3.11 us
  Pallas kernels: 0 us -> 27.5 us
  between operations: 16.2 us -> 0.99 us
    psum x1 -> x0, blocking collectives: 97.2 us -> none  [body(): kernel_grad = lax.psum(jnp.stack(taps) * norm_factor, ('lat', 'lon'))]
    dot_general x30 -> x0, matrix products: 43.9 us -> none  [the longest x5 14.7 us: window_backward(): jnp.einsum('rhqk,rqhd->rkhd', dscore, query_heads, preferred_element_type...]
    all_gather x2 -> x0, waiting for transfers between devices: 40.1 us -> none  [the longest x1 40.1 us: body(): lax.all_gather(cand_value, 'lon', axis=1, tiled=True)]
    reduce_scatter x2 -> x0, waiting for transfers between devices: 27.9 us -> none  [the longest x1 27.9 us: body(): lax.psum_scatter(pole_terms_value.astype(jnp.bfloat16), 'lon', scatter_di...]
    pallas_call x0 -> x6, Pallas kernels: none -> 27.5 us  [the longest x1 10.6 us: body(): pl.pallas_call(window_kernel, grid=(PAIRS,), in_specs=[full_rows] * 4 + [...]
    reshape x15 -> x2, local copies, waits for them, and re-layouts: 25.3 us -> 0.01 us  [the longest x1 0.01 us: body(): (kg + jnp.where(mine, pole_kg[None], 0.0))[:, :9].reshape(PAIRS * 9, LANES)]
    ppermute x16 -> x13, starting transfers between devices: 23.8 us -> 45.9 us  [the longest x8 26.4 us: shift(): return lax.ppermute(array, axis, route)]
    slice x19 -> x0, local copies, waits for them, and re-layouts: 14.4 us -> none  [the longest x2 4.33 us: body(): part_key[REACH:REACH + row_count]]
  transfers between devices with their start and end apart: 20 -> 15, of which waited for: 7 -> 8; matrix products, arithmetic and copies ran while one was open for 23% -> 2% of each run, Pallas kernels for 0% -> 10%
where the time goes in v1:
time: 141 us; the launch traced here: 138 us
  starting transfers between devices  56.6 us (40%)
  waiting for transfers between devices  36.5 us (26%)
  Pallas kernels  27.5 us (20%)
  local copies, waits for them, and re-layouts  13.8 us (10%)
  other arithmetic  3.11 us (2%)
    ppermute x8, starting transfers between devices, shift(): return lax.ppermute(array, axis, route)  26.4 us
    ppermute x8, waiting for transfers between devices, shift(): return lax.ppermute(array, axis, route)  19.7 us
    ppermute x5, starting transfers between devices, body(): lax.ppermute(kg_sum, 'lat', [(i, i ^ step) for i in range(lat_count)])  19.6 us
    unnamed x60, local copies, waits for them, and re-layouts  12.4 us
    pallas_call x1, Pallas kernels, body(): pl.pallas_call(window_kernel, grid=(PAIRS,), in_specs=[full_rows] * 4 + [...  10.6 us
    ppermute x5, waiting for transfers between devices, body(): lax.ppermute(kg_sum, 'lat', [(i, i ^ step) for i in range(lat_count)])  10.3 us
    all_to_all x1, starting transfers between devices, body(): pole_in = lax.all_to_all(pole_pay, 'lon', 0, 0)  7.06 us
    all_to_all x1, waiting for transfers between devices, body(): pole_back = lax.all_to_all(back_pay, 'lon', 0, 0)  6.51 us
  transfers between devices with their start and end apart: 15, of which 8 were waited for; matrix products, arithmetic and copies ran while one was open for 2% of the time, Pallas kernels for 10%

profile of v1, /device:TPU:32, one launch (start us, length us, event | category | flops | bytes accessed | tf_op | source)
XLA Modules:
  0.0 138.4 jit_solution(14075503265389036123)
XLA Ops:
  5.3 3.5 %pack_lon.1 = (bf16[144,1024]{1,0:T(8,128)(2,1)S(1)}, bf16[144,1024]{1,0:T(8,128)(2,1)S(1)}, bf16[8,320,128]{2,1,0:T(8,128)(2,1)}) custom-call(s32[3]{0:T(128)S(1)} %pad_add_fusion.pole_ref.flag_ref, bf16[4,32,1024]{2,1,0:T(8,128)(2,1)S(1)} %copy-done.19, bf16[4,32,1024]{2,1,0:T(8,128)(2,1)S(1)} %copy-done.4, bf16[4,32,1024]{2,1,0:T(8,128)(2,1)S(1)} %copy-done.6, ...), custom_call_target="tpu_custom_call" | custom-call | bytes 3145728 | tf_op jit(solution)/shard_map/pack_lon/pallas_call | solution.py:385
  8.8 7.1 %all-to-all-start = ((bf16[8,320,128]{2,1,0:T(8,128)(2,1)}), bf16[8,320,128]{2,1,0:T(8,128)(2,1)S(1)}, u32[]{:S(2)}, u32[]{:S(2)}) async-start(bf16[8,320,128]{2,1,0:T(8,128)(2,1)} %get-tuple-element.35), calls=%async_computation | async-start | bytes 1310720 | tf_op jit(solution)/shard_map/all_to_all | solution.py:406
  15.9 2.0 %collective-permute-start = (bf16[144,1024]{1,0:T(8,128)(2,1)S(1)}, bf16[144,1024]{1,0:T(8,128)(2,1)S(1)}, u32[]{:S(2)}, u32[]{:S(2)}) collective-permute-start(bf16[144,1024]{1,0:T(8,128)(2,1)S(1)} %get-tuple-element.24), channel_id=1, source_target_pairs={{0,1},{1,2},{2,3},{3,4},{4,5},{5,6},{6,7},{7,0},{8,9},{9,10},{10,1... | collective-permute-start | bytes 884744 | tf_op jit(solution)/shard_map/ppermute | solution.py:358
  17.9 3.6 %collective-permute-start.1 = (bf16[144,1024]{1,0:T(8,128)(2,1)S(1)}, bf16[144,1024]{1,0:T(8,128)(2,1)S(1)}, u32[]{:S(2)}, u32[]{:S(2)}) collective-permute-start(bf16[144,1024]{1,0:T(8,128)(2,1)S(1)} %get-tuple-element.25), channel_id=1, source_target_pairs={{0,7},{1,0},{2,1},{3,2},{4,3},{5,4},{6,5},{7,6},{8,15},{9,8},{10,9... | collective-permute-start | bytes 884744 | tf_op jit(solution)/shard_map/ppermute | solution.py:358
  22.3 12.9 %collective-permute-done.w_ref = bf16[144,1024]{1,0:T(8,128)(2,1)S(1)} collective-permute-done((bf16[144,1024]{1,0:T(8,128)(2,1)S(1)}, bf16[144,1024]{1,0:T(8,128)(2,1)S(1)}, u32[]{:S(2)}, u32[]{:S(2)}) %collective-permute-start) | collective-permute-done | bytes 294944 | tf_op jit(solution)/shard_map/ppermute | solution.py:358
  35.2 3.2 %pack_lat.1 = (bf16[304,1024]{1,0:T(8,128)(2,1)}, bf16[304,1024]{1,0:T(8,128)(2,1)}) custom-call(bf16[4,32,1024]{2,1,0:T(8,128)(2,1)S(1)} %copy-done.5, bf16[4,32,1024]{2,1,0:T(8,128)(2,1)S(1)} %copy-done.7, bf16[4,32,1024]{2,1,0:T(8,128)(2,1)S(1)} %copy-done.9, bf16[144,1024]{1,0:T(8,128)(2,1)S(1)} %collective-permute-done.w_ref, ...), custom_call_target="tpu_custom_call" | custom-call | bytes 3145728 | tf_op jit(solution)/shard_map/pack_lat/pallas_call | solution.py:408
  40.4 4.5 %collective-permute-start.3 = (bf16[304,1024]{1,0:T(8,128)(2,1)}, bf16[304,1024]{1,0:T(8,128)(2,1)}, u32[]{:S(2)}, u32[]{:S(2)}) collective-permute-start(bf16[304,1024]{1,0:T(8,128)(2,1)} %get-tuple-element.27), channel_id=1, source_target_pairs={{8,0},{16,8},{24,16},{32,24},{40,32},{48,40},{56,48},{64,56},{72,6... | collective-permute-start | bytes 1867784 | tf_op jit(solution)/shard_map/ppermute | solution.py:358
  47.4 3.9 %collective-permute-done.2.n_ref = bf16[304,1024]{1,0:T(8,128)(2,1)S(1)} collective-permute-done((bf16[304,1024]{1,0:T(8,128)(2,1)}, bf16[304,1024]{1,0:T(8,128)(2,1)S(1)}, u32[]{:S(2)}, u32[]{:S(2)}) %collective-permute-start.2) | collective-permute-done | bytes 622624 | tf_op jit(solution)/shard_map/ppermute | solution.py:358
  56.0 10.6 %window.1 = (bf16[128,1024]{1,0:T(8,128)(2,1)S(1)}, bf16[128,1024]{1,0:T(8,128)(2,1)S(1)}, bf16[288,1024]{1,0:T(8,128)(2,1)S(1)}, bf16[288,1024]{1,0:T(8,128)(2,...) custom-call(bf16[4,32,1024]{2,1,0:T(8,128)(2,1)S(1)} %copy-done.20, bf16[4,32,1024]{2,1,0:T(8,128)(2,1)S(1)} %copy-done.5, ...), custom_call_target="tpu_custom_call" | custom-call | flops 4000000000 | bytes 8388608 | tf_op jit(solution)/shard_map/window/pallas_call | solution.py:455
  70.8 3.5 %all-to-all-start.1 = ((bf16[8,416,128]{2,1,0:T(8,128)(2,1)}), bf16[8,416,128]{2,1,0:T(8,128)(2,1)S(1)}, u32[]{:S(2)}, u32[]{:S(2)}) async-start(bf16[8,416,128]{2,1,0:T(8,128)(2,1)} %pad_maximum_fusion), calls=%async_computation.1 | async-start | bytes 1703936 | tf_op jit(solution)/shard_map/all_to_all | solution.py:502
  74.3 6.6 %collective-permute-start.4 = (bf16[288,1024]{1,0:T(8,128)(2,1)}, bf16[288,1024]{1,0:T(8,128)(2,1)S(1)}, u32[]{:S(2)}, u32[]{:S(2)}) collective-permute-start(bf16[288,1024]{1,0:T(8,128)(2,1)} %copy-done.24), channel_id=1, source_target_pairs={{0,8},{8,16},{16,24},{24,32},{32,40},{40,48},{48,56},{56,64},{64,7... | collective-permute-start | bytes 1769480 | tf_op jit(solution)/shard_map/ppermute | solution.py:358
  80.9 1.9 %collective-permute-start.5 = (bf16[288,1024]{1,0:T(8,128)(2,1)}, bf16[288,1024]{1,0:T(8,128)(2,1)}, u32[]{:S(2)}, u32[]{:S(2)}) collective-permute-start(bf16[288,1024]{1,0:T(8,128)(2,1)} %copy-done.23), channel_id=1, source_target_pairs={{8,0},{16,8},{24,16},{32,24},{40,32},{48,40},{56,48},{64,56},{72,6... | collective-permute-start | bytes 1769480 | tf_op jit(solution)/shard_map/ppermute | solution.py:358
  82.9 6.5 %all-to-all-done.1.y_ref = bf16[8,416,128]{2,1,0:T(8,128)(2,1)S(1)} async-done(((bf16[8,416,128]{2,1,0:T(8,128)(2,1)}), bf16[8,416,128]{2,1,0:T(8,128)(2,1)S(1)}, u32[]{:S(2)}, u32[]{:S(2)}) %all-to-all-start.1) | async-done | bytes 852000 | tf_op jit(solution)/shard_map/all_to_all | solution.py:502
  89.4 2.4 %collective-permute-start.8 = (f32[72,128]{1,0:T(8,128)S(1)}, f32[72,128]{1,0:T(8,128)S(1)}, u32[]{:S(2)}, u32[]{:S(2)}) collective-permute-start(f32[72,128]{1,0:T(8,128)S(1)} %slice_add_fusion.1), channel_id=1, source_target_pairs={{0,8},{8,0},{16,24},{24,16},{32,40},{40,32},{48,56},{56,48},{64,72... | collective-permute-start | bytes 110600 | tf_op jit(solution)/shard_map/ppermute | solution.py:507
  91.9 1.9 %collective-permute-done.4.n_ref = bf16[288,1024]{1,0:T(8,128)(2,1)S(1)} collective-permute-done((bf16[288,1024]{1,0:T(8,128)(2,1)}, bf16[288,1024]{1,0:T(8,128)(2,1)S(1)}, u32[]{:S(2)}, u32[]{:S(2)}) %collective-permute-start.4) | collective-permute-done | bytes 589856 | tf_op jit(solution)/shard_map/ppermute | solution.py:358
  94.8 4.1 %pack_back.1 = (bf16[144,1024]{1,0:T(8,128)(2,1)S(1)}, bf16[144,1024]{1,0:T(8,128)(2,1)S(1)}) custom-call(f32[2,256,1024]{2,1,0:T(8,128)S(1)} %get-tuple-element.30.mid_ref, bf16[128,1024]{1,0:T(8,128)(2,1)S(1)} %copy-done.2, bf16[288,1024]{1,0:T(8,128)(2,1)S(1)} %collective-permute-done.4.n_ref, bf16[288,1024]{1,0:T(8,128)(2,1)} %collective-permute-done.5.s_ref), custom_call_target="tpu_custom_call" | custom-call | bytes 3145728 | tf_op jit(solution)/shard_map/pack_back/pallas_call | solution.py:514
  100.6 4.0 %collective-permute-start.7 = (bf16[144,1024]{1,0:T(8,128)(2,1)S(1)}, bf16[144,1024]{1,0:T(8,128)(2,1)S(1)}, u32[]{:S(2)}, u32[]{:S(2)}) collective-permute-start(bf16[144,1024]{1,0:T(8,128)(2,1)S(1)} %get-tuple-element.34), channel_id=1, source_target_pairs={{0,7},{1,0},{2,1},{3,2},{4,3},{5,4},{6,5},{7,6},{8,15},{9,8},{10,9... | collective-permute-start | bytes 884744 | tf_op jit(solution)/shard_map/ppermute | solution.py:358
  104.6 7.8 %collective-permute-start.9 = (f32[72,128]{1,0:T(8,128)S(1)}, f32[72,128]{1,0:T(8,128)S(1)}, u32[]{:S(2)}, u32[]{:S(2)}) collective-permute-start(f32[72,128]{1,0:T(8,128)S(1)} %fusion.5), channel_id=1, source_target_pairs={{0,16},{8,24},{16,0},{24,8},{32,48},{40,56},{48,32},{56,40},{64,80... | collective-permute-start | bytes 110600 | tf_op jit(solution)/shard_map/ppermute | solution.py:507
  112.5 4.4 %collective-permute-done.9 = f32[72,128]{1,0:T(8,128)S(1)} collective-permute-done((f32[72,128]{1,0:T(8,128)S(1)}, f32[72,128]{1,0:T(8,128)S(1)}, u32[]{:S(2)}, u32[]{:S(2)}) %collective-permute-start.9) | collective-permute-done | bytes 36896 | tf_op jit(solution)/shard_map/ppermute | solution.py:507
  116.9 3.9 %collective-permute-done.10 = f32[72,128]{1,0:T(8,128)S(1)} collective-permute-done((f32[72,128]{1,0:T(8,128)S(1)}, f32[72,128]{1,0:T(8,128)S(1)}, u32[]{:S(2)}, u32[]{:S(2)}) %collective-permute-start.10) | collective-permute-done | bytes 36896 | tf_op jit(solution)/shard_map/ppermute | solution.py:507
  120.8 4.2 %collective-permute-start.11 = (f32[72,128]{1,0:T(8,128)S(1)}, f32[72,128]{1,0:T(8,128)S(1)}, u32[]{:S(2)}, u32[]{:S(2)}) collective-permute-start(f32[72,128]{1,0:T(8,128)S(1)} %add.46), channel_id=1, source_target_pairs={{0,64},{8,72},{16,80},{24,88},{32,96},{40,104},{48,112},{56,120},{... | collective-permute-start | bytes 110600 | tf_op jit(solution)/shard_map/ppermute | solution.py:507
  125.0 1.9 %collective-permute-done.11 = f32[72,128]{1,0:T(8,128)S(1)} collective-permute-done((f32[72,128]{1,0:T(8,128)S(1)}, f32[72,128]{1,0:T(8,128)S(1)}, u32[]{:S(2)}, u32[]{:S(2)}) %collective-permute-start.11) | collective-permute-done | bytes 36896 | tf_op jit(solution)/shard_map/ppermute | solution.py:507
  126.9 5.1 %collective-permute-start.12 = (f32[72,128]{1,0:T(8,128)S(1)}, f32[72,128]{1,0:T(8,128)S(1)}, u32[]{:S(2)}, u32[]{:S(2)}) collective-permute-start(f32[72,128]{1,0:T(8,128)S(1)} %add.47), channel_id=1, source_target_pairs={{0,128},{8,136},{16,144},{24,152},{32,160},{40,168},{48,176},{56,1... | collective-permute-start | bytes 110600 | tf_op jit(solution)/shard_map/ppermute | solution.py:507
  132.1 5.6 %final.1 = (bf16[4,32,1024]{2,1,0:T(8,128)(2,1)}, bf16[4,32,1024]{2,1,0:T(8,128)(2,1)}, bf16[4,32,1024]{2,1,0:T(8,128)(2,1)}, bf16[4,32,1024]{2,1,0:T(8,128)(2,1)}) custom-call(s32[3]{0:T(128)S(1)} %pad_add_fusion.pole_ref.flag_ref, bf16[128,1024]{1,0:T(8,128)(2,1)S(1)} %copy-done.3, bf16[128,1024]{1,0:T(8,128)(2,1)S(1)} %copy-done.17, ...), custom_call_target="tpu_custom_call" | custom-call | bytes 6291456 | tf_op jit(solution)/shard_map/final/pallas_call | solution.py:534
  (103 shorter events, 22.1 us)
Async XLA Ops:
  0.6 21.2 %copy-start.27 = (s32[128]{0:T(128)S(1)}, s32[128]{0:T(128)}, u32[]{:S(2)}) copy-start(s32[128]{0:T(128)} %param.16) | copy-start | bytes 1540
  5.3 29.9 %copy-start.5 = (bf16[4,32,1024]{2,1,0:T(8,128)(2,1)S(1)}, bf16[4,32,1024]{2,1,0:T(8,128)(2,1)}, u32[]{:S(2)}) copy-start(bf16[4,32,1024]{2,1,0:T(8,128)(2,1)} %k_ref.5) | copy-start | bytes 786436
  5.3 29.9 %copy-start.7 = (bf16[4,32,1024]{2,1,0:T(8,128)(2,1)S(1)}, bf16[4,32,1024]{2,1,0:T(8,128)(2,1)}, u32[]{:S(2)}) copy-start(bf16[4,32,1024]{2,1,0:T(8,128)(2,1)} %v_ref.5) | copy-start | bytes 786436
  5.3 29.9 %copy-start.9 = (bf16[4,32,1024]{2,1,0:T(8,128)(2,1)S(1)}, bf16[4,32,1024]{2,1,0:T(8,128)(2,1)}, u32[]{:S(2)}) copy-start(bf16[4,32,1024]{2,1,0:T(8,128)(2,1)} %c_ref.5) | copy-start | bytes 786436
  8.8 36.1 %copy-start.26 = (s32[512]{0:T(512)S(1)}, s32[512]{0:T(512)}, u32[]{:S(2)}) copy-start(s32[512]{0:T(512)} %constant.44.clone) | copy-start | bytes 6148
  8.8 36.2 %copy-start.25 = (pred[512,128]{1,0:T(32,128)(4,1)S(1)}, pred[512,128]{1,0:T(32,128)(4,1)}, u32[]{:S(2)}) copy-start(pred[512,128]{1,0:T(32,128)(4,1)} %constant.45.clone) | copy-start | bytes 196612
  8.8 38.0 %all-to-all-start = ((bf16[8,320,128]{2,1,0:T(8,128)(2,1)}), bf16[8,320,128]{2,1,0:T(8,128)(2,1)S(1)}, u32[]{:S(2)}, u32[]{:S(2)}) async-start(bf16[8,320,128]{2,1,0:T(8,128)(2,1)} %get-tuple-element.35), calls=%async_computation | async-start | bytes 1310720 | tf_op jit(solution)/shard_map/all_to_all | solution.py:406
  15.9 19.3 %collective-permute-start = (bf16[144,1024]{1,0:T(8,128)(2,1)S(1)}, bf16[144,1024]{1,0:T(8,128)(2,1)S(1)}, u32[]{:S(2)}, u32[]{:S(2)}) collective-permute-start(bf16[144,1024]{1,0:T(8,128)(2,1)S(1)} %get-tuple-element.24), channel_id=1, source_target_pairs={{0,1},{1,2},{2,3},{3,4},{4,5},{5,6},{6,7},{7,0},{8,9},{9,10},{10,1... | collective-permute-start | bytes 884744 | tf_op jit(solution)/shard_map/ppermute | solution.py:358
  17.9 17.3 %collective-permute-start.1 = (bf16[144,1024]{1,0:T(8,128)(2,1)S(1)}, bf16[144,1024]{1,0:T(8,128)(2,1)S(1)}, u32[]{:S(2)}, u32[]{:S(2)}) collective-permute-start(bf16[144,1024]{1,0:T(8,128)(2,1)S(1)} %get-tuple-element.25), channel_id=1, source_target_pairs={{0,7},{1,0},{2,1},{3,2},{4,3},{5,4},{6,5},{7,6},{8,15},{9,8},{10,9... | collective-permute-start | bytes 884744 | tf_op jit(solution)/shard_map/ppermute | solution.py:358
  38.5 12.8 %collective-permute-start.2 = (bf16[304,1024]{1,0:T(8,128)(2,1)}, bf16[304,1024]{1,0:T(8,128)(2,1)S(1)}, u32[]{:S(2)}, u32[]{:S(2)}) collective-permute-start(bf16[304,1024]{1,0:T(8,128)(2,1)} %get-tuple-element.26), channel_id=1, source_target_pairs={{0,8},{8,16},{16,24},{24,32},{32,40},{40,48},{48,56},{56,64},{64,7... | collective-permute-start | bytes 1867784 | tf_op jit(solution)/shard_map/ppermute | solution.py:358
  40.4 12.6 %collective-permute-start.3 = (bf16[304,1024]{1,0:T(8,128)(2,1)}, bf16[304,1024]{1,0:T(8,128)(2,1)}, u32[]{:S(2)}, u32[]{:S(2)}) collective-permute-start(bf16[304,1024]{1,0:T(8,128)(2,1)} %get-tuple-element.27), channel_id=1, source_target_pairs={{8,0},{16,8},{24,16},{32,24},{40,32},{48,40},{56,48},{64,56},{72,6... | collective-permute-start | bytes 1867784 | tf_op jit(solution)/shard_map/ppermute | solution.py:358
  70.8 18.6 %all-to-all-start.1 = ((bf16[8,416,128]{2,1,0:T(8,128)(2,1)}), bf16[8,416,128]{2,1,0:T(8,128)(2,1)S(1)}, u32[]{:S(2)}, u32[]{:S(2)}) async-start(bf16[8,416,128]{2,1,0:T(8,128)(2,1)} %pad_maximum_fusion), calls=%async_computation.1 | async-start | bytes 1703936 | tf_op jit(solution)/shard_map/all_to_all | solution.py:502
  74.3 19.5 %collective-permute-start.4 = (bf16[288,1024]{1,0:T(8,128)(2,1)}, bf16[288,1024]{1,0:T(8,128)(2,1)S(1)}, u32[]{:S(2)}, u32[]{:S(2)}) collective-permute-start(bf16[288,1024]{1,0:T(8,128)(2,1)} %copy-done.24), channel_id=1, source_target_pairs={{0,8},{8,16},{16,24},{24,32},{32,40},{40,48},{48,56},{56,64},{64,7... | collective-permute-start | bytes 1769480 | tf_op jit(solution)/shard_map/ppermute | solution.py:358
  80.9 12.9 %collective-permute-start.5 = (bf16[288,1024]{1,0:T(8,128)(2,1)}, bf16[288,1024]{1,0:T(8,128)(2,1)}, u32[]{:S(2)}, u32[]{:S(2)}) collective-permute-start(bf16[288,1024]{1,0:T(8,128)(2,1)} %copy-done.23), channel_id=1, source_target_pairs={{8,0},{16,8},{24,16},{32,24},{40,32},{48,40},{56,48},{64,56},{72,6... | collective-permute-start | bytes 1769480 | tf_op jit(solution)/shard_map/ppermute | solution.py:358
  89.4 15.2 %collective-permute-start.8 = (f32[72,128]{1,0:T(8,128)S(1)}, f32[72,128]{1,0:T(8,128)S(1)}, u32[]{:S(2)}, u32[]{:S(2)}) collective-permute-start(f32[72,128]{1,0:T(8,128)S(1)} %slice_add_fusion.1), channel_id=1, source_target_pairs={{0,8},{8,0},{16,24},{24,16},{32,40},{40,32},{48,56},{56,48},{64,72... | collective-permute-start | bytes 110600 | tf_op jit(solution)/shard_map/ppermute | solution.py:507
  94.8 37.3 %copy-start.3 = (bf16[128,1024]{1,0:T(8,128)(2,1)S(1)}, bf16[128,1024]{1,0:T(8,128)(2,1)}, u32[]{:S(2)}) copy-start(bf16[128,1024]{1,0:T(8,128)(2,1)} %copy-done.1) | copy-start | bytes 786436
  94.8 37.3 %copy-start.15 = (f32[9,1024]{1,0:T(8,128)S(1)}, f32[9,1024]{1,0:T(8,128)}, u32[]{:S(2)}) copy-start(f32[9,1024]{1,0:T(8,128)} %conv_ref.3) | copy-start | bytes 110596
  94.8 37.3 %copy-start.17 = (bf16[128,1024]{1,0:T(8,128)(2,1)S(1)}, bf16[128,1024]{1,0:T(8,128)(2,1)}, u32[]{:S(2)}) copy-start(bf16[128,1024]{1,0:T(8,128)(2,1)} %copy-done.16) | copy-start | bytes 786436
  98.9 33.2 %collective-permute-start.6 = (bf16[144,1024]{1,0:T(8,128)(2,1)S(1)}, bf16[144,1024]{1,0:T(8,128)(2,1)S(1)}, u32[]{:S(2)}, u32[]{:S(2)}) collective-permute-start(bf16[144,1024]{1,0:T(8,128)(2,1)S(1)} %get-tuple-element.33), channel_id=1, source_target_pairs={{0,1},{1,2},{2,3},{3,4},{4,5},{5,6},{6,7},{7,0},{8,9},{9,10},{10,1... | collective-permute-start | bytes 884744 | tf_op jit(solution)/shard_map/ppermute | solution.py:358
  100.6 31.4 %collective-permute-start.7 = (bf16[144,1024]{1,0:T(8,128)(2,1)S(1)}, bf16[144,1024]{1,0:T(8,128)(2,1)S(1)}, u32[]{:S(2)}, u32[]{:S(2)}) collective-permute-start(bf16[144,1024]{1,0:T(8,128)(2,1)S(1)} %get-tuple-element.34), channel_id=1, source_target_pairs={{0,7},{1,0},{2,1},{3,2},{4,3},{5,4},{6,5},{7,6},{8,15},{9,8},{10,9... | collective-permute-start | bytes 884744 | tf_op jit(solution)/shard_map/ppermute | solution.py:358
  104.6 12.2 %collective-permute-start.9 = (f32[72,128]{1,0:T(8,128)S(1)}, f32[72,128]{1,0:T(8,128)S(1)}, u32[]{:S(2)}, u32[]{:S(2)}) collective-permute-start(f32[72,128]{1,0:T(8,128)S(1)} %fusion.5), channel_id=1, source_target_pairs={{0,16},{8,24},{16,0},{24,8},{32,48},{40,56},{48,32},{56,40},{64,80... | collective-permute-start | bytes 110600 | tf_op jit(solution)/shard_map/ppermute | solution.py:507
  116.9 4.0 %collective-permute-start.10 = (f32[72,128]{1,0:T(8,128)S(1)}, f32[72,128]{1,0:T(8,128)S(1)}, u32[]{:S(2)}, u32[]{:S(2)}) collective-permute-start(f32[72,128]{1,0:T(8,128)S(1)} %add.45), channel_id=1, source_target_pairs={{0,32},{8,40},{16,48},{24,56},{32,0},{40,8},{48,16},{56,24},{64,96... | collective-permute-start | bytes 110600 | tf_op jit(solution)/shard_map/ppermute | solution.py:507
  120.8 6.1 %collective-permute-start.11 = (f32[72,128]{1,0:T(8,128)S(1)}, f32[72,128]{1,0:T(8,128)S(1)}, u32[]{:S(2)}, u32[]{:S(2)}) collective-permute-start(f32[72,128]{1,0:T(8,128)S(1)} %add.46), channel_id=1, source_target_pairs={{0,64},{8,72},{16,80},{24,88},{32,96},{40,104},{48,112},{56,120},{... | collective-permute-start | bytes 110600 | tf_op jit(solution)/shard_map/ppermute | solution.py:507
  126.9 10.7 %collective-permute-start.12 = (f32[72,128]{1,0:T(8,128)S(1)}, f32[72,128]{1,0:T(8,128)S(1)}, u32[]{:S(2)}, u32[]{:S(2)}) collective-permute-start(f32[72,128]{1,0:T(8,128)S(1)} %add.47), channel_id=1, source_target_pairs={{0,128},{8,136},{16,144},{24,152},{32,160},{40,168},{48,176},{56,1... | collective-permute-start | bytes 110600 | tf_op jit(solution)/shard_map/ppermute | solution.py:507
  (19 other events, 86.2 us)

commit v2 on v1

v2 whole, which is shorter than its diff:
```python
import functools

import jax
import jax.numpy as jnp
from jax import lax
from jax.experimental import pallas as pl
from jax.experimental.pallas import tpu as pltpu
from jax.sharding import PartitionSpec as P

HEADS = 16
HEAD = 64
BLK = 8
REACH = 2
NLAT = 128
NLON = 256
ROWS = 4
COLS = 32
SIDE = REACH * BLK
LANES = 128
PAIRS = 8
NEG = -1e30
SCALE = HEAD ** (-0.5)
F32 = jnp.float32
BF16 = jnp.bfloat16
GRANT = 64

LON_TOK = 144
LAT_TOK = 304
BACK_LAT = 288
BACK_LON = 144
POLE_IN = 320
KG_ROWS = 80
POLE_OUT = 272


def params(mib, steps=1):
    return pltpu.CompilerParams(
        vmem_limit_bytes=mib * 2**20, dimension_semantics=("arbitrary",) * steps
    )


def lane_spec(*lead, wide=LANES):
    zeros = (0,) * len(lead)
    return pl.BlockSpec(lead + (wide,), lambda j: zeros + (j,))


SMEM = pl.BlockSpec(memory_space=pltpu.SMEM)


def nt(lhs, rhs):
    return lax.dot_general(lhs, rhs, (((1,), (1,)), ((), ())), preferred_element_type=F32)


def tn(lhs, rhs):
    return lax.dot_general(lhs, rhs, (((0,), (0,)), ((), ())), preferred_element_type=F32)


def nn(lhs, rhs):
    return lax.dot_general(lhs, rhs, (((1,), (0,)), ((), ())), preferred_element_type=F32)


def two_heads(array):
    first = lax.broadcasted_iota(jnp.int32, array.shape, 1) < HEAD
    return jnp.concatenate(
        [jnp.where(first, array, 0.0), jnp.where(first, 0.0, array)], axis=0
    ).astype(BF16)


def own_features(array):
    half = array.shape[1] // 2
    first = lax.broadcasted_iota(jnp.int32, (LANES, half), 0) < HEAD
    return jnp.where(first, array[:, :half], array[:, half:])


def attention(query, key, value, d_att, bias, valid):
    query2 = two_heads(query * SCALE)
    grad2 = two_heads(d_att)
    scores = nt(key, query2)
    if bias is not None:
        scores = scores + jnp.concatenate([bias, bias], axis=1)
    top = jnp.max(scores, axis=0, keepdims=True)
    weights = jnp.exp(scores - top)
    inverse = 1.0 / jnp.sum(weights, axis=0, keepdims=True)
    if valid is not None:
        inverse = inverse * jnp.concatenate([valid, valid], axis=1)
    att_t = own_features(tn(value, weights.astype(BF16)) * inverse).astype(BF16).astype(F32)
    product = d_att.T * att_t
    delta = jnp.concatenate(
        [
            jnp.sum(product[:HEAD], axis=0, keepdims=True),
            jnp.sum(product[HEAD:], axis=0, keepdims=True),
        ],
        axis=1,
    )
    probs = weights * inverse
    dscore = (probs * (nt(value, grad2) - delta)).astype(BF16)
    d_query = own_features(tn(key, dscore)).T * SCALE
    d_key = nn(dscore, query2)
    d_value = nn(probs.astype(BF16), grad2)
    return att_t.T, d_query, d_key, d_value


def place():
    lat = lax.axis_index("lat")
    return lat, lax.axis_index("lon"), jnp.where(lat == 0, 0, ROWS - REACH)


def at_pole(lat):
    return (lat == 0) | (lat == NLAT // ROWS - 1)


def run_copies(pairs, sems):
    copies = [
        pltpu.make_async_copy(source, target, sems.at[index])
        for index, (source, target) in enumerate(pairs)
    ]
    for copy in copies:
        copy.start()
    for copy in copies:
        copy.wait()


def pack_lon_kernel(q_ref, k_ref, v_ref, c_ref, east_ref, west_ref, pole_out, edge):
    half = ROWS * SIDE
    wide = edge.shape[1]
    for out, start, col in ((east_ref, COLS - SIDE, COLS - 1), (west_ref, 0, 0)):
        out[0:half] = k_ref[:, start : start + SIDE].reshape(half, wide)
        out[half : 2 * half] = v_ref[:, start : start + SIDE].reshape(half, wide)
        edge[...] = jnp.zeros_like(edge)
        for row in range(ROWS):
            cells = c_ref[row].astype(F32)
            edge[row : row + 1] = cells[col : col + 1]
        out[2 * half :] = edge[...].astype(BF16)
    lat, lon, start = place()
    both = REACH * COLS

    @pl.when(at_pole(lat))
    def _():
        for part in range(wide // LANES):
            lanes = slice(part * LANES, (part + 1) * LANES)
            for index, ref in enumerate((q_ref, k_ref, v_ref)):
                pole_out[part, index * both : (index + 1) * both] = ref[
                    pl.ds(start, REACH), :, lanes
                ].reshape(both, LANES)
            pole_out[part, 3 * both :] = c_ref[:, :, lanes].reshape(ROWS * COLS, LANES)


def pack_lat_kernel(k_ref, v_ref, c_ref, w_ref, e_ref, south_ref, north_ref, edge):
    own = REACH * COLS
    side = REACH * SIDE
    half = ROWS * SIDE
    wide = edge.shape[1]
    west_cot = w_ref[2 * half :].astype(F32)
    east_cot = e_ref[2 * half :].astype(F32)
    for out, start, row in ((south_ref, ROWS - REACH, ROWS - 1), (north_ref, 0, 0)):
        for index, ref in enumerate((k_ref, v_ref)):
            base = index * (own + 2 * side)
            near = index * half + start * SIDE
            out[base : base + own] = ref[start : start + REACH].reshape(own, wide)
            out[base + own : base + own + side] = w_ref[near : near + side]
            out[base + own + side : base + own + 2 * side] = e_ref[near : near + side]
        base = 2 * (own + 2 * side)
        out[base : base + COLS] = c_ref[row]
        edge[...] = jnp.zeros_like(edge)
        edge[0:1] = west_cot[row : row + 1]
        edge[1:2] = east_cot[row : row + 1]
        out[base + COLS :] = edge[...].astype(BF16)


def fill_rim(pad, row, middle, west, east):
    pad[row, 8 : 8 + COLS] = middle
    pad[row, 7:8] = west
    pad[row, 8 + COLS : 9 + COLS] = east


def key_groups():
    groups, start = [], 0
    for row_range in ((0, ROWS), (-REACH, REACH), (ROWS, REACH)):
        for first_col, width in ((0, COLS), (-SIDE, SIDE), (COLS, SIDE)):
            size = row_range[1] * width
            groups.append((start, size, row_range[0], width, first_col))
            start += size
    return groups


def window_kernel(
    pattern_ref, polar_ref, q_ref, k_ref, v_ref, c_ref, w_ref, e_ref, n_ref, s_ref, conv_ref,
    att_ref, dq_ref, south_ref, north_ref, mid_ref, kg_ref, pad, bias_ref,
):
    tokens = ROWS * COLS
    base = lax.axis_index("lat") * ROWS
    query_at = lax.broadcasted_iota(jnp.int32, (1, tokens), 1)
    query_row = query_at >> COLS.bit_length() - 1

    def by_row(values):
        out = jnp.full((1, tokens), values[0], values[0].dtype)
        for row in range(1, ROWS):
            out = jnp.where(query_row == row, values[row], out)
        return out

    valid = by_row([jnp.where(polar_ref[base + row] > 0, 0.0, 1.0) for row in range(ROWS)])

    @pl.when(pl.program_id(0) == 0)
    def _():
        offset = by_row([pattern_ref[0, base + row] for row in range(ROWS)])
        count = by_row([pattern_ref[1, base + row] for row in range(ROWS)])
        bits = BLK.bit_length() - 1
        block = ((query_at & COLS - 1) >> bits) + offset
        for start, size, first_row, width, first_col in key_groups():
            index = lax.broadcasted_iota(jnp.int32, (size, tokens), 0)
            row = (index >> width.bit_length() - 1) + first_row
            distance = ((index & width - 1) >> bits) + first_col // BLK - block
            inside = (jnp.abs(row - query_row) <= REACH) & (distance >= 0) & (distance < count)
            inside = inside & (base + row >= 0) & (base + row < NLAT)
            bias_ref[start : start + size] = jnp.where(inside, 0.0, NEG)

    half = ROWS * SIDE
    rim = 2 * REACH * SIDE + REACH * COLS
    wide = pad.shape[2]
    west_cot = w_ref[2 * half :].astype(F32)
    east_cot = e_ref[2 * half :].astype(F32)
    for row in range(ROWS):
        fill_rim(
            pad, row + 1, c_ref[row].astype(F32), west_cot[row : row + 1], east_cot[row : row + 1]
        )
    for row, ref in ((0, n_ref), (ROWS + 1, s_ref)):
        cells = ref[2 * rim :].astype(F32)
        fill_rim(pad, row, cells[:COLS], cells[COLS : COLS + 1], cells[COLS + 1 : COLS + 2])
    for part in range(wide // LANES):
        lanes = slice(part * LANES, (part + 1) * LANES)
        taps = [
            pad[2 - a : 2 - a + ROWS, 9 - b : 9 - b + COLS, lanes].reshape(tokens, LANES)
            for a in range(3)
            for b in range(3)
        ]
        back = taps[4]
        for tap in range(9):
            back = back + conv_ref[tap : tap + 1, lanes] * taps[tap]
        d_att = back.astype(BF16).astype(F32)
        key, value = (
            jnp.concatenate(
                [
                    ref[:, :, lanes].reshape(tokens, LANES),
                    w_ref[index * half : (index + 1) * half, lanes],
                    e_ref[index * half : (index + 1) * half, lanes],
                    n_ref[index * rim : (index + 1) * rim, lanes],
                    s_ref[index * rim : (index + 1) * rim, lanes],
                ],
                axis=0,
            )
            for index, ref in enumerate((k_ref, v_ref))
        )
        query = q_ref[:, :, lanes].reshape(tokens, LANES).astype(F32)
        att, d_query, d_key, d_value = attention(
            query, key, value, d_att, bias_ref[...], valid
        )
        att_b = att.astype(BF16)
        att_ref[:, lanes] = att_b
        dq_ref[:, lanes] = d_query.astype(BF16)
        near = tokens + 2 * half
        mid_ref[0, :, lanes] = d_key[:near]
        mid_ref[1, :, lanes] = d_value[:near]
        for ref, start, row in ((north_ref, near, 0), (south_ref, near + rim, ROWS - 1)):
            ref[:rim, lanes] = d_key[start : start + rim].astype(BF16)
            ref[rim : 2 * rim, lanes] = d_value[start : start + rim].astype(BF16)
            ref[2 * rim :, lanes] = att_b[row * COLS : (row + 1) * COLS]
        for tap in range(9):
            kg_ref[tap : tap + 1, lanes] = jnp.sum(att * taps[tap], axis=0, keepdims=True)


def pole_kernel(
    polar_ref, pole_in_ref, conv_ref, kgin_ref,
    out_ref, x_ref, y_ref, edge, weights_ref, kg_ref, kg_rows, kg_pair, sems,
):
    both = REACH * COLS
    lat, lon, start = place()
    base = lat * ROWS + start
    mine = pl.ds(pl.multiple_of(lon * LANES, LANES), LANES)
    run_copies([(kgin_ref, kg_ref)], sems)

    @pl.when(at_pole(lat))
    def _():
        run_copies([(conv_ref.at[:, mine], weights_ref), (pole_in_ref, x_ref)], sems)
        edge[...] = jnp.zeros_like(edge)
        weights = weights_ref[...]
        rows = []
        for step in range(REACH + 2):
            row = start + step - 1
            inside = jnp.where((row >= 0) & (row < ROWS), 1.0, 0.0)
            at = pl.multiple_of(3 * both + jnp.clip(row, 0, ROWS - 1) * COLS, COLS)
            rows.append(x_ref[:, pl.ds(at, COLS)].reshape(NLON, LANES).astype(F32) * inside)
        for r in range(REACH):
            taps = []
            back = rows[r + 1]
            for a in range(3):
                cells = rows[r + 2 - a]
                for b, shifted in enumerate(
                    (pltpu.roll(cells, NLON - 1, 0), cells, pltpu.roll(cells, 1, 0))
                ):
                    taps.append(shifted)
                    back = back + weights[3 * a + b : 3 * a + b + 1] * shifted
            query, key, value = (
                x_ref[:, part * both + r * COLS : part * both + (r + 1) * COLS].reshape(NLON, LANES)
                for part in range(3)
            )
            d_att = back.astype(BF16).astype(F32)
            att, d_query, d_key, d_value = attention(
                query.astype(F32), key, value, d_att, None, None
            )
            for part, array in enumerate((att, d_query, d_key, d_value)):
                y_ref[:, part * both + r * COLS : part * both + (r + 1) * COLS] = array.astype(
                    BF16
                ).reshape(PAIRS, COLS, LANES)
            for dest in range(PAIRS):
                west = (dest * COLS - 1) % NLON
                east = (dest * COLS + COLS) % NLON
                edge[dest, 2 * r : 2 * r + 1] = att[west : west + 1]
                edge[dest, 2 * r + 1 : 2 * r + 2] = att[east : east + 1]
            counted = jnp.where(polar_ref[base + r] > 0, 1.0, 0.0)
            for tap in range(9):
                kg_ref[tap : tap + 1, mine] += counted * jnp.sum(
                    att * taps[tap], axis=0, keepdims=True
                )
        y_ref[:, 4 * both :] = edge[...].astype(BF16)
        run_copies([(y_ref, out_ref.at[:, pl.ds(0, POLE_OUT)])], sems)

    kg_rows[...] = jnp.zeros_like(kg_rows)
    for block in range(PAIRS):
        kg_rows[9 * block : 9 * (block + 1)] = kg_ref[:, block * LANES : (block + 1) * LANES]
    high = kg_rows[...].astype(BF16)
    kg_pair[:KG_ROWS] = high
    kg_pair[KG_ROWS:] = (kg_rows[...] - high.astype(F32)).astype(BF16)
    tail = pl.ds(POLE_OUT, 2 * KG_ROWS)
    run_copies([(kg_pair, out_ref.at[dest, tail]) for dest in range(PAIRS)], sems)


def pack_back_kernel(mid_ref, att_ref, n_ref, s_ref, west_ref, east_ref, edge):
    half = ROWS * SIDE
    side = REACH * SIDE
    own = REACH * COLS
    rim = own + 2 * side
    for out, first, col in ((west_ref, 0, 0), (east_ref, 1, COLS - 1)):
        for index in range(2):
            source = index * rim + own + first * side
            cells = mid_ref[index, first * half : (first + 1) * half]
            out[index * half : index * half + side] = (
                cells[:side] + n_ref[source : source + side].astype(F32)
            ).astype(BF16)
            out[index * half + side : (index + 1) * half] = (
                cells[side:] + s_ref[source : source + side].astype(F32)
            ).astype(BF16)
        edge[...] = jnp.zeros_like(edge)
        edge[0:1] = n_ref[2 * rim :].astype(F32)[col : col + 1]
        edge[ROWS + 1 : ROWS + 2] = s_ref[2 * rim :].astype(F32)[col : col + 1]
        for row in range(ROWS):
            cells = att_ref[row * COLS : (row + 1) * COLS].astype(F32)
            edge[row + 1 : row + 2] = cells[col : col + 1]
        out[2 * half :] = edge[...].astype(BF16)


def final_kernel(
    polar_ref, att_ref, dq_ref, mid_ref, n_ref, s_ref, w_ref, e_ref,
    back_ref, conv_ref,
    mixed_out, dq_out, dk_out, dv_out, pad, dk_sum, dv_sum, y_ref, sems,
):
    half = ROWS * SIDE
    own = REACH * COLS
    both = own
    rim = own + 2 * REACH * SIDE
    west_att = w_ref[2 * half :].astype(F32)
    east_att = e_ref[2 * half :].astype(F32)
    middles = [n_ref[2 * rim :].astype(F32)]
    middles += [att_ref[row * COLS : (row + 1) * COLS].astype(F32) for row in range(ROWS)]
    middles += [s_ref[2 * rim :].astype(F32)]
    for row in range(ROWS + 2):
        fill_rim(pad, row, middles[row], west_att[row : row + 1], east_att[row : row + 1])
    dq_out[...] = dq_ref[...].reshape(ROWS, COLS, -1)
    wide = pad.shape[2]
    for index, total in ((0, dk_sum), (1, dv_sum)):
        north = n_ref[index * rim : index * rim + own].astype(F32)
        south = s_ref[index * rim : index * rim + own].astype(F32)
        cells = mid_ref[index] + jnp.concatenate([north, south], axis=0)
        sides = jnp.concatenate(
            [
                w_ref[index * half : (index + 1) * half].astype(F32).reshape(ROWS, SIDE, wide),
                e_ref[index * half : (index + 1) * half].astype(F32).reshape(ROWS, SIDE, wide),
            ],
            axis=1,
        )
        total[...] = cells.reshape(ROWS, COLS, wide) + sides
    lat, lon, start = place()

    @pl.when(at_pole(lat) & (pl.program_id(0) == 0))
    def _():
        run_copies([(back_ref.at[:, pl.ds(0, POLE_OUT)], y_ref)], sems)

    for r in range(REACH):

        @pl.when(at_pole(lat) & (polar_ref[lat * ROWS + start + r] > 0))
        def _():
            row = start + r
            for part_index in range(wide // LANES):
                block = pl.program_id(0) * (wide // LANES) + part_index
                lanes = slice(part_index * LANES, (part_index + 1) * LANES)
                ends = y_ref[block, 4 * both : POLE_OUT].astype(F32)
                part = [
                    y_ref[block, p * both + r * COLS : p * both + (r + 1) * COLS]
                    for p in range(4)
                ]
                pad[row + 1, 8 : 8 + COLS, lanes] = part[0].astype(F32)
                pad[row + 1, 7:8, lanes] = ends[2 * r : 2 * r + 1]
                pad[row + 1, 8 + COLS : 9 + COLS, lanes] = ends[2 * r + 1 : 2 * r + 2]
                dq_out[row, :, lanes] = part[1]
                dk_sum[row, :, lanes] += part[2].astype(F32)
                dv_sum[row, :, lanes] += part[3].astype(F32)

    dk_out[...] = dk_sum[...].astype(BF16)
    dv_out[...] = dv_sum[...].astype(BF16)
    mixed = pad[1 : 1 + ROWS, 8 : 8 + COLS]
    for a in range(3):
        for b in range(3):
            weight = conv_ref[3 * a + b : 3 * a + b + 1][None]
            mixed = mixed + weight * pad[a : a + ROWS, 7 + b : 7 + b + COLS]
    mixed_out[...] = mixed.astype(BF16)


def shift(array, axis, step, wrap):
    count = lax.axis_size(axis)
    route = [(i, (i + step) % count) for i in range(count) if wrap or 0 <= i + step < count]
    return lax.ppermute(array, axis, route)


def sds(shape, dtype=BF16):
    return jax.ShapeDtypeStruct(shape, dtype)


def cost(flops, moved):
    return pl.CostEstimate(flops=flops, bytes_accessed=moved, transcendentals=0)


def halo(*shape, wide):
    return pltpu.VMEM(shape + (wide,), F32)


def body(queries, keys, values, conv_kernel, cotangent, pattern, polar):
    width = queries.shape[2]
    lat_count = lax.axis_size("lat")
    tokens = ROWS * COLS
    pack = 512
    span = 256
    packed = functools.partial(lane_spec, wide=pack)
    spanned = functools.partial(lane_spec, wide=span)

    anywhere = pl.BlockSpec(memory_space=pl.ANY)

    east_pay, west_pay, pole_pay = pl.pallas_call(
        pack_lon_kernel,
        grid=(width // pack,),
        in_specs=[packed(ROWS, COLS)] * 4,
        out_specs=[packed(LON_TOK)] * 2
        + [pl.BlockSpec((pack // LANES, POLE_IN, LANES), lambda j: (j, 0, 0))],
        out_shape=[sds((LON_TOK, width))] * 2 + [sds((PAIRS, POLE_IN, LANES))],
        scratch_shapes=[halo(16, wide=pack)],
        compiler_params=params(GRANT),
        cost_estimate=cost(0, 3 * 2**20),
        name="pack_lon",
    )(queries, keys, values, cotangent)
    from_west = shift(east_pay, "lon", 1, True)
    from_east = shift(west_pay, "lon", -1, True)

    south_pay, north_pay = pl.pallas_call(
        pack_lat_kernel,
        grid=(width // pack,),
        in_specs=[packed(ROWS, COLS)] * 3 + [packed(LON_TOK)] * 2,
        out_specs=[packed(LAT_TOK)] * 2,
        out_shape=[sds((LAT_TOK, width))] * 2,
        scratch_shapes=[halo(16, wide=pack)],
        compiler_params=params(GRANT),
        cost_estimate=cost(0, 3 * 2**20),
        name="pack_lat",
    )(keys, values, cotangent, from_west, from_east)
    from_north = shift(south_pay, "lat", 1, False)
    from_south = shift(north_pay, "lat", -1, False)
    pole_pay, _ = lax.optimization_barrier((pole_pay, south_pay))
    pole_in = lax.all_to_all(pole_pay, "lon", 0, 0)

    att, dq_near, south_back, north_back, mid, kg = pl.pallas_call(
        window_kernel,
        grid=(width // span,),
        in_specs=[SMEM, SMEM]
        + [spanned(ROWS, COLS)] * 4
        + [spanned(LON_TOK)] * 2
        + [spanned(LAT_TOK)] * 2
        + [spanned(9)],
        out_specs=[
            spanned(tokens),
            spanned(tokens),
            spanned(BACK_LAT),
            spanned(BACK_LAT),
            spanned(2, 2 * tokens),
            spanned(9),
        ],
        out_shape=[
            sds((tokens, width)),
            sds((tokens, width)),
            sds((BACK_LAT, width)),
            sds((BACK_LAT, width)),
            sds((2, 2 * tokens, width), F32),
            sds((9, width), F32),
        ],
        scratch_shapes=[halo(ROWS + 2, 48, wide=span), pltpu.VMEM((4 * tokens, tokens), F32)],
        compiler_params=params(GRANT),
        cost_estimate=cost(4 * 10**9, 8 * 2**20),
        name="window",
    )(
        pattern.T, polar, queries, keys, values, cotangent, from_west, from_east,
        from_north, from_south, conv_kernel,
    )
    back_north = shift(south_back, "lat", 1, False)
    back_south = shift(north_back, "lat", -1, False)

    pole_out = pl.pallas_call(
        pole_kernel,
        in_specs=[SMEM] + [anywhere] * 3,
        out_specs=anywhere,
        out_shape=sds((PAIRS, POLE_OUT + 2 * KG_ROWS, LANES)),
        scratch_shapes=[
            pltpu.VMEM((PAIRS, POLE_IN, LANES), BF16),
            pltpu.VMEM((PAIRS, POLE_OUT, LANES), BF16),
            pltpu.VMEM((PAIRS, 16, LANES), F32),
            pltpu.VMEM((9, LANES), F32),
            pltpu.VMEM((9, width), F32),
            pltpu.VMEM((KG_ROWS, LANES), F32),
            pltpu.VMEM((2 * KG_ROWS, LANES), BF16),
            pltpu.SemaphoreType.DMA((PAIRS,)),
        ],
        compiler_params=params(GRANT, 0),
        cost_estimate=cost(10**9, 4 * 2**20),
        name="pole",
    )(polar, pole_in, conv_kernel, kg)
    pole_back = lax.all_to_all(pole_out, "lon", 0, 0)

    def summed(array, step):
        route = [(i, i ^ step) for i in range(lat_count)]
        return array + lax.ppermute(array, "lat", route)

    def after(array, *others):
        return lax.optimization_barrier((array,) + others)[0]

    west_back, east_back = pl.pallas_call(
        pack_back_kernel,
        grid=(width // pack,),
        in_specs=[
            pl.BlockSpec((2, tokens, pack), lambda j: (0, 1, j)),
            packed(tokens),
            packed(BACK_LAT),
            packed(BACK_LAT),
        ],
        out_specs=[packed(BACK_LON)] * 2,
        out_shape=[sds((BACK_LON, width))] * 2,
        scratch_shapes=[halo(16, wide=pack)],
        compiler_params=params(GRANT),
        cost_estimate=cost(0, 3 * 2**20),
        name="pack_back",
    )(mid, att, back_north, back_south)
    back_east = shift(west_back, "lon", -1, True)
    back_west = shift(east_back, "lon", 1, True)

    kg = jnp.sum(after(pole_back, west_back)[:, POLE_OUT:].astype(F32), axis=0)
    kg = kg[:KG_ROWS] + kg[KG_ROWS:]
    for step in (1, 2, 4):
        kg = summed(kg, step)
    kg, back_east, back_west = lax.optimization_barrier((kg, back_east, back_west))
    kg = summed(kg, 8)

    mixed, query_grad, key_grad, value_grad = pl.pallas_call(
        final_kernel,
        grid=(width // span,),
        in_specs=[
            SMEM,
            spanned(tokens),
            spanned(tokens),
            spanned(2, tokens),
            spanned(BACK_LAT),
            spanned(BACK_LAT),
            spanned(BACK_LON),
            spanned(BACK_LON),
        ]
        + [anywhere, spanned(9)],
        out_specs=[spanned(ROWS, COLS)] * 4,
        out_shape=[sds((ROWS, COLS, width))] * 4,
        scratch_shapes=[
            halo(ROWS + 2, 48, wide=span),
            halo(ROWS, COLS, wide=span),
            halo(ROWS, COLS, wide=span),
            pltpu.VMEM((PAIRS, POLE_OUT, LANES), BF16),
            pltpu.SemaphoreType.DMA((1,)),
        ],
        compiler_params=params(GRANT),
        cost_estimate=cost(0, 6 * 2**20),
        name="final",
    )(
        polar, att, dq_near, mid, back_north, back_south, back_west, back_east,
        pole_back, conv_kernel,
    )
    kg, mixed, query_grad, key_grad, value_grad = lax.optimization_barrier(
        (kg, mixed, query_grad, key_grad, value_grad)
    )
    kg = summed(kg, 16)[: 9 * PAIRS].reshape(PAIRS, 9, LANES) * (NLAT * NLON) ** (-0.5)
    kernel_grad = jnp.transpose(kg, (1, 0, 2)).reshape(9, width)
    return mixed, query_grad, key_grad, value_grad, kernel_grad


def solution(mesh):
    return jax.shard_map(
        body,
        mesh=mesh,
        in_specs=(
            P("lat", "lon", None),
            P("lat", "lon", None),
            P("lat", "lon", None),
            P(),
            P("lat", "lon", None),
            P(),
            P(),
        ),
        out_specs=(
            P("lat", "lon", None),
            P("lat", "lon", None),
            P("lat", "lon", None),
            P("lat", "lon", None),
            P(),
        ),
        check_vma=False,
    )
```

time: 141 us -> 123 us (0.87)
  local copies, waits for them, and re-layouts: 13.8 us -> 0.67 us
  Pallas kernels: 27.5 us -> 23.7 us
  starting transfers between devices: 56.6 us -> 58.7 us
  waiting for transfers between devices: 36.5 us -> 34.6 us
    unnamed x60 -> x2, local copies, waits for them, and re-layouts: 12.4 us -> 0.65 us
    all_to_all x1, waiting for transfers between devices: 6.51 us -> 0.01 us  [body(): pole_back = lax.all_to_all(pole_out, 'lon', 0, 0)]
    all_to_all x1, starting transfers between devices: 3.55 us -> 8.8 us  [body(): pole_back = lax.all_to_all(pole_out, 'lon', 0, 0)]
    ppermute x5, waiting for transfers between devices: 10.3 us -> 15 us  [summed(): return array + lax.ppermute(array, 'lat', route)]
    pallas_call x6, Pallas kernels: 27.5 us -> 23.7 us  [the longest x1 10.1 us: body(): pl.pallas_call(window_kernel, grid=(width // span,), in_specs=[SMEM, SMEM...]
    ppermute x5, starting transfers between devices: 19.6 us -> 17.7 us  [summed(): return array + lax.ppermute(array, 'lat', route)]
    select_n x2 -> x0, other arithmetic: 1.88 us -> none  [the longest x1 1.8 us: body(): bias = jnp.where(allowed, 0.0, NEG).astype(F32)]
  transfers between devices with their start and end apart: 15 -> 15, of which waited for: 8 -> 8; matrix products, arithmetic and copies ran while one was open for 2% -> 1% of each run, Pallas kernels for 10% -> 14%
where the time goes in v2:
time: 123 us; the launch traced here: 121 us
  starting transfers between devices  58.7 us (48%)
  waiting for transfers between devices  34.6 us (28%)
  Pallas kernels  23.7 us (19%)
  other arithmetic  2.49 us (2%)
    ppermute x8, starting transfers between devices, shift(): return lax.ppermute(array, axis, route)  25.4 us
    ppermute x8, waiting for transfers between devices, shift(): return lax.ppermute(array, axis, route)  19.1 us
    ppermute x5, starting transfers between devices, summed(): return array + lax.ppermute(array, 'lat', route)  17.7 us
    ppermute x5, waiting for transfers between devices, summed(): return array + lax.ppermute(array, 'lat', route)  15 us
    pallas_call x1, Pallas kernels, body(): pl.pallas_call(window_kernel, grid=(width // span,), in_specs=[SMEM, SMEM...  10.1 us
    all_to_all x1, starting transfers between devices, body(): pole_back = lax.all_to_all(pole_out, 'lon', 0, 0)  8.8 us
    all_to_all x1, starting transfers between devices, body(): pole_in = lax.all_to_all(pole_pay, 'lon', 0, 0)  6.83 us
    pallas_call x1, Pallas kernels, body(): pl.pallas_call(final_kernel, grid=(width // span,), in_specs=[SMEM, spann...  4.19 us
  transfers between devices with their start and end apart: 15, of which 8 were waited for; matrix products, arithmetic and copies ran while one was open for 1% of the time, Pallas kernels for 14%

profile of v2, /device:TPU:32, one launch (start us, length us, event | category | flops | bytes accessed | tf_op | source)
XLA Modules:
  0.0 121.0 jit_solution(17550693547634143813)
XLA Ops:
  0.6 2.2 %pack_lon.1 = (bf16[144,1024]{1,0:T(8,128)(2,1)}, bf16[144,1024]{1,0:T(8,128)(2,1)}, bf16[8,320,128]{2,1,0:T(8,128)(2,1)}) custom-call(bf16[4,32,1024]{2,1,0:T(8,128)(2,1)} %q_ref.3, bf16[4,32,1024]{2,1,0:T(8,128)(2,1)} %k_ref.5, bf16[4,32,1024]{2,1,0:T(8,128)(2,1)} %v_ref.5, bf16[4,32,1024]{2,1,0:T(8,128)(2,1)} %c_ref.5), custom_call_target="tpu_custom_call" | custom-call | bytes 3145728 | tf_op jit(solution)/shard_map/pack_lon/pallas_call | solution.py:456
  4.3 4.1 %collective-permute-start.1 = (bf16[144,1024]{1,0:T(8,128)(2,1)}, bf16[144,1024]{1,0:T(8,128)(2,1)}, u32[]{:S(2)}, u32[]{:S(2)}) collective-permute-start(bf16[144,1024]{1,0:T(8,128)(2,1)} %get-tuple-element.34), channel_id=1, source_target_pairs={{0,7},{1,0},{2,1},{3,2},{4,3},{5,4},{6,5},{7,6},{8,15},{9,8},{10,9... | collective-permute-start | bytes 884744 | tf_op jit(solution)/shard_map/ppermute | solution.py:430
  8.5 7.1 %collective-permute-done.w_ref = bf16[144,1024]{1,0:T(8,128)(2,1)} collective-permute-done((bf16[144,1024]{1,0:T(8,128)(2,1)}, bf16[144,1024]{1,0:T(8,128)(2,1)}, u32[]{:S(2)}, u32[]{:S(2)}) %collective-permute-start) | collective-permute-done | bytes 294944 | tf_op jit(solution)/shard_map/ppermute | solution.py:430
  15.6 2.4 %pack_lat.1 = (bf16[304,1024]{1,0:T(8,128)(2,1)}, bf16[304,1024]{1,0:T(8,128)(2,1)}) custom-call(bf16[4,32,1024]{2,1,0:T(8,128)(2,1)} %k_ref.5, bf16[4,32,1024]{2,1,0:T(8,128)(2,1)} %v_ref.5, bf16[4,32,1024]{2,1,0:T(8,128)(2,1)} %c_ref.5, bf16[144,1024]{1,0:T(8,128)(2,1)} %collective-permute-done.w_ref, bf16[144,1024]{1,0:T(8,128)(2,1)} %collective-permute-done.1.e_ref), custom_call_target="tpu_custom_call" | custom-call | bytes 3145728 | tf_op jit(solution)/shard_map/pack_lat/pallas_call | solution.py:471
  19.8 2.4 %collective-permute-start.2 = (bf16[304,1024]{1,0:T(8,128)(2,1)}, bf16[304,1024]{1,0:T(8,128)(2,1)}, u32[]{:S(2)}, u32[]{:S(2)}) collective-permute-start(bf16[304,1024]{1,0:T(8,128)(2,1)} %get-tuple-element.35), channel_id=1, source_target_pairs={{0,8},{8,16},{16,24},{24,32},{32,40},{40,48},{48,56},{56,64},{64,7... | collective-permute-start | bytes 1867784 | tf_op jit(solution)/shard_map/ppermute | solution.py:430
  22.3 6.8 %all-to-all-start = ((bf16[8,320,128]{2,1,0:T(8,128)(2,1)}), bf16[8,320,128]{2,1,0:T(8,128)(2,1)}, u32[]{:S(2)}, u32[]{:S(2)}) async-start(bf16[8,320,128]{2,1,0:T(8,128)(2,1)} %get-tuple-element.36), calls=%async_computation | async-start | bytes 1310720 | tf_op jit(solution)/shard_map/all_to_all | solution.py:485
  29.1 3.6 %collective-permute-done.2.n_ref = bf16[304,1024]{1,0:T(8,128)(2,1)} collective-permute-done((bf16[304,1024]{1,0:T(8,128)(2,1)}, bf16[304,1024]{1,0:T(8,128)(2,1)}, u32[]{:S(2)}, u32[]{:S(2)}) %collective-permute-start.2) | collective-permute-done | bytes 622624 | tf_op jit(solution)/shard_map/ppermute | solution.py:430
  32.7 10.1 %window.1 = (bf16[128,1024]{1,0:T(8,128)(2,1)}, bf16[128,1024]{1,0:T(8,128)(2,1)}, bf16[288,1024]{1,0:T(8,128)(2,1)}, bf16[288,1024]{1,0:T(8,128)(2,1)}, f32[2,256,1024]{2,1,0:T(8,128)}, /*index=5*/f32[9,1024]{1,0:T(8,128)}) custom-call(s32[2,128]{1,0:T(2,128)} %bitcast.8, s32[128]{0:T(128)} %polar_ref.5, bf16[4,32,1024]{2,1,0:T(8,128)(2,1)} %q_ref.3, ...), custom_call_target="tpu_custom_call" | custom-call | flops 4000000000 | bytes 8388608 | tf_op jit(solution)/shard_map/window/pallas_call | solution.py:487
  43.4 2.4 %pole.1 = bf16[8,432,128]{2,1,0:T(8,128)(2,1)} custom-call(s32[128]{0:T(128)} %polar_ref.5, bf16[8,320,128]{2,1,0:T(8,128)(2,1)} %all-to-all-done.pole_in_ref, f32[9,1024]{1,0:T(8,128)} %conv_ref.5, f32[9,1024]{1,0:T(8,128)} %get-tuple-element.38.kgin_ref), custom_call_target="tpu_custom_call" | custom-call | flops 1000000000 | bytes 4194304 | tf_op jit(solution)/shard_map/pole/pallas_call | solution.py:522
  45.8 8.8 %all-to-all-start.1 = ((bf16[8,432,128]{2,1,0:T(8,128)(2,1)}), bf16[8,432,128]{2,1,0:T(8,128)(2,1)}, u32[]{:S(2)}, u32[]{:S(2)}) async-start(bf16[8,432,128]{2,1,0:T(8,128)(2,1)} %pole.1), calls=%async_computation.1 | async-start | bytes 1769472 | tf_op jit(solution)/shard_map/all_to_all | solution.py:541
  54.6 9.4 %collective-permute-start.4 = (bf16[288,1024]{1,0:T(8,128)(2,1)}, bf16[288,1024]{1,0:T(8,128)(2,1)}, u32[]{:S(2)}, u32[]{:S(2)}) collective-permute-start(bf16[288,1024]{1,0:T(8,128)(2,1)} %get-tuple-element.41), channel_id=1, source_target_pairs={{0,8},{8,16},{16,24},{24,32},{32,40},{40,48},{48,56},{56,64},{64,7... | collective-permute-start | bytes 1769480 | tf_op jit(solution)/shard_map/ppermute | solution.py:430
  63.9 1.9 %collective-permute-start.5 = (bf16[288,1024]{1,0:T(8,128)(2,1)}, bf16[288,1024]{1,0:T(8,128)(2,1)}, u32[]{:S(2)}, u32[]{:S(2)}) collective-permute-start(bf16[288,1024]{1,0:T(8,128)(2,1)} %get-tuple-element.42), channel_id=1, source_target_pairs={{8,0},{16,8},{24,16},{32,24},{40,32},{48,40},{56,48},{64,56},{72,6... | collective-permute-start | bytes 1769480 | tf_op jit(solution)/shard_map/ppermute | solution.py:430
  65.9 2.4 %collective-permute-done.4.n_ref = bf16[288,1024]{1,0:T(8,128)(2,1)} collective-permute-done((bf16[288,1024]{1,0:T(8,128)(2,1)}, bf16[288,1024]{1,0:T(8,128)(2,1)}, u32[]{:S(2)}, u32[]{:S(2)}) %collective-permute-start.4) | collective-permute-done | bytes 589856 | tf_op jit(solution)/shard_map/ppermute | solution.py:430
  68.3 6.0 %collective-permute-done.5.s_ref = bf16[288,1024]{1,0:T(8,128)(2,1)} collective-permute-done((bf16[288,1024]{1,0:T(8,128)(2,1)}, bf16[288,1024]{1,0:T(8,128)(2,1)}, u32[]{:S(2)}, u32[]{:S(2)}) %collective-permute-start.5) | collective-permute-done | bytes 589856 | tf_op jit(solution)/shard_map/ppermute | solution.py:430
  74.3 2.4 %pack_back.1 = (bf16[144,1024]{1,0:T(8,128)(2,1)}, bf16[144,1024]{1,0:T(8,128)(2,1)}) custom-call(f32[2,256,1024]{2,1,0:T(8,128)} %get-tuple-element.39.mid_ref, bf16[128,1024]{1,0:T(8,128)(2,1)} %get-tuple-element.40.att_ref, bf16[288,1024]{1,0:T(8,128)(2,1)} %collective-permute-done.4.n_ref, bf16[288,1024]{1,0:T(8,128)(2,1)} %collective-permute-done.5.s_ref), custom_call_target="tpu_custom_call" | custom-call | bytes 3145728 | tf_op jit(solution)/shard_map/pack_back/pallas_call | solution.py:550
  77.8 7.5 %collective-permute-start.6 = (f32[80,128]{1,0:T(8,128)S(1)}, f32[80,128]{1,0:T(8,128)S(1)}, u32[]{:S(2)}, u32[]{:S(2)}) collective-permute-start(f32[80,128]{1,0:T(8,128)S(1)} %slice_add_fusion), channel_id=1, source_target_pairs={{0,8},{8,0},{16,24},{24,16},{32,40},{40,32},{48,56},{56,48},{64,72... | collective-permute-start | bytes 122888 | tf_op jit(solution)/shard_map/ppermute | solution.py:545
  85.3 4.2 %collective-permute-start.9 = (bf16[144,1024]{1,0:T(8,128)(2,1)}, bf16[144,1024]{1,0:T(8,128)(2,1)}, u32[]{:S(2)}, u32[]{:S(2)}) collective-permute-start(bf16[144,1024]{1,0:T(8,128)(2,1)} %get-tuple-element.43), channel_id=1, source_target_pairs={{0,7},{1,0},{2,1},{3,2},{4,3},{5,4},{6,5},{7,6},{8,15},{9,8},{10,9... | collective-permute-start | bytes 884744 | tf_op jit(solution)/shard_map/ppermute | solution.py:430
  89.5 1.9 %collective-permute-start.7 = (f32[80,128]{1,0:T(8,128)S(1)}, f32[80,128]{1,0:T(8,128)S(1)}, u32[]{:S(2)}, u32[]{:S(2)}) collective-permute-start(f32[80,128]{1,0:T(8,128)S(1)} %fusion.1), channel_id=1, source_target_pairs={{0,16},{8,24},{16,0},{24,8},{32,48},{40,56},{48,32},{56,40},{64,80... | collective-permute-start | bytes 122888 | tf_op jit(solution)/shard_map/ppermute | solution.py:545
  91.5 7.6 %collective-permute-done.7 = f32[80,128]{1,0:T(8,128)S(1)} collective-permute-done((f32[80,128]{1,0:T(8,128)S(1)}, f32[80,128]{1,0:T(8,128)S(1)}, u32[]{:S(2)}, u32[]{:S(2)}) %collective-permute-start.7) | collective-permute-done | bytes 40992 | tf_op jit(solution)/shard_map/ppermute | solution.py:545
  99.1 4.0 %collective-permute-done.8 = f32[80,128]{1,0:T(8,128)S(1)} collective-permute-done((f32[80,128]{1,0:T(8,128)S(1)}, f32[80,128]{1,0:T(8,128)S(1)}, u32[]{:S(2)}, u32[]{:S(2)}) %collective-permute-start.8) | collective-permute-done | bytes 40992 | tf_op jit(solution)/shard_map/ppermute | solution.py:545
  103.7 3.6 %collective-permute-start.11 = (f32[80,128]{1,0:T(8,128)}, f32[80,128]{1,0:T(8,128)}, u32[]{:S(2)}, u32[]{:S(2)}) collective-permute-start(f32[80,128]{1,0:T(8,128)} %add.21), channel_id=1, source_target_pairs={{0,64},{8,72},{16,80},{24,88},{32,96},{40,104},{48,112},{56,120},{... | collective-permute-start | bytes 122888 | tf_op jit(solution)/shard_map/ppermute | solution.py:545
  107.3 4.2 %final.1 = (bf16[4,32,1024]{2,1,0:T(8,128)(2,1)}, bf16[4,32,1024]{2,1,0:T(8,128)(2,1)}, bf16[4,32,1024]{2,1,0:T(8,128)(2,1)}, bf16[4,32,1024]{2,1,0:T(8,128)(2,1)}) custom-call(s32[128]{0:T(128)} %polar_ref.5, bf16[128,1024]{1,0:T(8,128)(2,1)} %get-tuple-element.40.att_ref, bf16[128,1024]{1,0:T(8,128)(2,1)} %get-tuple-element.47.dq_ref, ...), custom_call_target="tpu_custom_call" | custom-call | bytes 6291456 | tf_op jit(solution)/shard_map/final/pallas_call | solution.py:576
  112.4 4.6 %collective-permute-start.12 = (f32[80,128]{1,0:T(8,128)S(1)}, f32[80,128]{1,0:T(8,128)S(1)}, u32[]{:S(2)}, u32[]{:S(2)}) collective-permute-start(f32[80,128]{1,0:T(8,128)S(1)} %add.22), channel_id=1, source_target_pairs={{0,128},{8,136},{16,144},{24,152},{32,160},{40,168},{48,176},{56,1... | collective-permute-start | bytes 122888 | tf_op jit(solution)/shard_map/ppermute | solution.py:545
  117.0 3.3 %collective-permute-done.12 = f32[80,128]{1,0:T(8,128)S(1)} collective-permute-done((f32[80,128]{1,0:T(8,128)S(1)}, f32[80,128]{1,0:T(8,128)S(1)}, u32[]{:S(2)}, u32[]{:S(2)}) %collective-permute-start.12) | collective-permute-done | bytes 40992 | tf_op jit(solution)/shard_map/ppermute | solution.py:545
  (23 shorter events, 7.1 us)
Async XLA Ops:
  2.9 12.7 %collective-permute-start = (bf16[144,1024]{1,0:T(8,128)(2,1)}, bf16[144,1024]{1,0:T(8,128)(2,1)}, u32[]{:S(2)}, u32[]{:S(2)}) collective-permute-start(bf16[144,1024]{1,0:T(8,128)(2,1)} %get-tuple-element.33), channel_id=1, source_target_pairs={{0,1},{1,2},{2,3},{3,4},{4,5},{5,6},{6,7},{7,0},{8,9},{9,10},{10,1... | collective-permute-start | bytes 884744 | tf_op jit(solution)/shard_map/ppermute | solution.py:430
  4.3 11.2 %collective-permute-start.1 = (bf16[144,1024]{1,0:T(8,128)(2,1)}, bf16[144,1024]{1,0:T(8,128)(2,1)}, u32[]{:S(2)}, u32[]{:S(2)}) collective-permute-start(bf16[144,1024]{1,0:T(8,128)(2,1)} %get-tuple-element.34), channel_id=1, source_target_pairs={{0,7},{1,0},{2,1},{3,2},{4,3},{5,4},{6,5},{7,6},{8,15},{9,8},{10,9... | collective-permute-start | bytes 884744 | tf_op jit(solution)/shard_map/ppermute | solution.py:430
  17.9 11.2 %collective-permute-start.3 = (bf16[304,1024]{1,0:T(8,128)(2,1)}, bf16[304,1024]{1,0:T(8,128)(2,1)}, u32[]{:S(2)}, u32[]{:S(2)}) collective-permute-start(bf16[304,1024]{1,0:T(8,128)(2,1)} %get-tuple-element.37), channel_id=1, source_target_pairs={{8,0},{16,8},{24,16},{32,24},{40,32},{48,40},{56,48},{64,56},{72,6... | collective-permute-start | bytes 1867784 | tf_op jit(solution)/shard_map/ppermute | solution.py:430
  19.8 12.9 %collective-permute-start.2 = (bf16[304,1024]{1,0:T(8,128)(2,1)}, bf16[304,1024]{1,0:T(8,128)(2,1)}, u32[]{:S(2)}, u32[]{:S(2)}) collective-permute-start(bf16[304,1024]{1,0:T(8,128)(2,1)} %get-tuple-element.35), channel_id=1, source_target_pairs={{0,8},{8,16},{16,24},{24,32},{32,40},{40,48},{48,56},{56,64},{64,7... | collective-permute-start | bytes 1867784 | tf_op jit(solution)/shard_map/ppermute | solution.py:430
  22.3 21.1 %all-to-all-start = ((bf16[8,320,128]{2,1,0:T(8,128)(2,1)}), bf16[8,320,128]{2,1,0:T(8,128)(2,1)}, u32[]{:S(2)}, u32[]{:S(2)}) async-start(bf16[8,320,128]{2,1,0:T(8,128)(2,1)} %get-tuple-element.36), calls=%async_computation | async-start | bytes 1310720 | tf_op jit(solution)/shard_map/all_to_all | solution.py:485
  45.8 31.0 %all-to-all-start.1 = ((bf16[8,432,128]{2,1,0:T(8,128)(2,1)}), bf16[8,432,128]{2,1,0:T(8,128)(2,1)}, u32[]{:S(2)}, u32[]{:S(2)}) async-start(bf16[8,432,128]{2,1,0:T(8,128)(2,1)} %pole.1), calls=%async_computation.1 | async-start | bytes 1769472 | tf_op jit(solution)/shard_map/all_to_all | solution.py:541
  54.6 13.7 %collective-permute-start.4 = (bf16[288,1024]{1,0:T(8,128)(2,1)}, bf16[288,1024]{1,0:T(8,128)(2,1)}, u32[]{:S(2)}, u32[]{:S(2)}) collective-permute-start(bf16[288,1024]{1,0:T(8,128)(2,1)} %get-tuple-element.41), channel_id=1, source_target_pairs={{0,8},{8,16},{16,24},{24,32},{32,40},{40,48},{48,56},{56,64},{64,7... | collective-permute-start | bytes 1769480 | tf_op jit(solution)/shard_map/ppermute | solution.py:430
  63.9 10.4 %collective-permute-start.5 = (bf16[288,1024]{1,0:T(8,128)(2,1)}, bf16[288,1024]{1,0:T(8,128)(2,1)}, u32[]{:S(2)}, u32[]{:S(2)}) collective-permute-start(bf16[288,1024]{1,0:T(8,128)(2,1)} %get-tuple-element.42), channel_id=1, source_target_pairs={{8,0},{16,8},{24,16},{32,24},{40,32},{48,40},{56,48},{64,56},{72,6... | collective-permute-start | bytes 1769480 | tf_op jit(solution)/shard_map/ppermute | solution.py:430
  77.8 11.7 %collective-permute-start.6 = (f32[80,128]{1,0:T(8,128)S(1)}, f32[80,128]{1,0:T(8,128)S(1)}, u32[]{:S(2)}, u32[]{:S(2)}) collective-permute-start(f32[80,128]{1,0:T(8,128)S(1)} %slice_add_fusion), channel_id=1, source_target_pairs={{0,8},{8,0},{16,24},{24,16},{32,40},{40,32},{48,56},{56,48},{64,72... | collective-permute-start | bytes 122888 | tf_op jit(solution)/shard_map/ppermute | solution.py:545
  85.3 18.4 %collective-permute-start.9 = (bf16[144,1024]{1,0:T(8,128)(2,1)}, bf16[144,1024]{1,0:T(8,128)(2,1)}, u32[]{:S(2)}, u32[]{:S(2)}) collective-permute-start(bf16[144,1024]{1,0:T(8,128)(2,1)} %get-tuple-element.43), channel_id=1, source_target_pairs={{0,7},{1,0},{2,1},{3,2},{4,3},{5,4},{6,5},{7,6},{8,15},{9,8},{10,9... | collective-permute-start | bytes 884744 | tf_op jit(solution)/shard_map/ppermute | solution.py:430
  89.5 14.2 %collective-permute-start.10 = (bf16[144,1024]{1,0:T(8,128)(2,1)}, bf16[144,1024]{1,0:T(8,128)(2,1)}, u32[]{:S(2)}, u32[]{:S(2)}) collective-permute-start(bf16[144,1024]{1,0:T(8,128)(2,1)} %get-tuple-element.45), channel_id=1, source_target_pairs={{0,1},{1,2},{2,3},{3,4},{4,5},{5,6},{6,7},{7,0},{8,9},{9,10},{10,1... | collective-permute-start | bytes 884744 | tf_op jit(solution)/shard_map/ppermute | solution.py:430
  89.5 9.6 %collective-permute-start.7 = (f32[80,128]{1,0:T(8,128)S(1)}, f32[80,128]{1,0:T(8,128)S(1)}, u32[]{:S(2)}, u32[]{:S(2)}) collective-permute-start(f32[80,128]{1,0:T(8,128)S(1)} %fusion.1), channel_id=1, source_target_pairs={{0,16},{8,24},{16,0},{24,8},{32,48},{40,56},{48,32},{56,40},{64,80... | collective-permute-start | bytes 122888 | tf_op jit(solution)/shard_map/ppermute | solution.py:545
  99.1 4.0 %collective-permute-start.8 = (f32[80,128]{1,0:T(8,128)S(1)}, f32[80,128]{1,0:T(8,128)S(1)}, u32[]{:S(2)}, u32[]{:S(2)}) collective-permute-start(f32[80,128]{1,0:T(8,128)S(1)} %add.20), channel_id=1, source_target_pairs={{0,32},{8,40},{16,48},{24,56},{32,0},{40,8},{48,16},{56,24},{64,96... | collective-permute-start | bytes 122888 | tf_op jit(solution)/shard_map/ppermute | solution.py:545
  103.7 7.8 %collective-permute-start.11 = (f32[80,128]{1,0:T(8,128)}, f32[80,128]{1,0:T(8,128)}, u32[]{:S(2)}, u32[]{:S(2)}) collective-permute-start(f32[80,128]{1,0:T(8,128)} %add.21), channel_id=1, source_target_pairs={{0,64},{8,72},{16,80},{24,88},{32,96},{40,104},{48,112},{56,120},{... | collective-permute-start | bytes 122888 | tf_op jit(solution)/shard_map/ppermute | solution.py:545
  112.4 7.9 %collective-permute-start.12 = (f32[80,128]{1,0:T(8,128)S(1)}, f32[80,128]{1,0:T(8,128)S(1)}, u32[]{:S(2)}, u32[]{:S(2)}) collective-permute-start(f32[80,128]{1,0:T(8,128)S(1)} %add.22), channel_id=1, source_target_pairs={{0,128},{8,136},{16,144},{24,152},{32,160},{40,168},{48,176},{56,1... | collective-permute-start | bytes 122888 | tf_op jit(solution)/shard_map/ppermute | solution.py:545

commit v3 on v2

--- a/solution.py
+++ b/solution.py
@@ -25,7 +25,8 @@
 GRANT = 64
 
 LON_TOK = 144
-LAT_TOK = 304
+LAT_TOK = 160
+CORNER_TOK = 144
 BACK_LAT = 288
 BACK_LON = 144
 POLE_IN = 320
@@ -120,7 +121,7 @@
         copy.wait()
 
 
-def pack_lon_kernel(q_ref, k_ref, v_ref, c_ref, east_ref, west_ref, pole_out, edge):
+def pack_lon_kernel(q_ref, k_ref, v_ref, c_ref, east_ref, west_ref, south_ref, north_ref, pole_out, edge):
     half = ROWS * SIDE
     wide = edge.shape[1]
     for out, start, col in ((east_ref, COLS - SIDE, COLS - 1), (west_ref, 0, 0)):
@@ -133,6 +134,10 @@
         out[2 * half :] = edge[...].astype(BF16)
     lat, lon, start = place()
     both = REACH * COLS
+    for out, first, row in ((south_ref, ROWS - REACH, ROWS - 1), (north_ref, 0, 0)):
+        out[:both] = k_ref[first : first + REACH].reshape(both, wide)
+        out[both : 2 * both] = v_ref[first : first + REACH].reshape(both, wide)
+        out[2 * both :] = c_ref[row]
 
     @pl.when(at_pole(lat))
     def _():
@@ -145,26 +150,20 @@
             pole_out[part, 3 * both :] = c_ref[:, :, lanes].reshape(ROWS * COLS, LANES)
 
 
-def pack_lat_kernel(k_ref, v_ref, c_ref, w_ref, e_ref, south_ref, north_ref, edge):
-    own = REACH * COLS
+def pack_corner_kernel(w_ref, e_ref, south_ref, north_ref, edge):
     side = REACH * SIDE
     half = ROWS * SIDE
-    wide = edge.shape[1]
     west_cot = w_ref[2 * half :].astype(F32)
     east_cot = e_ref[2 * half :].astype(F32)
     for out, start, row in ((south_ref, ROWS - REACH, ROWS - 1), (north_ref, 0, 0)):
-        for index, ref in enumerate((k_ref, v_ref)):
-            base = index * (own + 2 * side)
+        for index in range(2):
             near = index * half + start * SIDE
-            out[base : base + own] = ref[start : start + REACH].reshape(own, wide)
-            out[base + own : base + own + side] = w_ref[near : near + side]
-            out[base + own + side : base + own + 2 * side] = e_ref[near : near + side]
-        base = 2 * (own + 2 * side)
-        out[base : base + COLS] = c_ref[row]
+            out[2 * index * side : (2 * index + 1) * side] = w_ref[near : near + side]
+            out[(2 * index + 1) * side : (2 * index + 2) * side] = e_ref[near : near + side]
         edge[...] = jnp.zeros_like(edge)
         edge[0:1] = west_cot[row : row + 1]
         edge[1:2] = east_cot[row : row + 1]
-        out[base + COLS :] = edge[...].astype(BF16)
+        out[4 * side :] = edge[...].astype(BF16)
 
 
 def fill_rim(pad, row, middle, west, east):
@@ -184,7 +183,8 @@
 
 
 def window_kernel(
-    pattern_ref, polar_ref, q_ref, k_ref, v_ref, c_ref, w_ref, e_ref, n_ref, s_ref, conv_ref,
+    pattern_ref, polar_ref, q_ref, k_ref, v_ref, c_ref, w_ref, e_ref,
+    n_ref, s_ref, nc_ref, sc_ref, conv_ref,
     att_ref, dq_ref, south_ref, north_ref, mid_ref, kg_ref, pad, bias_ref,
 ):
     tokens = ROWS * COLS
@@ -223,9 +223,11 @@
         fill_rim(
             pad, row + 1, c_ref[row].astype(F32), west_cot[row : row + 1], east_cot[row : row + 1]
         )
-    for row, ref in ((0, n_ref), (ROWS + 1, s_ref)):
-        cells = ref[2 * rim :].astype(F32)
-        fill_rim(pad, row, cells[:COLS], cells[COLS : COLS + 1], cells[COLS + 1 : COLS + 2])
+    own = REACH * COLS
+    corner = 2 * REACH * SIDE
+    for row, ref, corner_ref in ((0, n_ref, nc_ref), (ROWS + 1, s_ref, sc_ref)):
+        cells = corner_ref[2 * corner :].astype(F32)
+        fill_rim(pad, row, ref[2 * own :].astype(F32), cells[0:1], cells[1:2])
     for part in range(wide // LANES):
         lanes = slice(part * LANES, (part + 1) * LANES)
         taps = [
@@ -243,8 +245,10 @@
                     ref[:, :, lanes].reshape(tokens, LANES),
                     w_ref[index * half : (index + 1) * half, lanes],
                     e_ref[index * half : (index + 1) * half, lanes],
-                    n_ref[index * rim : (index + 1) * rim, lanes],
-                    s_ref[index * rim : (index + 1) * rim, lanes],
+                    n_ref[index * own : (index + 1) * own, lanes],
+                    nc_ref[index * corner : (index + 1) * corner, lanes],
+                    s_ref[index * own : (index + 1) * own, lanes],
+                    sc_ref[index * corner : (index + 1) * corner, lanes],
                 ],
                 axis=0,
             )
@@ -453,13 +457,16 @@
 
     anywhere = pl.BlockSpec(memory_space=pl.ANY)
 
-    east_pay, west_pay, pole_pay = pl.pallas_call(
+    east_pay, west_pay, south_pay, north_pay, pole_pay = pl.pallas_call(
         pack_lon_kernel,
         grid=(width // pack,),
         in_specs=[packed(ROWS, COLS)] * 4,
         out_specs=[packed(LON_TOK)] * 2
+        + [packed(LAT_TOK)] * 2
         + [pl.BlockSpec((pack // LANES, POLE_IN, LANES), lambda j: (j, 0, 0))],
-        out_shape=[sds((LON_TOK, width))] * 2 + [sds((PAIRS, POLE_IN, LANES))],
+        out_shape=[sds((LON_TOK, width))] * 2
+        + [sds((LAT_TOK, width))] * 2
+        + [sds((PAIRS, POLE_IN, LANES))],
         scratch_shapes=[halo(16, wide=pack)],
         compiler_params=params(GRANT),
         cost_estimate=cost(0, 3 * 2**20),
@@ -468,20 +475,22 @@
     from_west = shift(east_pay, "lon", 1, True)
     from_east = shift(west_pay, "lon", -1, True)
 
-    south_pay, north_pay = pl.pallas_call(
-        pack_lat_kernel,
+    from_north = shift(south_pay, "lat", 1, False)
+    from_south = shift(north_pay, "lat", -1, False)
+    south_corner, north_corner = pl.pallas_call(
+        pack_corner_kernel,
         grid=(width // pack,),
-        in_specs=[packed(ROWS, COLS)] * 3 + [packed(LON_TOK)] * 2,
-        out_specs=[packed(LAT_TOK)] * 2,
-        out_shape=[sds((LAT_TOK, width))] * 2,
+        in_specs=[packed(LON_TOK)] * 2,
+        out_specs=[packed(CORNER_TOK)] * 2,
+        out_shape=[sds((CORNER_TOK, width))] * 2,
         scratch_shapes=[halo(16, wide=pack)],
         compiler_params=params(GRANT),
-        cost_estimate=cost(0, 3 * 2**20),
-        name="pack_lat",
-    )(keys, values, cotangent, from_west, from_east)
-    from_north = shift(south_pay, "lat", 1, False)
-    from_south = shift(north_pay, "lat", -1, False)
-    pole_pay, _ = lax.optimization_barrier((pole_pay, south_pay))
+        cost_estimate=cost(0, 2 * 2**20),
+        name="pack_corner",
+    )(from_west, from_east)
+    north_corners = shift(south_corner, "lat", 1, False)
+    south_corners = shift(north_corner, "lat", -1, False)
+    pole_pay, _ = lax.optimization_barrier((pole_pay, south_corner))
     pole_in = lax.all_to_all(pole_pay, "lon", 0, 0)
 
     att, dq_near, south_back, north_back, mid, kg = pl.pallas_call(
@@ -491,6 +500,7 @@
         + [spanned(ROWS, COLS)] * 4
         + [spanned(LON_TOK)] * 2
         + [spanned(LAT_TOK)] * 2
+        + [spanned(CORNER_TOK)] * 2
         + [spanned(9)],
         out_specs=[
             spanned(tokens),
@@ -514,7 +524,7 @@
         name="window",
     )(
         pattern.T, polar, queries, keys, values, cotangent, from_west, from_east,
-        from_north, from_south, conv_kernel,
+        from_north, from_south, north_corners, south_corners, conv_kernel,
     )
     back_north = shift(south_back, "lat", 1, False)
     back_south = shift(north_back, "lat", -1, False)

time: 123 us -> 119 us (0.967); the launches traced: 121 us -> 119 us
  starting transfers between devices: 58.7 us -> 57.2 us
    all_to_all x1, starting transfers between devices: 8.8 us -> 4.23 us  [body(): pole_back = lax.all_to_all(pole_out, 'lon', 0, 0)]
    ppermute x8 -> x10, waiting for transfers between devices: 19.1 us -> 14.7 us  [shift(): return lax.ppermute(array, axis, route)]
    ppermute x8 -> x10, starting transfers between devices: 25.4 us -> 29.7 us  [shift(): return lax.ppermute(array, axis, route)]
    all_to_all x1, waiting for transfers between devices: 0.52 us -> 3.01 us  [body(): pole_in = lax.all_to_all(pole_pay, 'lon', 0, 0)]
    ppermute x5, starting transfers between devices: 17.7 us -> 15.7 us  [summed(): return array + lax.ppermute(array, 'lat', route)]
  transfers between devices with their start and end apart: 15 -> 17, of which waited for: 8 -> 7; matrix products, arithmetic and copies ran while one was open for 1% -> 1% of each run, Pallas kernels for 14% -> 16%
where the time goes in v3:
time: 119 us
  starting transfers between devices  57.2 us (48%)
  waiting for transfers between devices  33.9 us (28%)
  Pallas kernels  23.5 us (20%)
  other arithmetic  2.49 us (2%)
    ppermute x10, starting transfers between devices, shift(): return lax.ppermute(array, axis, route)  29.7 us
    ppermute x5, waiting for transfers between devices, summed(): return array + lax.ppermute(array, 'lat', route)  16.1 us
    ppermute x5, starting transfers between devices, summed(): return array + lax.ppermute(array, 'lat', route)  15.7 us
    ppermute x10, waiting for transfers between devices, shift(): return lax.ppermute(array, axis, route)  14.7 us
    pallas_call x1, Pallas kernels, body(): pl.pallas_call(window_kernel, grid=(width // span,), in_specs=[SMEM, SMEM...  10.2 us
    all_to_all x1, starting transfers between devices, body(): pole_in = lax.all_to_all(pole_pay, 'lon', 0, 0)  7.6 us
    all_to_all x1, starting transfers between devices, body(): pole_back = lax.all_to_all(pole_out, 'lon', 0, 0)  4.23 us
    pallas_call x1, Pallas kernels, body(): pl.pallas_call(final_kernel, grid=(width // span,), in_specs=[SMEM, spann...  4.19 us
  transfers between devices with their start and end apart: 17, of which 7 were waited for; matrix products, arithmetic and copies ran while one was open for 1% of the time, Pallas kernels for 16%

profile of v3, /device:TPU:32, one launch (start us, length us, event | category | flops | bytes accessed | tf_op | source)
XLA Modules:
  0.0 118.5 jit_solution(8546472516476505617)
XLA Ops:
  0.6 2.5 %pack_lon.1 = (bf16[144,1024]{1,0:T(8,128)(2,1)}, bf16[144,1024]{1,0:T(8,128)(2,1)}, bf16[160,1024]{1,0:T(8,128)(2,1)}, bf16[160,1024]{1,0:T(8,128)(2,1)}, bf16[8,320,128]{2,1,0:T(8,128)(2,1)}) custom-call(bf16[4,32,1024]{2,1,0:T(8,128)(2,1)} %q_ref.3, bf16[4,32,1024]{2,1,0:T(8,128)(2,1)} %k_ref.3, bf16[4,32,1024]{2,1,0:T(8,128)(2,1)} %v_ref.3, ...), custom_call_target="tpu_custom_call" | custom-call | bytes 3145728 | tf_op jit(solution)/shard_map/pack_lon/pallas_call | solution.py:460
  4.6 4.1 %collective-permute-start.1 = (bf16[144,1024]{1,0:T(8,128)(2,1)}, bf16[144,1024]{1,0:T(8,128)(2,1)}, u32[]{:S(2)}, u32[]{:S(2)}) collective-permute-start(bf16[144,1024]{1,0:T(8,128)(2,1)} %get-tuple-element.36), channel_id=1, source_target_pairs={{0,7},{1,0},{2,1},{3,2},{4,3},{5,4},{6,5},{7,6},{8,15},{9,8},{10,9... | collective-permute-start | bytes 884744 | tf_op jit(solution)/shard_map/ppermute | solution.py:434
  10.7 4.5 %collective-permute-start.3 = (bf16[160,1024]{1,0:T(8,128)(2,1)}, bf16[160,1024]{1,0:T(8,128)(2,1)}, u32[]{:S(2)}, u32[]{:S(2)}) collective-permute-start(bf16[160,1024]{1,0:T(8,128)(2,1)} %get-tuple-element.40), channel_id=1, source_target_pairs={{8,0},{16,8},{24,16},{32,24},{40,32},{48,40},{56,48},{64,56},{72,6... | collective-permute-start | bytes 983048 | tf_op jit(solution)/shard_map/ppermute | solution.py:434
  15.8 1.9 %pack_corner.1 = (bf16[144,1024]{1,0:T(8,128)(2,1)}, bf16[144,1024]{1,0:T(8,128)(2,1)}) custom-call(bf16[144,1024]{1,0:T(8,128)(2,1)} %collective-permute-done.w_ref, bf16[144,1024]{1,0:T(8,128)(2,1)} %collective-permute-done.1.e_ref), custom_call_target="tpu_custom_call" | custom-call | bytes 2097152 | tf_op jit(solution)/shard_map/pack_corner/pallas_call | solution.py:480
  17.7 1.9 %collective-permute-start.5 = (bf16[144,1024]{1,0:T(8,128)(2,1)}, bf16[144,1024]{1,0:T(8,128)(2,1)}, u32[]{:S(2)}, u32[]{:S(2)}) collective-permute-start(bf16[144,1024]{1,0:T(8,128)(2,1)} %get-tuple-element.41), channel_id=1, source_target_pairs={{8,0},{16,8},{24,16},{32,24},{40,32},{48,40},{56,48},{64,56},{72,6... | collective-permute-start | bytes 884744 | tf_op jit(solution)/shard_map/ppermute | solution.py:434
  19.7 2.4 %collective-permute-start.4 = (bf16[144,1024]{1,0:T(8,128)(2,1)}, bf16[144,1024]{1,0:T(8,128)(2,1)}, u32[]{:S(2)}, u32[]{:S(2)}) collective-permute-start(bf16[144,1024]{1,0:T(8,128)(2,1)} %get-tuple-element.37), channel_id=1, source_target_pairs={{0,8},{8,16},{16,24},{24,32},{32,40},{40,48},{48,56},{56,64},{64,7... | collective-permute-start | bytes 884744 | tf_op jit(solution)/shard_map/ppermute | solution.py:434
  22.1 7.6 %all-to-all-start = ((bf16[8,320,128]{2,1,0:T(8,128)(2,1)}), bf16[8,320,128]{2,1,0:T(8,128)(2,1)}, u32[]{:S(2)}, u32[]{:S(2)}) async-start(bf16[8,320,128]{2,1,0:T(8,128)(2,1)} %get-tuple-element.38), calls=%async_computation | async-start | bytes 1310720 | tf_op jit(solution)/shard_map/all_to_all | solution.py:494
  29.7 10.2 %window.1 = (bf16[128,1024]{1,0:T(8,128)(2,1)}, bf16[128,1024]{1,0:T(8,128)(2,1)}, bf16[288,1024]{1,0:T(8,128)(2,1)}, bf16[288,1024]{1,0:T(8,128)(2,1)}, f32[2,256,1024]{2,1,0:T(8,128)}, /*index=5*/f32[9,1024]{1,0:T(8,128)}) custom-call(s32[2,128]{1,0:T(2,128)} %bitcast.8, s32[128]{0:T(128)} %polar_ref.5, bf16[4,32,1024]{2,1,0:T(8,128)(2,1)} %q_ref.3, ...), custom_call_target="tpu_custom_call" | custom-call | flops 4000000000 | bytes 8388608 | tf_op jit(solution)/shard_map/window/pallas_call | solution.py:496
  39.9 3.0 %all-to-all-done.pole_in_ref = bf16[8,320,128]{2,1,0:T(8,128)(2,1)} async-done(((bf16[8,320,128]{2,1,0:T(8,128)(2,1)}), bf16[8,320,128]{2,1,0:T(8,128)(2,1)}, u32[]{:S(2)}, u32[]{:S(2)}) %all-to-all-start) | async-done | bytes 655392 | tf_op jit(solution)/shard_map/all_to_all | solution.py:494
  42.9 2.3 %pole.1 = bf16[8,432,128]{2,1,0:T(8,128)(2,1)} custom-call(s32[128]{0:T(128)} %polar_ref.5, bf16[8,320,128]{2,1,0:T(8,128)(2,1)} %all-to-all-done.pole_in_ref, f32[9,1024]{1,0:T(8,128)} %conv_ref.5, f32[9,1024]{1,0:T(8,128)} %get-tuple-element.42.kgin_ref), custom_call_target="tpu_custom_call" | custom-call | flops 1000000000 | bytes 4194304 | tf_op jit(solution)/shard_map/pole/pallas_call | solution.py:532
  45.2 4.2 %all-to-all-start.1 = ((bf16[8,432,128]{2,1,0:T(8,128)(2,1)}), bf16[8,432,128]{2,1,0:T(8,128)(2,1)}, u32[]{:S(2)}, u32[]{:S(2)}) async-start(bf16[8,432,128]{2,1,0:T(8,128)(2,1)} %pole.1), calls=%async_computation.1 | async-start | bytes 1769472 | tf_op jit(solution)/shard_map/all_to_all | solution.py:551
  49.5 5.5 %collective-permute-start.6 = (bf16[288,1024]{1,0:T(8,128)(2,1)}, bf16[288,1024]{1,0:T(8,128)(2,1)}, u32[]{:S(2)}, u32[]{:S(2)}) collective-permute-start(bf16[288,1024]{1,0:T(8,128)(2,1)} %get-tuple-element.45), channel_id=1, source_target_pairs={{0,8},{8,16},{16,24},{24,32},{32,40},{40,48},{48,56},{56,64},{64,7... | collective-permute-start | bytes 1769480 | tf_op jit(solution)/shard_map/ppermute | solution.py:434
  55.0 1.9 %collective-permute-start.7 = (bf16[288,1024]{1,0:T(8,128)(2,1)}, bf16[288,1024]{1,0:T(8,128)(2,1)}, u32[]{:S(2)}, u32[]{:S(2)}) collective-permute-start(bf16[288,1024]{1,0:T(8,128)(2,1)} %get-tuple-element.46), channel_id=1, source_target_pairs={{8,0},{16,8},{24,16},{32,24},{40,32},{48,40},{56,48},{64,56},{72,6... | collective-permute-start | bytes 1769480 | tf_op jit(solution)/shard_map/ppermute | solution.py:434
  56.9 12.2 %collective-permute-done.6.n_ref = bf16[288,1024]{1,0:T(8,128)(2,1)} collective-permute-done((bf16[288,1024]{1,0:T(8,128)(2,1)}, bf16[288,1024]{1,0:T(8,128)(2,1)}, u32[]{:S(2)}, u32[]{:S(2)}) %collective-permute-start.6) | collective-permute-done | bytes 589856 | tf_op jit(solution)/shard_map/ppermute | solution.py:434
  69.1 1.9 %collective-permute-done.7.s_ref = bf16[288,1024]{1,0:T(8,128)(2,1)} collective-permute-done((bf16[288,1024]{1,0:T(8,128)(2,1)}, bf16[288,1024]{1,0:T(8,128)(2,1)}, u32[]{:S(2)}, u32[]{:S(2)}) %collective-permute-start.7) | collective-permute-done | bytes 589856 | tf_op jit(solution)/shard_map/ppermute | solution.py:434
  71.0 2.4 %pack_back.1 = (bf16[144,1024]{1,0:T(8,128)(2,1)}, bf16[144,1024]{1,0:T(8,128)(2,1)}) custom-call(f32[2,256,1024]{2,1,0:T(8,128)} %get-tuple-element.43.mid_ref, bf16[128,1024]{1,0:T(8,128)(2,1)} %get-tuple-element.44.att_ref, bf16[288,1024]{1,0:T(8,128)(2,1)} %collective-permute-done.6.n_ref, bf16[288,1024]{1,0:T(8,128)(2,1)} %collective-permute-done.7.s_ref), custom_call_target="tpu_custom_call" | custom-call | bytes 3145728 | tf_op jit(solution)/shard_map/pack_back/pallas_call | solution.py:560
  74.5 5.4 %collective-permute-start.8 = (f32[80,128]{1,0:T(8,128)S(1)}, f32[80,128]{1,0:T(8,128)S(1)}, u32[]{:S(2)}, u32[]{:S(2)}) collective-permute-start(f32[80,128]{1,0:T(8,128)S(1)} %slice_add_fusion), channel_id=1, source_target_pairs={{0,8},{8,0},{16,24},{24,16},{32,40},{40,32},{48,56},{56,48},{64,72... | collective-permute-start | bytes 122888 | tf_op jit(solution)/shard_map/ppermute | solution.py:555
  79.9 5.9 %collective-permute-start.11 = (bf16[144,1024]{1,0:T(8,128)(2,1)}, bf16[144,1024]{1,0:T(8,128)(2,1)}, u32[]{:S(2)}, u32[]{:S(2)}) collective-permute-start(bf16[144,1024]{1,0:T(8,128)(2,1)} %get-tuple-element.47), channel_id=1, source_target_pairs={{0,7},{1,0},{2,1},{3,2},{4,3},{5,4},{6,5},{7,6},{8,15},{9,8},{10,9... | collective-permute-start | bytes 884744 | tf_op jit(solution)/shard_map/ppermute | solution.py:434
  85.8 9.6 %collective-permute-done.9 = f32[80,128]{1,0:T(8,128)S(1)} collective-permute-done((f32[80,128]{1,0:T(8,128)S(1)}, f32[80,128]{1,0:T(8,128)S(1)}, u32[]{:S(2)}, u32[]{:S(2)}) %collective-permute-start.9) | collective-permute-done | bytes 40992 | tf_op jit(solution)/shard_map/ppermute | solution.py:555
  96.1 3.4 %collective-permute-done.10 = f32[80,128]{1,0:T(8,128)S(1)} collective-permute-done((f32[80,128]{1,0:T(8,128)S(1)}, f32[80,128]{1,0:T(8,128)S(1)}, u32[]{:S(2)}, u32[]{:S(2)}) %collective-permute-start.10) | collective-permute-done | bytes 40992 | tf_op jit(solution)/shard_map/ppermute | solution.py:555
  100.1 4.7 %collective-permute-start.13 = (f32[80,128]{1,0:T(8,128)}, f32[80,128]{1,0:T(8,128)}, u32[]{:S(2)}, u32[]{:S(2)}) collective-permute-start(f32[80,128]{1,0:T(8,128)} %add.21), channel_id=1, source_target_pairs={{0,64},{8,72},{16,80},{24,88},{32,96},{40,104},{48,112},{56,120},{... | collective-permute-start | bytes 122888 | tf_op jit(solution)/shard_map/ppermute | solution.py:555
  104.8 4.2 %final.1 = (bf16[4,32,1024]{2,1,0:T(8,128)(2,1)}, bf16[4,32,1024]{2,1,0:T(8,128)(2,1)}, bf16[4,32,1024]{2,1,0:T(8,128)(2,1)}, bf16[4,32,1024]{2,1,0:T(8,128)(2,1)}) custom-call(s32[128]{0:T(128)} %polar_ref.5, bf16[128,1024]{1,0:T(8,128)(2,1)} %get-tuple-element.44.att_ref, bf16[128,1024]{1,0:T(8,128)(2,1)} %get-tuple-element.51.dq_ref, ...), custom_call_target="tpu_custom_call" | custom-call | bytes 6291456 | tf_op jit(solution)/shard_map/final/pallas_call | solution.py:586
  109.8 4.9 %collective-permute-start.14 = (f32[80,128]{1,0:T(8,128)S(1)}, f32[80,128]{1,0:T(8,128)S(1)}, u32[]{:S(2)}, u32[]{:S(2)}) collective-permute-start(f32[80,128]{1,0:T(8,128)S(1)} %add.22), channel_id=1, source_target_pairs={{0,128},{8,136},{16,144},{24,152},{32,160},{40,168},{48,176},{56,1... | collective-permute-start | bytes 122888 | tf_op jit(solution)/shard_map/ppermute | solution.py:555
  114.7 3.2 %collective-permute-done.14 = f32[80,128]{1,0:T(8,128)S(1)} collective-permute-done((f32[80,128]{1,0:T(8,128)S(1)}, f32[80,128]{1,0:T(8,128)S(1)}, u32[]{:S(2)}, u32[]{:S(2)}) %collective-permute-start.14) | collective-permute-done | bytes 40992 | tf_op jit(solution)/shard_map/ppermute | solution.py:555
  (27 shorter events, 7.9 us)
Async XLA Ops:
  3.1 12.7 %collective-permute-start = (bf16[144,1024]{1,0:T(8,128)(2,1)}, bf16[144,1024]{1,0:T(8,128)(2,1)}, u32[]{:S(2)}, u32[]{:S(2)}) collective-permute-start(bf16[144,1024]{1,0:T(8,128)(2,1)} %get-tuple-element.35), channel_id=1, source_target_pairs={{0,1},{1,2},{2,3},{3,4},{4,5},{5,6},{6,7},{7,0},{8,9},{9,10},{10,1... | collective-permute-start | bytes 884744 | tf_op jit(solution)/shard_map/ppermute | solution.py:434
  4.6 11.2 %collective-permute-start.1 = (bf16[144,1024]{1,0:T(8,128)(2,1)}, bf16[144,1024]{1,0:T(8,128)(2,1)}, u32[]{:S(2)}, u32[]{:S(2)}) collective-permute-start(bf16[144,1024]{1,0:T(8,128)(2,1)} %get-tuple-element.36), channel_id=1, source_target_pairs={{0,7},{1,0},{2,1},{3,2},{4,3},{5,4},{6,5},{7,6},{8,15},{9,8},{10,9... | collective-permute-start | bytes 884744 | tf_op jit(solution)/shard_map/ppermute | solution.py:434
  8.7 20.9 %collective-permute-start.2 = (bf16[160,1024]{1,0:T(8,128)(2,1)}, bf16[160,1024]{1,0:T(8,128)(2,1)}, u32[]{:S(2)}, u32[]{:S(2)}) collective-permute-start(bf16[160,1024]{1,0:T(8,128)(2,1)} %get-tuple-element.39), channel_id=1, source_target_pairs={{0,8},{8,16},{16,24},{24,32},{32,40},{40,48},{48,56},{56,64},{64,7... | collective-permute-start | bytes 983048 | tf_op jit(solution)/shard_map/ppermute | solution.py:434
  10.7 19.0 %collective-permute-start.3 = (bf16[160,1024]{1,0:T(8,128)(2,1)}, bf16[160,1024]{1,0:T(8,128)(2,1)}, u32[]{:S(2)}, u32[]{:S(2)}) collective-permute-start(bf16[160,1024]{1,0:T(8,128)(2,1)} %get-tuple-element.40), channel_id=1, source_target_pairs={{8,0},{16,8},{24,16},{32,24},{40,32},{48,40},{56,48},{64,56},{72,6... | collective-permute-start | bytes 983048 | tf_op jit(solution)/shard_map/ppermute | solution.py:434
  17.7 12.0 %collective-permute-start.5 = (bf16[144,1024]{1,0:T(8,128)(2,1)}, bf16[144,1024]{1,0:T(8,128)(2,1)}, u32[]{:S(2)}, u32[]{:S(2)}) collective-permute-start(bf16[144,1024]{1,0:T(8,128)(2,1)} %get-tuple-element.41), channel_id=1, source_target_pairs={{8,0},{16,8},{24,16},{32,24},{40,32},{48,40},{56,48},{64,56},{72,6... | collective-permute-start | bytes 884744 | tf_op jit(solution)/shard_map/ppermute | solution.py:434
  19.7 10.0 %collective-permute-start.4 = (bf16[144,1024]{1,0:T(8,128)(2,1)}, bf16[144,1024]{1,0:T(8,128)(2,1)}, u32[]{:S(2)}, u32[]{:S(2)}) collective-permute-start(bf16[144,1024]{1,0:T(8,128)(2,1)} %get-tuple-element.37), channel_id=1, source_target_pairs={{0,8},{8,16},{16,24},{24,32},{32,40},{40,48},{48,56},{56,64},{64,7... | collective-permute-start | bytes 884744 | tf_op jit(solution)/shard_map/ppermute | solution.py:434
  22.1 20.8 %all-to-all-start = ((bf16[8,320,128]{2,1,0:T(8,128)(2,1)}), bf16[8,320,128]{2,1,0:T(8,128)(2,1)}, u32[]{:S(2)}, u32[]{:S(2)}) async-start(bf16[8,320,128]{2,1,0:T(8,128)(2,1)} %get-tuple-element.38), calls=%async_computation | async-start | bytes 1310720 | tf_op jit(solution)/shard_map/all_to_all | solution.py:494
  45.2 28.2 %all-to-all-start.1 = ((bf16[8,432,128]{2,1,0:T(8,128)(2,1)}), bf16[8,432,128]{2,1,0:T(8,128)(2,1)}, u32[]{:S(2)}, u32[]{:S(2)}) async-start(bf16[8,432,128]{2,1,0:T(8,128)(2,1)} %pole.1), calls=%async_computation.1 | async-start | bytes 1769472 | tf_op jit(solution)/shard_map/all_to_all | solution.py:551
  49.5 19.6 %collective-permute-start.6 = (bf16[288,1024]{1,0:T(8,128)(2,1)}, bf16[288,1024]{1,0:T(8,128)(2,1)}, u32[]{:S(2)}, u32[]{:S(2)}) collective-permute-start(bf16[288,1024]{1,0:T(8,128)(2,1)} %get-tuple-element.45), channel_id=1, source_target_pairs={{0,8},{8,16},{16,24},{24,32},{32,40},{40,48},{48,56},{56,64},{64,7... | collective-permute-start | bytes 1769480 | tf_op jit(solution)/shard_map/ppermute | solution.py:434
  55.0 16.0 %collective-permute-start.7 = (bf16[288,1024]{1,0:T(8,128)(2,1)}, bf16[288,1024]{1,0:T(8,128)(2,1)}, u32[]{:S(2)}, u32[]{:S(2)}) collective-permute-start(bf16[288,1024]{1,0:T(8,128)(2,1)} %get-tuple-element.46), channel_id=1, source_target_pairs={{8,0},{16,8},{24,16},{32,24},{40,32},{48,40},{56,48},{64,56},{72,6... | collective-permute-start | bytes 1769480 | tf_op jit(solution)/shard_map/ppermute | solution.py:434
  74.5 11.3 %collective-permute-start.8 = (f32[80,128]{1,0:T(8,128)S(1)}, f32[80,128]{1,0:T(8,128)S(1)}, u32[]{:S(2)}, u32[]{:S(2)}) collective-permute-start(f32[80,128]{1,0:T(8,128)S(1)} %slice_add_fusion), channel_id=1, source_target_pairs={{0,8},{8,0},{16,24},{24,16},{32,40},{40,32},{48,56},{56,48},{64,72... | collective-permute-start | bytes 122888 | tf_op jit(solution)/shard_map/ppermute | solution.py:555
  79.9 20.2 %collective-permute-start.11 = (bf16[144,1024]{1,0:T(8,128)(2,1)}, bf16[144,1024]{1,0:T(8,128)(2,1)}, u32[]{:S(2)}, u32[]{:S(2)}) collective-permute-start(bf16[144,1024]{1,0:T(8,128)(2,1)} %get-tuple-element.47), channel_id=1, source_target_pairs={{0,7},{1,0},{2,1},{3,2},{4,3},{5,4},{6,5},{7,6},{8,15},{9,8},{10,9... | collective-permute-start | bytes 884744 | tf_op jit(solution)/shard_map/ppermute | solution.py:434
  85.7 14.4 %collective-permute-start.12 = (bf16[144,1024]{1,0:T(8,128)(2,1)}, bf16[144,1024]{1,0:T(8,128)(2,1)}, u32[]{:S(2)}, u32[]{:S(2)}) collective-permute-start(bf16[144,1024]{1,0:T(8,128)(2,1)} %get-tuple-element.49), channel_id=1, source_target_pairs={{0,1},{1,2},{2,3},{3,4},{4,5},{5,6},{6,7},{7,0},{8,9},{9,10},{10,1... | collective-permute-start | bytes 884744 | tf_op jit(solution)/shard_map/ppermute | solution.py:434
  85.7 9.7 %collective-permute-start.9 = (f32[80,128]{1,0:T(8,128)S(1)}, f32[80,128]{1,0:T(8,128)S(1)}, u32[]{:S(2)}, u32[]{:S(2)}) collective-permute-start(f32[80,128]{1,0:T(8,128)S(1)} %fusion.1), channel_id=1, source_target_pairs={{0,16},{8,24},{16,0},{24,8},{32,48},{40,56},{48,32},{56,40},{64,80... | collective-permute-start | bytes 122888 | tf_op jit(solution)/shard_map/ppermute | solution.py:555
  95.5 4.0 %collective-permute-start.10 = (f32[80,128]{1,0:T(8,128)S(1)}, f32[80,128]{1,0:T(8,128)S(1)}, u32[]{:S(2)}, u32[]{:S(2)}) collective-permute-start(f32[80,128]{1,0:T(8,128)S(1)} %add.20), channel_id=1, source_target_pairs={{0,32},{8,40},{16,48},{24,56},{32,0},{40,8},{48,16},{56,24},{64,96... | collective-permute-start | bytes 122888 | tf_op jit(solution)/shard_map/ppermute | solution.py:555
  100.1 8.9 %collective-permute-start.13 = (f32[80,128]{1,0:T(8,128)}, f32[80,128]{1,0:T(8,128)}, u32[]{:S(2)}, u32[]{:S(2)}) collective-permute-start(f32[80,128]{1,0:T(8,128)} %add.21), channel_id=1, source_target_pairs={{0,64},{8,72},{16,80},{24,88},{32,96},{40,104},{48,112},{56,120},{... | collective-permute-start | bytes 122888 | tf_op jit(solution)/shard_map/ppermute | solution.py:555
  109.8 8.0 %collective-permute-start.14 = (f32[80,128]{1,0:T(8,128)S(1)}, f32[80,128]{1,0:T(8,128)S(1)}, u32[]{:S(2)}, u32[]{:S(2)}) collective-permute-start(f32[80,128]{1,0:T(8,128)S(1)} %add.22), channel_id=1, source_target_pairs={{0,128},{8,136},{16,144},{24,152},{32,160},{40,168},{48,176},{56,1... | collective-permute-start | bytes 122888 | tf_op jit(solution)/shard_map/ppermute | solution.py:555

commit v4 on v3

--- a/solution.py
+++ b/solution.py
@@ -578,10 +578,10 @@
 
     kg = jnp.sum(after(pole_back, west_back)[:, POLE_OUT:].astype(F32), axis=0)
     kg = kg[:KG_ROWS] + kg[KG_ROWS:]
-    for step in (1, 2, 4):
+    for step in (1, 4, 8):
         kg = summed(kg, step)
     kg, back_east, back_west = lax.optimization_barrier((kg, back_east, back_west))
-    kg = summed(kg, 8)
+    kg = summed(kg, 16)
 
     mixed, query_grad, key_grad, value_grad = pl.pallas_call(
         final_kernel,
@@ -616,7 +616,7 @@
     kg, mixed, query_grad, key_grad, value_grad = lax.optimization_barrier(
         (kg, mixed, query_grad, key_grad, value_grad)
     )
-    kg = summed(kg, 16)[: 9 * PAIRS].reshape(PAIRS, 9, LANES) * (NLAT * NLON) ** (-0.5)
+    kg = summed(kg, 2)[: 9 * PAIRS].reshape(PAIRS, 9, LANES) * (NLAT * NLON) ** (-0.5)
     kernel_grad = jnp.transpose(kg, (1, 0, 2)).reshape(9, width)
     return mixed, query_grad, key_grad, value_grad, kernel_grad
 

time: 119 us -> 116 us (0.975)
  waiting for transfers between devices: 33.9 us -> 27.5 us
  starting transfers between devices: 57.2 us -> 59.4 us
    ppermute x5, waiting for transfers between devices: 16.1 us -> 8.01 us  [summed(): return array + lax.ppermute(array, 'lat', route)]
    ppermute x5, starting transfers between devices: 15.7 us -> 17.9 us  [summed(): return array + lax.ppermute(array, 'lat', route)]
    ppermute x10, waiting for transfers between devices: 14.7 us -> 16.5 us  [shift(): return lax.ppermute(array, axis, route)]
  transfers between devices with their start and end apart: 17 -> 17, of which waited for: 7 -> 8; matrix products, arithmetic and copies ran while one was open for 1% -> 1% of each run, Pallas kernels for 16% -> 16%
where the time goes in v4:
time: 116 us; the launch traced here: 114 us
  starting transfers between devices  59.4 us (51%)
  waiting for transfers between devices  27.5 us (24%)
  Pallas kernels  23.5 us (20%)
  other arithmetic  2.49 us (2%)
    ppermute x10, starting transfers between devices, shift(): return lax.ppermute(array, axis, route)  29.7 us
    ppermute x5, starting transfers between devices, summed(): return array + lax.ppermute(array, 'lat', route)  17.9 us
    ppermute x10, waiting for transfers between devices, shift(): return lax.ppermute(array, axis, route)  16.5 us
    pallas_call x1, Pallas kernels, body(): pl.pallas_call(window_kernel, grid=(width // span,), in_specs=[SMEM, SMEM...  10.2 us
    ppermute x5, waiting for transfers between devices, summed(): return array + lax.ppermute(array, 'lat', route)  8.01 us
    all_to_all x1, starting transfers between devices, body(): pole_in = lax.all_to_all(pole_pay, 'lon', 0, 0)  7.6 us
    all_to_all x1, starting transfers between devices, body(): pole_back = lax.all_to_all(pole_out, 'lon', 0, 0)  4.23 us
    pallas_call x1, Pallas kernels, body(): pl.pallas_call(final_kernel, grid=(width // span,), in_specs=[SMEM, spann...  4.19 us
  transfers between devices with their start and end apart: 17, of which 8 were waited for; matrix products, arithmetic and copies ran while one was open for 1% of the time, Pallas kernels for 16%

profile of v4, /device:TPU:32, one launch (start us, length us, event | category | flops | bytes accessed | tf_op | source)
XLA Modules:
  0.0 114.4 jit_solution(3532373820671605539)
XLA Ops:
  0.6 2.5 %pack_lon.1 = (bf16[144,1024]{1,0:T(8,128)(2,1)}, bf16[144,1024]{1,0:T(8,128)(2,1)}, bf16[160,1024]{1,0:T(8,128)(2,1)}, bf16[160,1024]{1,0:T(8,128)(2,1)}, bf16[8,320,128]{2,1,0:T(8,128)(2,1)}) custom-call(bf16[4,32,1024]{2,1,0:T(8,128)(2,1)} %q_ref.3, bf16[4,32,1024]{2,1,0:T(8,128)(2,1)} %k_ref.3, bf16[4,32,1024]{2,1,0:T(8,128)(2,1)} %v_ref.3, ...), custom_call_target="tpu_custom_call" | custom-call | bytes 3145728 | tf_op jit(solution)/shard_map/pack_lon/pallas_call | solution.py:460
  4.6 4.1 %collective-permute-start.1 = (bf16[144,1024]{1,0:T(8,128)(2,1)}, bf16[144,1024]{1,0:T(8,128)(2,1)}, u32[]{:S(2)}, u32[]{:S(2)}) collective-permute-start(bf16[144,1024]{1,0:T(8,128)(2,1)} %get-tuple-element.36), channel_id=1, source_target_pairs={{0,7},{1,0},{2,1},{3,2},{4,3},{5,4},{6,5},{7,6},{8,15},{9,8},{10,9... | collective-permute-start | bytes 884744 | tf_op jit(solution)/shard_map/ppermute | solution.py:434
  8.7 1.9 %collective-permute-start.2 = (bf16[160,1024]{1,0:T(8,128)(2,1)}, bf16[160,1024]{1,0:T(8,128)(2,1)}, u32[]{:S(2)}, u32[]{:S(2)}) collective-permute-start(bf16[160,1024]{1,0:T(8,128)(2,1)} %get-tuple-element.39), channel_id=1, source_target_pairs={{0,8},{8,16},{16,24},{24,32},{32,40},{40,48},{48,56},{56,64},{64,7... | collective-permute-start | bytes 983048 | tf_op jit(solution)/shard_map/ppermute | solution.py:434
  10.7 4.5 %collective-permute-start.3 = (bf16[160,1024]{1,0:T(8,128)(2,1)}, bf16[160,1024]{1,0:T(8,128)(2,1)}, u32[]{:S(2)}, u32[]{:S(2)}) collective-permute-start(bf16[160,1024]{1,0:T(8,128)(2,1)} %get-tuple-element.40), channel_id=1, source_target_pairs={{8,0},{16,8},{24,16},{32,24},{40,32},{48,40},{56,48},{64,56},{72,6... | collective-permute-start | bytes 983048 | tf_op jit(solution)/shard_map/ppermute | solution.py:434
  15.8 1.9 %pack_corner.1 = (bf16[144,1024]{1,0:T(8,128)(2,1)}, bf16[144,1024]{1,0:T(8,128)(2,1)}) custom-call(bf16[144,1024]{1,0:T(8,128)(2,1)} %collective-permute-done.w_ref, bf16[144,1024]{1,0:T(8,128)(2,1)} %collective-permute-done.1.e_ref), custom_call_target="tpu_custom_call" | custom-call | bytes 2097152 | tf_op jit(solution)/shard_map/pack_corner/pallas_call | solution.py:480
  19.7 2.4 %collective-permute-start.4 = (bf16[144,1024]{1,0:T(8,128)(2,1)}, bf16[144,1024]{1,0:T(8,128)(2,1)}, u32[]{:S(2)}, u32[]{:S(2)}) collective-permute-start(bf16[144,1024]{1,0:T(8,128)(2,1)} %get-tuple-element.37), channel_id=1, source_target_pairs={{0,8},{8,16},{16,24},{24,32},{32,40},{40,48},{48,56},{56,64},{64,7... | collective-permute-start | bytes 884744 | tf_op jit(solution)/shard_map/ppermute | solution.py:434
  22.1 7.6 %all-to-all-start = ((bf16[8,320,128]{2,1,0:T(8,128)(2,1)}), bf16[8,320,128]{2,1,0:T(8,128)(2,1)}, u32[]{:S(2)}, u32[]{:S(2)}) async-start(bf16[8,320,128]{2,1,0:T(8,128)(2,1)} %get-tuple-element.38), calls=%async_computation | async-start | bytes 1310720 | tf_op jit(solution)/shard_map/all_to_all | solution.py:494
  29.7 10.2 %window.1 = (bf16[128,1024]{1,0:T(8,128)(2,1)}, bf16[128,1024]{1,0:T(8,128)(2,1)}, bf16[288,1024]{1,0:T(8,128)(2,1)}, bf16[288,1024]{1,0:T(8,128)(2,1)}, f32[2,256,1024]{2,1,0:T(8,128)}, /*index=5*/f32[9,1024]{1,0:T(8,128)}) custom-call(s32[2,128]{1,0:T(2,128)} %bitcast.8, s32[128]{0:T(128)} %polar_ref.5, bf16[4,32,1024]{2,1,0:T(8,128)(2,1)} %q_ref.3, ...), custom_call_target="tpu_custom_call" | custom-call | flops 4000000000 | bytes 8388608 | tf_op jit(solution)/shard_map/window/pallas_call | solution.py:496
  39.9 3.0 %all-to-all-done.pole_in_ref = bf16[8,320,128]{2,1,0:T(8,128)(2,1)} async-done(((bf16[8,320,128]{2,1,0:T(8,128)(2,1)}), bf16[8,320,128]{2,1,0:T(8,128)(2,1)}, u32[]{:S(2)}, u32[]{:S(2)}) %all-to-all-start) | async-done | bytes 655392 | tf_op jit(solution)/shard_map/all_to_all | solution.py:494
  42.9 2.3 %pole.1 = bf16[8,432,128]{2,1,0:T(8,128)(2,1)} custom-call(s32[128]{0:T(128)} %polar_ref.5, bf16[8,320,128]{2,1,0:T(8,128)(2,1)} %all-to-all-done.pole_in_ref, f32[9,1024]{1,0:T(8,128)} %conv_ref.5, f32[9,1024]{1,0:T(8,128)} %get-tuple-element.42.kgin_ref), custom_call_target="tpu_custom_call" | custom-call | flops 1000000000 | bytes 4194304 | tf_op jit(solution)/shard_map/pole/pallas_call | solution.py:532
  45.2 4.2 %all-to-all-start.1 = ((bf16[8,432,128]{2,1,0:T(8,128)(2,1)}), bf16[8,432,128]{2,1,0:T(8,128)(2,1)}, u32[]{:S(2)}, u32[]{:S(2)}) async-start(bf16[8,432,128]{2,1,0:T(8,128)(2,1)} %pole.1), calls=%async_computation.1 | async-start | bytes 1769472 | tf_op jit(solution)/shard_map/all_to_all | solution.py:551
  49.5 5.5 %collective-permute-start.6 = (bf16[288,1024]{1,0:T(8,128)(2,1)}, bf16[288,1024]{1,0:T(8,128)(2,1)}, u32[]{:S(2)}, u32[]{:S(2)}) collective-permute-start(bf16[288,1024]{1,0:T(8,128)(2,1)} %get-tuple-element.45), channel_id=1, source_target_pairs={{0,8},{8,16},{16,24},{24,32},{32,40},{40,48},{48,56},{56,64},{64,7... | collective-permute-start | bytes 1769480 | tf_op jit(solution)/shard_map/ppermute | solution.py:434
  55.0 1.9 %collective-permute-start.7 = (bf16[288,1024]{1,0:T(8,128)(2,1)}, bf16[288,1024]{1,0:T(8,128)(2,1)}, u32[]{:S(2)}, u32[]{:S(2)}) collective-permute-start(bf16[288,1024]{1,0:T(8,128)(2,1)} %get-tuple-element.46), channel_id=1, source_target_pairs={{8,0},{16,8},{24,16},{32,24},{40,32},{48,40},{56,48},{64,56},{72,6... | collective-permute-start | bytes 1769480 | tf_op jit(solution)/shard_map/ppermute | solution.py:434
  56.9 12.2 %collective-permute-done.6.n_ref = bf16[288,1024]{1,0:T(8,128)(2,1)} collective-permute-done((bf16[288,1024]{1,0:T(8,128)(2,1)}, bf16[288,1024]{1,0:T(8,128)(2,1)}, u32[]{:S(2)}, u32[]{:S(2)}) %collective-permute-start.6) | collective-permute-done | bytes 589856 | tf_op jit(solution)/shard_map/ppermute | solution.py:434
  69.1 1.9 %collective-permute-done.7.s_ref = bf16[288,1024]{1,0:T(8,128)(2,1)} collective-permute-done((bf16[288,1024]{1,0:T(8,128)(2,1)}, bf16[288,1024]{1,0:T(8,128)(2,1)}, u32[]{:S(2)}, u32[]{:S(2)}) %collective-permute-start.7) | collective-permute-done | bytes 589856 | tf_op jit(solution)/shard_map/ppermute | solution.py:434
  71.0 2.4 %pack_back.1 = (bf16[144,1024]{1,0:T(8,128)(2,1)}, bf16[144,1024]{1,0:T(8,128)(2,1)}) custom-call(f32[2,256,1024]{2,1,0:T(8,128)} %get-tuple-element.43.mid_ref, bf16[128,1024]{1,0:T(8,128)(2,1)} %get-tuple-element.44.att_ref, bf16[288,1024]{1,0:T(8,128)(2,1)} %collective-permute-done.6.n_ref, bf16[288,1024]{1,0:T(8,128)(2,1)} %collective-permute-done.7.s_ref), custom_call_target="tpu_custom_call" | custom-call | bytes 3145728 | tf_op jit(solution)/shard_map/pack_back/pallas_call | solution.py:560
  74.5 5.4 %collective-permute-start.8 = (f32[80,128]{1,0:T(8,128)S(1)}, f32[80,128]{1,0:T(8,128)S(1)}, u32[]{:S(2)}, u32[]{:S(2)}) collective-permute-start(f32[80,128]{1,0:T(8,128)S(1)} %slice_add_fusion), channel_id=1, source_target_pairs={{0,8},{8,0},{16,24},{24,16},{32,40},{40,32},{48,56},{56,48},{64,72... | collective-permute-start | bytes 122888 | tf_op jit(solution)/shard_map/ppermute | solution.py:555
  79.9 5.9 %collective-permute-start.11 = (bf16[144,1024]{1,0:T(8,128)(2,1)}, bf16[144,1024]{1,0:T(8,128)(2,1)}, u32[]{:S(2)}, u32[]{:S(2)}) collective-permute-start(bf16[144,1024]{1,0:T(8,128)(2,1)} %get-tuple-element.47), channel_id=1, source_target_pairs={{0,7},{1,0},{2,1},{3,2},{4,3},{5,4},{6,5},{7,6},{8,15},{9,8},{10,9... | collective-permute-start | bytes 884744 | tf_op jit(solution)/shard_map/ppermute | solution.py:434
  86.7 3.1 %collective-permute-done.9 = f32[80,128]{1,0:T(8,128)S(1)} collective-permute-done((f32[80,128]{1,0:T(8,128)S(1)}, f32[80,128]{1,0:T(8,128)S(1)}, u32[]{:S(2)}, u32[]{:S(2)}) %collective-permute-start.9) | collective-permute-done | bytes 40992 | tf_op jit(solution)/shard_map/ppermute | solution.py:555
  89.8 4.2 %collective-permute-start.10 = (f32[80,128]{1,0:T(8,128)S(1)}, f32[80,128]{1,0:T(8,128)S(1)}, u32[]{:S(2)}, u32[]{:S(2)}) collective-permute-start(f32[80,128]{1,0:T(8,128)S(1)} %add.20), channel_id=1, source_target_pairs={{0,64},{8,72},{16,80},{24,88},{32,96},{40,104},{48,112},{56,120},{... | collective-permute-start | bytes 122888 | tf_op jit(solution)/shard_map/ppermute | solution.py:555
  94.0 2.0 %collective-permute-done.10 = f32[80,128]{1,0:T(8,128)S(1)} collective-permute-done((f32[80,128]{1,0:T(8,128)S(1)}, f32[80,128]{1,0:T(8,128)S(1)}, u32[]{:S(2)}, u32[]{:S(2)}) %collective-permute-start.10) | collective-permute-done | bytes 40992 | tf_op jit(solution)/shard_map/ppermute | solution.py:555
  98.4 6.3 %collective-permute-start.13 = (f32[80,128]{1,0:T(8,128)}, f32[80,128]{1,0:T(8,128)}, u32[]{:S(2)}, u32[]{:S(2)}) collective-permute-start(f32[80,128]{1,0:T(8,128)} %add.21), channel_id=1, source_target_pairs={{0,128},{8,136},{16,144},{24,152},{32,160},{40,168},{48,176},{56,1... | collective-permute-start | bytes 122888 | tf_op jit(solution)/shard_map/ppermute | solution.py:555
  104.7 4.2 %final.1 = (bf16[4,32,1024]{2,1,0:T(8,128)(2,1)}, bf16[4,32,1024]{2,1,0:T(8,128)(2,1)}, bf16[4,32,1024]{2,1,0:T(8,128)(2,1)}, bf16[4,32,1024]{2,1,0:T(8,128)(2,1)}) custom-call(s32[128]{0:T(128)} %polar_ref.5, bf16[128,1024]{1,0:T(8,128)(2,1)} %get-tuple-element.44.att_ref, bf16[128,1024]{1,0:T(8,128)(2,1)} %get-tuple-element.51.dq_ref, ...), custom_call_target="tpu_custom_call" | custom-call | bytes 6291456 | tf_op jit(solution)/shard_map/final/pallas_call | solution.py:586
  110.8 2.9 %collective-permute-done.14 = f32[80,128]{1,0:T(8,128)S(1)} collective-permute-done((f32[80,128]{1,0:T(8,128)S(1)}, f32[80,128]{1,0:T(8,128)S(1)}, u32[]{:S(2)}, u32[]{:S(2)}) %collective-permute-start.14) | collective-permute-done | bytes 40992 | tf_op jit(solution)/shard_map/ppermute | solution.py:555
  (27 shorter events, 11.0 us)
Async XLA Ops:
  3.1 12.7 %collective-permute-start = (bf16[144,1024]{1,0:T(8,128)(2,1)}, bf16[144,1024]{1,0:T(8,128)(2,1)}, u32[]{:S(2)}, u32[]{:S(2)}) collective-permute-start(bf16[144,1024]{1,0:T(8,128)(2,1)} %get-tuple-element.35), channel_id=1, source_target_pairs={{0,1},{1,2},{2,3},{3,4},{4,5},{5,6},{6,7},{7,0},{8,9},{9,10},{10,1... | collective-permute-start | bytes 884744 | tf_op jit(solution)/shard_map/ppermute | solution.py:434
  4.6 11.2 %collective-permute-start.1 = (bf16[144,1024]{1,0:T(8,128)(2,1)}, bf16[144,1024]{1,0:T(8,128)(2,1)}, u32[]{:S(2)}, u32[]{:S(2)}) collective-permute-start(bf16[144,1024]{1,0:T(8,128)(2,1)} %get-tuple-element.36), channel_id=1, source_target_pairs={{0,7},{1,0},{2,1},{3,2},{4,3},{5,4},{6,5},{7,6},{8,15},{9,8},{10,9... | collective-permute-start | bytes 884744 | tf_op jit(solution)/shard_map/ppermute | solution.py:434
  8.7 20.9 %collective-permute-start.2 = (bf16[160,1024]{1,0:T(8,128)(2,1)}, bf16[160,1024]{1,0:T(8,128)(2,1)}, u32[]{:S(2)}, u32[]{:S(2)}) collective-permute-start(bf16[160,1024]{1,0:T(8,128)(2,1)} %get-tuple-element.39), channel_id=1, source_target_pairs={{0,8},{8,16},{16,24},{24,32},{32,40},{40,48},{48,56},{56,64},{64,7... | collective-permute-start | bytes 983048 | tf_op jit(solution)/shard_map/ppermute | solution.py:434
  10.7 19.0 %collective-permute-start.3 = (bf16[160,1024]{1,0:T(8,128)(2,1)}, bf16[160,1024]{1,0:T(8,128)(2,1)}, u32[]{:S(2)}, u32[]{:S(2)}) collective-permute-start(bf16[160,1024]{1,0:T(8,128)(2,1)} %get-tuple-element.40), channel_id=1, source_target_pairs={{8,0},{16,8},{24,16},{32,24},{40,32},{48,40},{56,48},{64,56},{72,6... | collective-permute-start | bytes 983048 | tf_op jit(solution)/shard_map/ppermute | solution.py:434
  17.7 12.0 %collective-permute-start.5 = (bf16[144,1024]{1,0:T(8,128)(2,1)}, bf16[144,1024]{1,0:T(8,128)(2,1)}, u32[]{:S(2)}, u32[]{:S(2)}) collective-permute-start(bf16[144,1024]{1,0:T(8,128)(2,1)} %get-tuple-element.41), channel_id=1, source_target_pairs={{8,0},{16,8},{24,16},{32,24},{40,32},{48,40},{56,48},{64,56},{72,6... | collective-permute-start | bytes 884744 | tf_op jit(solution)/shard_map/ppermute | solution.py:434
  19.7 10.0 %collective-permute-start.4 = (bf16[144,1024]{1,0:T(8,128)(2,1)}, bf16[144,1024]{1,0:T(8,128)(2,1)}, u32[]{:S(2)}, u32[]{:S(2)}) collective-permute-start(bf16[144,1024]{1,0:T(8,128)(2,1)} %get-tuple-element.37), channel_id=1, source_target_pairs={{0,8},{8,16},{16,24},{24,32},{32,40},{40,48},{48,56},{56,64},{64,7... | collective-permute-start | bytes 884744 | tf_op jit(solution)/shard_map/ppermute | solution.py:434
  22.1 20.8 %all-to-all-start = ((bf16[8,320,128]{2,1,0:T(8,128)(2,1)}), bf16[8,320,128]{2,1,0:T(8,128)(2,1)}, u32[]{:S(2)}, u32[]{:S(2)}) async-start(bf16[8,320,128]{2,1,0:T(8,128)(2,1)} %get-tuple-element.38), calls=%async_computation | async-start | bytes 1310720 | tf_op jit(solution)/shard_map/all_to_all | solution.py:494
  45.2 28.2 %all-to-all-start.1 = ((bf16[8,432,128]{2,1,0:T(8,128)(2,1)}), bf16[8,432,128]{2,1,0:T(8,128)(2,1)}, u32[]{:S(2)}, u32[]{:S(2)}) async-start(bf16[8,432,128]{2,1,0:T(8,128)(2,1)} %pole.1), calls=%async_computation.1 | async-start | bytes 1769472 | tf_op jit(solution)/shard_map/all_to_all | solution.py:551
  49.5 19.6 %collective-permute-start.6 = (bf16[288,1024]{1,0:T(8,128)(2,1)}, bf16[288,1024]{1,0:T(8,128)(2,1)}, u32[]{:S(2)}, u32[]{:S(2)}) collective-permute-start(bf16[288,1024]{1,0:T(8,128)(2,1)} %get-tuple-element.45), channel_id=1, source_target_pairs={{0,8},{8,16},{16,24},{24,32},{32,40},{40,48},{48,56},{56,64},{64,7... | collective-permute-start | bytes 1769480 | tf_op jit(solution)/shard_map/ppermute | solution.py:434
  55.0 16.0 %collective-permute-start.7 = (bf16[288,1024]{1,0:T(8,128)(2,1)}, bf16[288,1024]{1,0:T(8,128)(2,1)}, u32[]{:S(2)}, u32[]{:S(2)}) collective-permute-start(bf16[288,1024]{1,0:T(8,128)(2,1)} %get-tuple-element.46), channel_id=1, source_target_pairs={{8,0},{16,8},{24,16},{32,24},{40,32},{48,40},{56,48},{64,56},{72,6... | collective-permute-start | bytes 1769480 | tf_op jit(solution)/shard_map/ppermute | solution.py:434
  74.5 11.3 %collective-permute-start.8 = (f32[80,128]{1,0:T(8,128)S(1)}, f32[80,128]{1,0:T(8,128)S(1)}, u32[]{:S(2)}, u32[]{:S(2)}) collective-permute-start(f32[80,128]{1,0:T(8,128)S(1)} %slice_add_fusion), channel_id=1, source_target_pairs={{0,8},{8,0},{16,24},{24,16},{32,40},{40,32},{48,56},{56,48},{64,72... | collective-permute-start | bytes 122888 | tf_op jit(solution)/shard_map/ppermute | solution.py:555
  79.9 18.5 %collective-permute-start.11 = (bf16[144,1024]{1,0:T(8,128)(2,1)}, bf16[144,1024]{1,0:T(8,128)(2,1)}, u32[]{:S(2)}, u32[]{:S(2)}) collective-permute-start(bf16[144,1024]{1,0:T(8,128)(2,1)} %get-tuple-element.47), channel_id=1, source_target_pairs={{0,7},{1,0},{2,1},{3,2},{4,3},{5,4},{6,5},{7,6},{8,15},{9,8},{10,9... | collective-permute-start | bytes 884744 | tf_op jit(solution)/shard_map/ppermute | solution.py:434
  85.7 12.7 %collective-permute-start.12 = (bf16[144,1024]{1,0:T(8,128)(2,1)}, bf16[144,1024]{1,0:T(8,128)(2,1)}, u32[]{:S(2)}, u32[]{:S(2)}) collective-permute-start(bf16[144,1024]{1,0:T(8,128)(2,1)} %get-tuple-element.49), channel_id=1, source_target_pairs={{0,1},{1,2},{2,3},{3,4},{4,5},{5,6},{6,7},{7,0},{8,9},{9,10},{10,1... | collective-permute-start | bytes 884744 | tf_op jit(solution)/shard_map/ppermute | solution.py:434
  85.7 4.1 %collective-permute-start.9 = (f32[80,128]{1,0:T(8,128)S(1)}, f32[80,128]{1,0:T(8,128)S(1)}, u32[]{:S(2)}, u32[]{:S(2)}) collective-permute-start(f32[80,128]{1,0:T(8,128)S(1)} %fusion.1), channel_id=1, source_target_pairs={{0,32},{8,40},{16,48},{24,56},{32,0},{40,8},{48,16},{56,24},{64,96... | collective-permute-start | bytes 122888 | tf_op jit(solution)/shard_map/ppermute | solution.py:555
  89.8 6.1 %collective-permute-start.10 = (f32[80,128]{1,0:T(8,128)S(1)}, f32[80,128]{1,0:T(8,128)S(1)}, u32[]{:S(2)}, u32[]{:S(2)}) collective-permute-start(f32[80,128]{1,0:T(8,128)S(1)} %add.20), channel_id=1, source_target_pairs={{0,64},{8,72},{16,80},{24,88},{32,96},{40,104},{48,112},{56,120},{... | collective-permute-start | bytes 122888 | tf_op jit(solution)/shard_map/ppermute | solution.py:555
  98.4 10.5 %collective-permute-start.13 = (f32[80,128]{1,0:T(8,128)}, f32[80,128]{1,0:T(8,128)}, u32[]{:S(2)}, u32[]{:S(2)}) collective-permute-start(f32[80,128]{1,0:T(8,128)} %add.21), channel_id=1, source_target_pairs={{0,128},{8,136},{16,144},{24,152},{32,160},{40,168},{48,176},{56,1... | collective-permute-start | bytes 122888 | tf_op jit(solution)/shard_map/ppermute | solution.py:555
  109.7 4.0 %collective-permute-start.14 = (f32[80,128]{1,0:T(8,128)S(1)}, f32[80,128]{1,0:T(8,128)S(1)}, u32[]{:S(2)}, u32[]{:S(2)}) collective-permute-start(f32[80,128]{1,0:T(8,128)S(1)} %add.22), channel_id=1, source_target_pairs={{0,16},{8,24},{16,0},{24,8},{32,48},{40,56},{48,32},{56,40},{64,80... | collective-permute-start | bytes 122888 | tf_op jit(solution)/shard_map/ppermute | solution.py:555

commit v5 on v4

--- a/solution.py
+++ b/solution.py
@@ -451,7 +451,7 @@
     lat_count = lax.axis_size("lat")
     tokens = ROWS * COLS
     pack = 512
-    span = 256
+    span = 512
     packed = functools.partial(lane_spec, wide=pack)
     spanned = functools.partial(lane_spec, wide=span)
 

time: 116 us -> 115 us (level)
  no operation moved by 1% of the time
where the time goes in v5:
time: 115 us; the launch traced here: 113 us
  starting transfers between devices  59.5 us (52%)
  waiting for transfers between devices  27.4 us (24%)
  Pallas kernels  22.5 us (20%)
  other arithmetic  2.49 us (2%)
    ppermute x10, starting transfers between devices, shift(): return lax.ppermute(array, axis, route)  29.7 us
    ppermute x5, starting transfers between devices, summed(): return array + lax.ppermute(array, 'lat', route)  17.9 us
    ppermute x10, waiting for transfers between devices, shift(): return lax.ppermute(array, axis, route)  16.5 us
    pallas_call x1, Pallas kernels, body(): pl.pallas_call(window_kernel, grid=(width // span,), in_specs=[SMEM, SMEM...  10.2 us
    ppermute x5, waiting for transfers between devices, summed(): return array + lax.ppermute(array, 'lat', route)  7.96 us
    all_to_all x1, starting transfers between devices, body(): pole_in = lax.all_to_all(pole_pay, 'lon', 0, 0)  7.6 us
    all_to_all x1, starting transfers between devices, body(): pole_back = lax.all_to_all(pole_out, 'lon', 0, 0)  4.25 us
    pallas_call x1, Pallas kernels, body(): pl.pallas_call(final_kernel, grid=(width // span,), in_specs=[SMEM, spann...  3.16 us
  transfers between devices with their start and end apart: 17, of which 8 were waited for; matrix products, arithmetic and copies ran while one was open for 1% of the time, Pallas kernels for 16%

profile of v5, /device:TPU:32, one launch (start us, length us, event | category | flops | bytes accessed | tf_op | source)
XLA Modules:
  0.0 113.4 jit_solution(17193745760540564620)
XLA Ops:
  0.6 2.5 %pack_lon.1 = (bf16[144,1024]{1,0:T(8,128)(2,1)}, bf16[144,1024]{1,0:T(8,128)(2,1)}, bf16[160,1024]{1,0:T(8,128)(2,1)}, bf16[160,1024]{1,0:T(8,128)(2,1)}, bf16[8,320,128]{2,1,0:T(8,128)(2,1)}) custom-call(bf16[4,32,1024]{2,1,0:T(8,128)(2,1)} %q_ref.3, bf16[4,32,1024]{2,1,0:T(8,128)(2,1)} %k_ref.3, bf16[4,32,1024]{2,1,0:T(8,128)(2,1)} %v_ref.3, ...), custom_call_target="tpu_custom_call" | custom-call | bytes 3145728 | tf_op jit(solution)/shard_map/pack_lon/pallas_call | solution.py:460
  4.6 4.1 %collective-permute-start.1 = (bf16[144,1024]{1,0:T(8,128)(2,1)}, bf16[144,1024]{1,0:T(8,128)(2,1)}, u32[]{:S(2)}, u32[]{:S(2)}) collective-permute-start(bf16[144,1024]{1,0:T(8,128)(2,1)} %get-tuple-element.36), channel_id=1, source_target_pairs={{0,7},{1,0},{2,1},{3,2},{4,3},{5,4},{6,5},{7,6},{8,15},{9,8},{10,9... | collective-permute-start | bytes 884744 | tf_op jit(solution)/shard_map/ppermute | solution.py:434
  8.7 1.9 %collective-permute-start.2 = (bf16[160,1024]{1,0:T(8,128)(2,1)}, bf16[160,1024]{1,0:T(8,128)(2,1)}, u32[]{:S(2)}, u32[]{:S(2)}) collective-permute-start(bf16[160,1024]{1,0:T(8,128)(2,1)} %get-tuple-element.39), channel_id=1, source_target_pairs={{0,8},{8,16},{16,24},{24,32},{32,40},{40,48},{48,56},{56,64},{64,7... | collective-permute-start | bytes 983048 | tf_op jit(solution)/shard_map/ppermute | solution.py:434
  10.7 4.5 %collective-permute-start.3 = (bf16[160,1024]{1,0:T(8,128)(2,1)}, bf16[160,1024]{1,0:T(8,128)(2,1)}, u32[]{:S(2)}, u32[]{:S(2)}) collective-permute-start(bf16[160,1024]{1,0:T(8,128)(2,1)} %get-tuple-element.40), channel_id=1, source_target_pairs={{8,0},{16,8},{24,16},{32,24},{40,32},{48,40},{56,48},{64,56},{72,6... | collective-permute-start | bytes 983048 | tf_op jit(solution)/shard_map/ppermute | solution.py:434
  15.8 1.9 %pack_corner.1 = (bf16[144,1024]{1,0:T(8,128)(2,1)}, bf16[144,1024]{1,0:T(8,128)(2,1)}) custom-call(bf16[144,1024]{1,0:T(8,128)(2,1)} %collective-permute-done.w_ref, bf16[144,1024]{1,0:T(8,128)(2,1)} %collective-permute-done.1.e_ref), custom_call_target="tpu_custom_call" | custom-call | bytes 2097152 | tf_op jit(solution)/shard_map/pack_corner/pallas_call | solution.py:480
  19.7 2.4 %collective-permute-start.4 = (bf16[144,1024]{1,0:T(8,128)(2,1)}, bf16[144,1024]{1,0:T(8,128)(2,1)}, u32[]{:S(2)}, u32[]{:S(2)}) collective-permute-start(bf16[144,1024]{1,0:T(8,128)(2,1)} %get-tuple-element.37), channel_id=1, source_target_pairs={{0,8},{8,16},{16,24},{24,32},{32,40},{40,48},{48,56},{56,64},{64,7... | collective-permute-start | bytes 884744 | tf_op jit(solution)/shard_map/ppermute | solution.py:434
  22.1 7.6 %all-to-all-start = ((bf16[8,320,128]{2,1,0:T(8,128)(2,1)}), bf16[8,320,128]{2,1,0:T(8,128)(2,1)}, u32[]{:S(2)}, u32[]{:S(2)}) async-start(bf16[8,320,128]{2,1,0:T(8,128)(2,1)} %get-tuple-element.38), calls=%async_computation | async-start | bytes 1310720 | tf_op jit(solution)/shard_map/all_to_all | solution.py:494
  29.7 10.2 %window.1 = (bf16[128,1024]{1,0:T(8,128)(2,1)}, bf16[128,1024]{1,0:T(8,128)(2,1)}, bf16[288,1024]{1,0:T(8,128)(2,1)}, bf16[288,1024]{1,0:T(8,128)(2,1)}, f32[2,256,1024]{2,1,0:T(8,128)}, /*index=5*/f32[9,1024]{1,0:T(8,128)}) custom-call(s32[2,128]{1,0:T(2,128)} %bitcast.8, s32[128]{0:T(128)} %polar_ref.5, bf16[4,32,1024]{2,1,0:T(8,128)(2,1)} %q_ref.3, ...), custom_call_target="tpu_custom_call" | custom-call | flops 4000000000 | bytes 8388608 | tf_op jit(solution)/shard_map/window/pallas_call | solution.py:496
  39.9 3.0 %all-to-all-done.pole_in_ref = bf16[8,320,128]{2,1,0:T(8,128)(2,1)} async-done(((bf16[8,320,128]{2,1,0:T(8,128)(2,1)}), bf16[8,320,128]{2,1,0:T(8,128)(2,1)}, u32[]{:S(2)}, u32[]{:S(2)}) %all-to-all-start) | async-done | bytes 655392 | tf_op jit(solution)/shard_map/all_to_all | solution.py:494
  42.9 2.3 %pole.1 = bf16[8,432,128]{2,1,0:T(8,128)(2,1)} custom-call(s32[128]{0:T(128)} %polar_ref.5, bf16[8,320,128]{2,1,0:T(8,128)(2,1)} %all-to-all-done.pole_in_ref, f32[9,1024]{1,0:T(8,128)} %conv_ref.5, f32[9,1024]{1,0:T(8,128)} %get-tuple-element.42.kgin_ref), custom_call_target="tpu_custom_call" | custom-call | flops 1000000000 | bytes 4194304 | tf_op jit(solution)/shard_map/pole/pallas_call | solution.py:532
  45.2 4.2 %all-to-all-start.1 = ((bf16[8,432,128]{2,1,0:T(8,128)(2,1)}), bf16[8,432,128]{2,1,0:T(8,128)(2,1)}, u32[]{:S(2)}, u32[]{:S(2)}) async-start(bf16[8,432,128]{2,1,0:T(8,128)(2,1)} %pole.1), calls=%async_computation.1 | async-start | bytes 1769472 | tf_op jit(solution)/shard_map/all_to_all | solution.py:551
  49.5 5.5 %collective-permute-start.6 = (bf16[288,1024]{1,0:T(8,128)(2,1)}, bf16[288,1024]{1,0:T(8,128)(2,1)}, u32[]{:S(2)}, u32[]{:S(2)}) collective-permute-start(bf16[288,1024]{1,0:T(8,128)(2,1)} %get-tuple-element.45), channel_id=1, source_target_pairs={{0,8},{8,16},{16,24},{24,32},{32,40},{40,48},{48,56},{56,64},{64,7... | collective-permute-start | bytes 1769480 | tf_op jit(solution)/shard_map/ppermute | solution.py:434
  55.0 1.9 %collective-permute-start.7 = (bf16[288,1024]{1,0:T(8,128)(2,1)}, bf16[288,1024]{1,0:T(8,128)(2,1)}, u32[]{:S(2)}, u32[]{:S(2)}) collective-permute-start(bf16[288,1024]{1,0:T(8,128)(2,1)} %get-tuple-element.46), channel_id=1, source_target_pairs={{8,0},{16,8},{24,16},{32,24},{40,32},{48,40},{56,48},{64,56},{72,6... | collective-permute-start | bytes 1769480 | tf_op jit(solution)/shard_map/ppermute | solution.py:434
  56.9 12.2 %collective-permute-done.6.n_ref = bf16[288,1024]{1,0:T(8,128)(2,1)} collective-permute-done((bf16[288,1024]{1,0:T(8,128)(2,1)}, bf16[288,1024]{1,0:T(8,128)(2,1)}, u32[]{:S(2)}, u32[]{:S(2)}) %collective-permute-start.6) | collective-permute-done | bytes 589856 | tf_op jit(solution)/shard_map/ppermute | solution.py:434
  69.1 1.9 %collective-permute-done.7.s_ref = bf16[288,1024]{1,0:T(8,128)(2,1)} collective-permute-done((bf16[288,1024]{1,0:T(8,128)(2,1)}, bf16[288,1024]{1,0:T(8,128)(2,1)}, u32[]{:S(2)}, u32[]{:S(2)}) %collective-permute-start.7) | collective-permute-done | bytes 589856 | tf_op jit(solution)/shard_map/ppermute | solution.py:434
  71.0 2.4 %pack_back.1 = (bf16[144,1024]{1,0:T(8,128)(2,1)}, bf16[144,1024]{1,0:T(8,128)(2,1)}) custom-call(f32[2,256,1024]{2,1,0:T(8,128)} %get-tuple-element.43.mid_ref, bf16[128,1024]{1,0:T(8,128)(2,1)} %get-tuple-element.44.att_ref, bf16[288,1024]{1,0:T(8,128)(2,1)} %collective-permute-done.6.n_ref, bf16[288,1024]{1,0:T(8,128)(2,1)} %collective-permute-done.7.s_ref), custom_call_target="tpu_custom_call" | custom-call | bytes 3145728 | tf_op jit(solution)/shard_map/pack_back/pallas_call | solution.py:560
  74.5 5.4 %collective-permute-start.8 = (f32[80,128]{1,0:T(8,128)S(1)}, f32[80,128]{1,0:T(8,128)S(1)}, u32[]{:S(2)}, u32[]{:S(2)}) collective-permute-start(f32[80,128]{1,0:T(8,128)S(1)} %slice_add_fusion), channel_id=1, source_target_pairs={{0,8},{8,0},{16,24},{24,16},{32,40},{40,32},{48,56},{56,48},{64,72... | collective-permute-start | bytes 122888 | tf_op jit(solution)/shard_map/ppermute | solution.py:555
  79.9 5.9 %collective-permute-start.11 = (bf16[144,1024]{1,0:T(8,128)(2,1)}, bf16[144,1024]{1,0:T(8,128)(2,1)}, u32[]{:S(2)}, u32[]{:S(2)}) collective-permute-start(bf16[144,1024]{1,0:T(8,128)(2,1)} %get-tuple-element.47), channel_id=1, source_target_pairs={{0,7},{1,0},{2,1},{3,2},{4,3},{5,4},{6,5},{7,6},{8,15},{9,8},{10,9... | collective-permute-start | bytes 884744 | tf_op jit(solution)/shard_map/ppermute | solution.py:434
  86.7 3.1 %collective-permute-done.9 = f32[80,128]{1,0:T(8,128)S(1)} collective-permute-done((f32[80,128]{1,0:T(8,128)S(1)}, f32[80,128]{1,0:T(8,128)S(1)}, u32[]{:S(2)}, u32[]{:S(2)}) %collective-permute-start.9) | collective-permute-done | bytes 40992 | tf_op jit(solution)/shard_map/ppermute | solution.py:555
  89.8 4.2 %collective-permute-start.10 = (f32[80,128]{1,0:T(8,128)S(1)}, f32[80,128]{1,0:T(8,128)S(1)}, u32[]{:S(2)}, u32[]{:S(2)}) collective-permute-start(f32[80,128]{1,0:T(8,128)S(1)} %add.20), channel_id=1, source_target_pairs={{0,64},{8,72},{16,80},{24,88},{32,96},{40,104},{48,112},{56,120},{... | collective-permute-start | bytes 122888 | tf_op jit(solution)/shard_map/ppermute | solution.py:555
  94.0 2.0 %collective-permute-done.10 = f32[80,128]{1,0:T(8,128)S(1)} collective-permute-done((f32[80,128]{1,0:T(8,128)S(1)}, f32[80,128]{1,0:T(8,128)S(1)}, u32[]{:S(2)}, u32[]{:S(2)}) %collective-permute-start.10) | collective-permute-done | bytes 40992 | tf_op jit(solution)/shard_map/ppermute | solution.py:555
  98.4 6.3 %collective-permute-start.13 = (f32[80,128]{1,0:T(8,128)}, f32[80,128]{1,0:T(8,128)}, u32[]{:S(2)}, u32[]{:S(2)}) collective-permute-start(f32[80,128]{1,0:T(8,128)} %add.21), channel_id=1, source_target_pairs={{0,128},{8,136},{16,144},{24,152},{32,160},{40,168},{48,176},{56,1... | collective-permute-start | bytes 122888 | tf_op jit(solution)/shard_map/ppermute | solution.py:555
  104.7 3.2 %final.1 = (bf16[4,32,1024]{2,1,0:T(8,128)(2,1)}, bf16[4,32,1024]{2,1,0:T(8,128)(2,1)}, bf16[4,32,1024]{2,1,0:T(8,128)(2,1)}, bf16[4,32,1024]{2,1,0:T(8,128)(2,1)}) custom-call(s32[128]{0:T(128)} %polar_ref.5, bf16[128,1024]{1,0:T(8,128)(2,1)} %get-tuple-element.44.att_ref, bf16[128,1024]{1,0:T(8,128)(2,1)} %get-tuple-element.51.dq_ref, ...), custom_call_target="tpu_custom_call" | custom-call | bytes 6291456 | tf_op jit(solution)/shard_map/final/pallas_call | solution.py:586
  109.8 2.9 %collective-permute-done.14 = f32[80,128]{1,0:T(8,128)S(1)} collective-permute-done((f32[80,128]{1,0:T(8,128)S(1)}, f32[80,128]{1,0:T(8,128)S(1)}, u32[]{:S(2)}, u32[]{:S(2)}) %collective-permute-start.14) | collective-permute-done | bytes 40992 | tf_op jit(solution)/shard_map/ppermute | solution.py:555
  (27 shorter events, 11.1 us)
Async XLA Ops:
  3.1 12.7 %collective-permute-start = (bf16[144,1024]{1,0:T(8,128)(2,1)}, bf16[144,1024]{1,0:T(8,128)(2,1)}, u32[]{:S(2)}, u32[]{:S(2)}) collective-permute-start(bf16[144,1024]{1,0:T(8,128)(2,1)} %get-tuple-element.35), channel_id=1, source_target_pairs={{0,1},{1,2},{2,3},{3,4},{4,5},{5,6},{6,7},{7,0},{8,9},{9,10},{10,1... | collective-permute-start | bytes 884744 | tf_op jit(solution)/shard_map/ppermute | solution.py:434
  4.6 11.2 %collective-permute-start.1 = (bf16[144,1024]{1,0:T(8,128)(2,1)}, bf16[144,1024]{1,0:T(8,128)(2,1)}, u32[]{:S(2)}, u32[]{:S(2)}) collective-permute-start(bf16[144,1024]{1,0:T(8,128)(2,1)} %get-tuple-element.36), channel_id=1, source_target_pairs={{0,7},{1,0},{2,1},{3,2},{4,3},{5,4},{6,5},{7,6},{8,15},{9,8},{10,9... | collective-permute-start | bytes 884744 | tf_op jit(solution)/shard_map/ppermute | solution.py:434
  8.7 20.9 %collective-permute-start.2 = (bf16[160,1024]{1,0:T(8,128)(2,1)}, bf16[160,1024]{1,0:T(8,128)(2,1)}, u32[]{:S(2)}, u32[]{:S(2)}) collective-permute-start(bf16[160,1024]{1,0:T(8,128)(2,1)} %get-tuple-element.39), channel_id=1, source_target_pairs={{0,8},{8,16},{16,24},{24,32},{32,40},{40,48},{48,56},{56,64},{64,7... | collective-permute-start | bytes 983048 | tf_op jit(solution)/shard_map/ppermute | solution.py:434
  10.7 19.0 %collective-permute-start.3 = (bf16[160,1024]{1,0:T(8,128)(2,1)}, bf16[160,1024]{1,0:T(8,128)(2,1)}, u32[]{:S(2)}, u32[]{:S(2)}) collective-permute-start(bf16[160,1024]{1,0:T(8,128)(2,1)} %get-tuple-element.40), channel_id=1, source_target_pairs={{8,0},{16,8},{24,16},{32,24},{40,32},{48,40},{56,48},{64,56},{72,6... | collective-permute-start | bytes 983048 | tf_op jit(solution)/shard_map/ppermute | solution.py:434
  17.7 12.0 %collective-permute-start.5 = (bf16[144,1024]{1,0:T(8,128)(2,1)}, bf16[144,1024]{1,0:T(8,128)(2,1)}, u32[]{:S(2)}, u32[]{:S(2)}) collective-permute-start(bf16[144,1024]{1,0:T(8,128)(2,1)} %get-tuple-element.41), channel_id=1, source_target_pairs={{8,0},{16,8},{24,16},{32,24},{40,32},{48,40},{56,48},{64,56},{72,6... | collective-permute-start | bytes 884744 | tf_op jit(solution)/shard_map/ppermute | solution.py:434
  19.7 10.0 %collective-permute-start.4 = (bf16[144,1024]{1,0:T(8,128)(2,1)}, bf16[144,1024]{1,0:T(8,128)(2,1)}, u32[]{:S(2)}, u32[]{:S(2)}) collective-permute-start(bf16[144,1024]{1,0:T(8,128)(2,1)} %get-tuple-element.37), channel_id=1, source_target_pairs={{0,8},{8,16},{16,24},{24,32},{32,40},{40,48},{48,56},{56,64},{64,7... | collective-permute-start | bytes 884744 | tf_op jit(solution)/shard_map/ppermute | solution.py:434
  22.1 20.8 %all-to-all-start = ((bf16[8,320,128]{2,1,0:T(8,128)(2,1)}), bf16[8,320,128]{2,1,0:T(8,128)(2,1)}, u32[]{:S(2)}, u32[]{:S(2)}) async-start(bf16[8,320,128]{2,1,0:T(8,128)(2,1)} %get-tuple-element.38), calls=%async_computation | async-start | bytes 1310720 | tf_op jit(solution)/shard_map/all_to_all | solution.py:494
  45.2 28.2 %all-to-all-start.1 = ((bf16[8,432,128]{2,1,0:T(8,128)(2,1)}), bf16[8,432,128]{2,1,0:T(8,128)(2,1)}, u32[]{:S(2)}, u32[]{:S(2)}) async-start(bf16[8,432,128]{2,1,0:T(8,128)(2,1)} %pole.1), calls=%async_computation.1 | async-start | bytes 1769472 | tf_op jit(solution)/shard_map/all_to_all | solution.py:551
  49.5 19.6 %collective-permute-start.6 = (bf16[288,1024]{1,0:T(8,128)(2,1)}, bf16[288,1024]{1,0:T(8,128)(2,1)}, u32[]{:S(2)}, u32[]{:S(2)}) collective-permute-start(bf16[288,1024]{1,0:T(8,128)(2,1)} %get-tuple-element.45), channel_id=1, source_target_pairs={{0,8},{8,16},{16,24},{24,32},{32,40},{40,48},{48,56},{56,64},{64,7... | collective-permute-start | bytes 1769480 | tf_op jit(solution)/shard_map/ppermute | solution.py:434
  55.0 16.0 %collective-permute-start.7 = (bf16[288,1024]{1,0:T(8,128)(2,1)}, bf16[288,1024]{1,0:T(8,128)(2,1)}, u32[]{:S(2)}, u32[]{:S(2)}) collective-permute-start(bf16[288,1024]{1,0:T(8,128)(2,1)} %get-tuple-element.46), channel_id=1, source_target_pairs={{8,0},{16,8},{24,16},{32,24},{40,32},{48,40},{56,48},{64,56},{72,6... | collective-permute-start | bytes 1769480 | tf_op jit(solution)/shard_map/ppermute | solution.py:434
  74.5 11.2 %collective-permute-start.8 = (f32[80,128]{1,0:T(8,128)S(1)}, f32[80,128]{1,0:T(8,128)S(1)}, u32[]{:S(2)}, u32[]{:S(2)}) collective-permute-start(f32[80,128]{1,0:T(8,128)S(1)} %slice_add_fusion), channel_id=1, source_target_pairs={{0,8},{8,0},{16,24},{24,16},{32,40},{40,32},{48,56},{56,48},{64,72... | collective-permute-start | bytes 122888 | tf_op jit(solution)/shard_map/ppermute | solution.py:555
  79.9 18.5 %collective-permute-start.11 = (bf16[144,1024]{1,0:T(8,128)(2,1)}, bf16[144,1024]{1,0:T(8,128)(2,1)}, u32[]{:S(2)}, u32[]{:S(2)}) collective-permute-start(bf16[144,1024]{1,0:T(8,128)(2,1)} %get-tuple-element.47), channel_id=1, source_target_pairs={{0,7},{1,0},{2,1},{3,2},{4,3},{5,4},{6,5},{7,6},{8,15},{9,8},{10,9... | collective-permute-start | bytes 884744 | tf_op jit(solution)/shard_map/ppermute | solution.py:434
  85.7 12.7 %collective-permute-start.12 = (bf16[144,1024]{1,0:T(8,128)(2,1)}, bf16[144,1024]{1,0:T(8,128)(2,1)}, u32[]{:S(2)}, u32[]{:S(2)}) collective-permute-start(bf16[144,1024]{1,0:T(8,128)(2,1)} %get-tuple-element.49), channel_id=1, source_target_pairs={{0,1},{1,2},{2,3},{3,4},{4,5},{5,6},{6,7},{7,0},{8,9},{9,10},{10,1... | collective-permute-start | bytes 884744 | tf_op jit(solution)/shard_map/ppermute | solution.py:434
  85.7 4.1 %collective-permute-start.9 = (f32[80,128]{1,0:T(8,128)S(1)}, f32[80,128]{1,0:T(8,128)S(1)}, u32[]{:S(2)}, u32[]{:S(2)}) collective-permute-start(f32[80,128]{1,0:T(8,128)S(1)} %fusion.1), channel_id=1, source_target_pairs={{0,32},{8,40},{16,48},{24,56},{32,0},{40,8},{48,16},{56,24},{64,96... | collective-permute-start | bytes 122888 | tf_op jit(solution)/shard_map/ppermute | solution.py:555
  89.8 6.1 %collective-permute-start.10 = (f32[80,128]{1,0:T(8,128)S(1)}, f32[80,128]{1,0:T(8,128)S(1)}, u32[]{:S(2)}, u32[]{:S(2)}) collective-permute-start(f32[80,128]{1,0:T(8,128)S(1)} %add.20), channel_id=1, source_target_pairs={{0,64},{8,72},{16,80},{24,88},{32,96},{40,104},{48,112},{56,120},{... | collective-permute-start | bytes 122888 | tf_op jit(solution)/shard_map/ppermute | solution.py:555
  98.4 9.5 %collective-permute-start.13 = (f32[80,128]{1,0:T(8,128)}, f32[80,128]{1,0:T(8,128)}, u32[]{:S(2)}, u32[]{:S(2)}) collective-permute-start(f32[80,128]{1,0:T(8,128)} %add.21), channel_id=1, source_target_pairs={{0,128},{8,136},{16,144},{24,152},{32,160},{40,168},{48,176},{56,1... | collective-permute-start | bytes 122888 | tf_op jit(solution)/shard_map/ppermute | solution.py:555
  108.7 4.0 %collective-permute-start.14 = (f32[80,128]{1,0:T(8,128)S(1)}, f32[80,128]{1,0:T(8,128)S(1)}, u32[]{:S(2)}, u32[]{:S(2)}) collective-permute-start(f32[80,128]{1,0:T(8,128)S(1)} %add.22), channel_id=1, source_target_pairs={{0,16},{8,24},{16,0},{24,8},{32,48},{40,56},{48,32},{56,40},{64,80... | collective-permute-start | bytes 122888 | tf_op jit(solution)/shard_map/ppermute | solution.py:555
